TPU v7x, 128 devices: a whole 4x4x4 slice. The times are simulated.
128 devices in a mesh: blk: 32 (over z_lo, x, y), tp: 4 (over z_hi, core).
Axes of the slice: x: 4, y: 4, z: 4 (z_hi: 2, z_lo: 2; z = z_hi * 2 + z_lo), core: 2. Of those that a mesh axis runs over, the one named last changes fastest.
Arguments:
- tokens: bfloat16 [8192, 1536], P('blk'), may hold values from -6 to 6
- norm_gain: float32 [1536], replicated, may hold values from 0.5 to 1.5
- query_weight: bfloat16 [1536, 1536], P(None, 'tp'), may hold values from -0.21875 to 0.21875
- key_matrix: bfloat16 [1536, 768], P(None, 'tp'), may hold values from -0.15625 to 0.15625
- value_matrix: bfloat16 [1536, 768], P(None, 'tp'), may hold values from -0.15625 to 0.15625
- out_weight: bfloat16 [1536, 1536], P('tp'), may hold values from -1.5 to 1.5
- ffn_gain: float32 [1536], replicated, may hold values from 0.5 to 1.5
- gate_weight: bfloat16 [1536, 4096], P(None, 'tp'), may hold values from -0.15625 to 0.15625
- up_weight: bfloat16 [1536, 4096], P(None, 'tp'), may hold values from -0.15625 to 0.15625
- down_weight: bfloat16 [4096, 1536], P('tp'), may hold values from -0.09375 to 0.09375
- cotangent: bfloat16 [8192, 1536], P('blk'), may hold values from -6 to 6
- lengths: int32 [5], replicated, may hold values from 1 to 7936, as said below
Outputs:
- result: bfloat16 [8192, 1536], P('blk')
- tokens_grad: bfloat16 [8192, 1536], P('blk')
- norm_gain_grad: float32 [1536], P('blk')
- query_weight_grad: float32 [1536, 1536], P('blk', 'tp')
- key_weight_grad: float32 [1536, 768], P('blk', 'tp')
- value_weight_grad: float32 [1536, 768], P('blk', 'tp')
- out_weight_grad: float32 [1536, 1536], P('tp', 'blk')
- ffn_gain_grad: float32 [1536], P('blk')
- gate_weight_grad: float32 [1536, 4096], P('blk', 'tp')
- up_weight_grad: float32 [1536, 4096], P('blk', 'tp')
- down_weight_grad: float32 [4096, 1536], P('tp', 'blk')
Inputs may be any that keep to these rules, and one draw needn't show every extreme that they name: The lengths sum to 8192; one of the second, third or fourth documents, which one drawn from the seed, has 7936 tokens, and the other four share the remaining 256 tokens.
All inputs are finite; a program needn't handle non-finite values.
Results may differ from a plain program's by a relative error of at most 0.033.
Values may be sent and summed in bfloat16 or wider, within the bound.
A program may use at most 128 MiB of HBM per device.

v0:
```python
import jax
import jax.numpy as jnp
from jax import lax
from jax.sharding import Mesh
from jax.sharding import PartitionSpec as P

HEAD_SIZE = 96
BLK = ("blk_0", "blk_1", "blk_2")


eps = 1e-05
theta = 100000.0
key_block = 512


def sent_to_all(shard, axis):
    copies = jnp.broadcast_to(shard, (lax.axis_size(axis), *shard.shape))
    return lax.all_to_all(copies, axis, split_axis=0, concat_axis=0, tiled=True)


def taken_together(shard, axis):
    return sent_to_all(shard, axis).astype(jnp.float32).sum(axis=0)


def side_by_side(arrays, axis, dim, along):
    columns = [a.reshape(*a.shape[:along], -1) for a in arrays]
    both = jnp.concatenate(columns, axis=along)
    result, at, gathered = (lax.psum_scatter(both, axis, scatter_dimension=dim, tiled=True), 0, [])
    for a, column in zip(arrays, columns):
        share = result[..., at : at + column.shape[along]]
        gathered.append(share.reshape(*share.shape[:along], *a.shape[along:]))
        at += column.shape[along]
    return tuple(gathered)


def own_block(parts, axes, order):
    shape = [lax.axis_size(a) for a in axes]
    parts = parts.reshape(*shape, *parts.shape[1:])
    parts = parts.transpose(*order, *range(len(axes), parts.ndim))
    parts = parts.reshape(-1, *parts.shape[len(axes) :])
    for k in order:
        parts = lax.psum_scatter(parts, axes[k], scatter_dimension=0, tiled=True)
    return parts[0]


def cut_along(shard, dim, length):
    before, after = (shard.shape[:dim], shard.shape[dim + 1 :])
    return jnp.moveaxis(shard.reshape(*before, length, -1, *after), dim, 0)


def summed_rows(shard, axes, order, dim):
    length = lax.axis_size(axes)
    return own_block(cut_along(shard, dim, length), axes, order)


def angles(token_position, width):
    half = width // 2
    freq = theta ** (-2.0 * jnp.arange(half).astype(jnp.float32) / width)
    angle = token_position.astype(jnp.float32)[:, None] * freq[None, :]
    return (jnp.cos(angle)[:, None, :], jnp.sin(angle)[:, None, :])


def apply_rotary(field, cosine, sine):
    half = field.shape[-1] // 2
    first = field[..., :half]
    second = field[..., half:]
    return jnp.concatenate([first * cosine - second * sine, second * cosine + first * sine], -1)


def unrotate(field, cosine, sine):
    half = field.shape[-1] // 2
    first = field[..., :half]
    second = field[..., half:]
    return jnp.concatenate([first * cosine + second * sine, second * cosine - first * sine], -1)


def norm_back(source, inverse, gain, grad):
    scaled = grad * gain
    gain_grad = jnp.sum(grad * source * inverse, 0)
    source_grad = inverse * scaled - source * inverse**3 * jnp.mean(
        scaled * source, -1, keepdims=True
    )
    return (source_grad, gain_grad)


def local(
    tokens,
    norm_gain,
    query_weight,
    key_matrix,
    value_matrix,
    out_weight,
    ffn_gain,
    gate_weight,
    up_weight,
    down_weight,
    cotangent,
    lengths,
):
    token_rows = tokens.shape[0]
    local_heads = query_weight.shape[1] // HEAD_SIZE
    local_pairs = key_matrix.shape[1] // HEAD_SIZE
    query_groups = local_heads // local_pairs
    pair_width = local_pairs * HEAD_SIZE
    scale = HEAD_SIZE ** (-0.5)
    ends = jnp.cumsum(lengths)

    def segment_of(index):
        return jnp.sum((index[:, None] >= ends[None, :]).astype(jnp.int32), 1)

    query_index = lax.axis_index(BLK) * token_rows + jnp.arange(token_rows, dtype=jnp.int32)
    last_query = lax.axis_index(BLK) * token_rows + token_rows - 1
    query_segment = segment_of(query_index)
    query_place = query_index - jnp.sum(
        jnp.where(query_index[:, None] >= ends[None, :], lengths[None, :], 0), 1
    )
    cosine, sine = angles(query_place, HEAD_SIZE)
    source = tokens.astype(jnp.float32)
    inverse_one = lax.rsqrt(jnp.mean(source * source, -1, keepdims=True) + eps)
    normalized_input = (source * inverse_one * norm_gain).astype(jnp.bfloat16)
    query_raw = jnp.dot(normalized_input, query_weight, preferred_element_type=jnp.float32).reshape(
        token_rows, local_heads, HEAD_SIZE
    )
    query_rows = (
        apply_rotary(query_raw, cosine, sine)
        .astype(jnp.bfloat16)
        .reshape(token_rows, local_pairs, query_groups, HEAD_SIZE)
    )
    key_raw = jnp.dot(normalized_input, key_matrix, preferred_element_type=jnp.float32).reshape(
        token_rows, local_pairs, HEAD_SIZE
    )
    key_rows = (
        apply_rotary(key_raw, cosine, sine).astype(jnp.bfloat16).reshape(token_rows, pair_width)
    )
    value_rows = jnp.dot(normalized_input, value_matrix, preferred_element_type=jnp.float32).astype(
        jnp.bfloat16
    )
    key_value = jnp.concatenate([key_rows, value_rows], 1)

    def scores_of(piece, start):
        count = piece.shape[0]
        piece_keys = piece[:, :pair_width].reshape(count, local_pairs, HEAD_SIZE)
        piece_values = piece[:, pair_width:].reshape(count, local_pairs, HEAD_SIZE)
        scores = (
            jnp.einsum("qkgd,skd->kgqs", query_rows, piece_keys, preferred_element_type=jnp.float32)
            * scale
        )
        key_index = start + jnp.arange(count, dtype=jnp.int32)
        allowed = (query_segment[:, None] == segment_of(key_index)[None, :]) & (
            key_index[None, :] <= query_index[:, None]
        )
        return (scores, allowed, piece_keys, piece_values)

    def absorb_live(carry, piece, start):
        peak, total, gathered = carry
        scores, allowed, piece_keys, piece_values = scores_of(piece, start)
        scores = jnp.where(allowed[None, None], scores, -1e30)
        new_peak = jnp.maximum(peak, jnp.max(scores, -1))
        weight = jnp.exp(scores - new_peak[..., None])
        fade = jnp.exp(peak - new_peak)
        total = total * fade + jnp.sum(weight, -1)
        gathered = gathered * fade[..., None] + jnp.einsum(
            "kgqs,skd->kgqd",
            weight.astype(jnp.bfloat16),
            piece_values,
            preferred_element_type=jnp.float32,
        )
        return (new_peak, total, gathered)

    def absorb(carry, piece, start):
        return lax.cond(
            start > last_query,
            lambda inner: inner,
            lambda inner: absorb_live(inner, piece, start),
            carry,
        )

    initial = (
        jnp.full((local_pairs, query_groups, token_rows), -1e30, jnp.float32),
        jnp.zeros((local_pairs, query_groups, token_rows), jnp.float32),
        jnp.zeros((local_pairs, query_groups, token_rows, HEAD_SIZE), jnp.float32),
    )
    carry = initial
    piece = lax.all_gather(key_value, BLK, axis=0, tiled=True)
    count = piece.shape[0]
    stacked = piece.reshape(count // key_block, key_block, piece.shape[1])

    def step_block(inner, inputs):
        block_piece, number = inputs
        return (absorb(inner, block_piece, number * key_block), None)

    carry, unused = lax.scan(
        step_block, carry, (stacked, jnp.arange(count // key_block, dtype=jnp.int32))
    )
    peak, total, gathered = carry
    log_total = peak + jnp.log(total)
    attention = jnp.transpose(gathered / total[..., None], (2, 0, 1, 3))
    attended = attention.reshape(token_rows, local_heads * HEAD_SIZE).astype(jnp.bfloat16)
    branch = taken_together(
        jnp.dot(attended, out_weight, preferred_element_type=jnp.float32).astype(jnp.bfloat16), "tp"
    ).astype(jnp.float32)
    mixed = source + branch
    inverse_two = lax.rsqrt(jnp.mean(mixed * mixed, -1, keepdims=True) + eps)
    normed_two = (mixed * inverse_two * ffn_gain).astype(jnp.bfloat16)
    gate = jnp.dot(normed_two, gate_weight, preferred_element_type=jnp.float32)
    upper = jnp.dot(normed_two, up_weight, preferred_element_type=jnp.float32)
    sigmoid_gate = jax.nn.sigmoid(gate)
    silu_gate = gate * sigmoid_gate
    hidden = (silu_gate * upper).astype(jnp.bfloat16)
    feed = taken_together(
        jnp.dot(hidden, down_weight, preferred_element_type=jnp.float32).astype(jnp.bfloat16), "tp"
    ).astype(jnp.float32)
    result = (mixed + feed).astype(jnp.bfloat16)
    down_weight_grad = jnp.dot(hidden.T, cotangent, preferred_element_type=jnp.float32)
    hidden_grad = jnp.dot(cotangent, down_weight.T, preferred_element_type=jnp.float32)
    gate_grad = (hidden_grad * upper * sigmoid_gate * (1.0 + gate * (1.0 - sigmoid_gate))).astype(
        jnp.bfloat16
    )
    upper_grad = (hidden_grad * silu_gate).astype(jnp.bfloat16)
    gate_weight_grad = jnp.dot(normed_two.T, gate_grad, preferred_element_type=jnp.float32)
    up_weight_grad = jnp.dot(normed_two.T, upper_grad, preferred_element_type=jnp.float32)
    normed_two_grad = taken_together(
        (
            jnp.dot(gate_grad, gate_weight.T, preferred_element_type=jnp.float32)
            + jnp.dot(upper_grad, up_weight.T, preferred_element_type=jnp.float32)
        ).astype(jnp.bfloat16),
        "tp",
    ).astype(jnp.float32)
    mixed_part, ffn_gain_grad = norm_back(mixed, inverse_two, ffn_gain, normed_two_grad)
    mixed_grad = cotangent.astype(jnp.float32) + mixed_part
    ffn_sent = (
        *tuple(
            (
                part.astype(jnp.float32)
                for part in side_by_side(
                    (
                        ffn_gain_grad.astype(jnp.bfloat16),
                        gate_weight_grad.astype(jnp.bfloat16),
                        up_weight_grad.astype(jnp.bfloat16),
                    ),
                    BLK,
                    0,
                    1,
                )
            )
        ),
        lax.psum_scatter(
            down_weight_grad.astype(jnp.bfloat16), BLK, scatter_dimension=1, tiled=True
        ).astype(jnp.float32),
    )
    branch_grad = mixed_grad.astype(jnp.bfloat16)
    out_weight_grad = jnp.dot(attended.T, branch_grad, preferred_element_type=jnp.float32)
    attended_grad = (
        jnp.dot(branch_grad, out_weight.T, preferred_element_type=jnp.float32)
        .astype(jnp.bfloat16)
        .reshape(token_rows, local_pairs, query_groups, HEAD_SIZE)
    )
    delta = jnp.transpose(jnp.sum(attended_grad.astype(jnp.float32) * attention, -1), (1, 2, 0))
    every_pair = lax.all_gather(key_value, BLK, axis=0, tiled=True)
    all_rows = every_pair.shape[0]
    stacked = every_pair.reshape(all_rows // key_block, key_block, every_pair.shape[1])

    def backward_live(query_sum, piece, start):
        scores, allowed, piece_keys, piece_values = scores_of(piece, start)
        prob = jnp.where(allowed[None, None], jnp.exp(scores - log_total[..., None]), 0.0)
        value_grad = jnp.einsum(
            "kgqs,qkgd->skd",
            prob.astype(jnp.bfloat16),
            attended_grad,
            preferred_element_type=jnp.float32,
        )
        prob_grad = jnp.einsum(
            "qkgd,skd->kgqs", attended_grad, piece_values, preferred_element_type=jnp.float32
        )
        score_grad = (prob * (prob_grad - delta[..., None])).astype(jnp.bfloat16)
        query_sum = query_sum + jnp.einsum(
            "kgqs,skd->qkgd", score_grad, piece_keys, preferred_element_type=jnp.float32
        )
        key_grad = (
            jnp.einsum("kgqs,qkgd->skd", score_grad, query_rows, preferred_element_type=jnp.float32)
            * scale
        )
        return (
            query_sum,
            jnp.concatenate(
                [
                    key_grad.reshape(key_block, pair_width),
                    value_grad.reshape(key_block, pair_width),
                ],
                1,
            ),
        )

    def backward_block(query_sum, inputs):
        piece, number = inputs
        start = number * key_block
        return lax.cond(
            start > last_query,
            lambda inner: (inner, jnp.zeros((key_block, 2 * pair_width), jnp.float32)),
            lambda inner: backward_live(inner, piece, start),
            query_sum,
        )

    query_sum, pair_terms = lax.scan(
        backward_block,
        jnp.zeros((token_rows, local_pairs, query_groups, HEAD_SIZE), jnp.float32),
        (stacked, jnp.arange(all_rows // key_block, dtype=jnp.int32)),
    )
    pair_grad = summed_rows(
        pair_terms.reshape(all_rows, 2 * pair_width).astype(jnp.bfloat16), BLK, (1, 2, 0), 0
    ).astype(jnp.float32)
    key_grad = (
        unrotate(
            pair_grad[:, :pair_width].reshape(token_rows, local_pairs, HEAD_SIZE), cosine, sine
        )
        .reshape(token_rows, pair_width)
        .astype(jnp.bfloat16)
    )
    value_grad = pair_grad[:, pair_width:].astype(jnp.bfloat16)
    query_grad = (
        unrotate((query_sum * scale).reshape(token_rows, local_heads, HEAD_SIZE), cosine, sine)
        .reshape(token_rows, local_heads * HEAD_SIZE)
        .astype(jnp.bfloat16)
    )
    query_weight_grad = jnp.dot(normalized_input.T, query_grad, preferred_element_type=jnp.float32)
    key_weight_grad = jnp.dot(normalized_input.T, key_grad, preferred_element_type=jnp.float32)
    value_weight_grad = jnp.dot(normalized_input.T, value_grad, preferred_element_type=jnp.float32)
    normed_grad = taken_together(
        (
            jnp.dot(query_grad, query_weight.T, preferred_element_type=jnp.float32)
            + jnp.dot(key_grad, key_matrix.T, preferred_element_type=jnp.float32)
            + jnp.dot(value_grad, value_matrix.T, preferred_element_type=jnp.float32)
        ).astype(jnp.bfloat16),
        "tp",
    ).astype(jnp.float32)
    source_part, norm_gain_grad = norm_back(source, inverse_one, norm_gain, normed_grad)
    tokens_grad = (mixed_grad + source_part).astype(jnp.bfloat16)
    attn_sent = (
        *tuple(
            (
                part.astype(jnp.float32)
                for part in side_by_side(
                    (
                        norm_gain_grad.astype(jnp.bfloat16),
                        query_weight_grad.astype(jnp.bfloat16),
                        key_weight_grad.astype(jnp.bfloat16),
                        value_weight_grad.astype(jnp.bfloat16),
                    ),
                    BLK,
                    0,
                    1,
                )
            )
        ),
        lax.psum_scatter(
            out_weight_grad.astype(jnp.bfloat16), BLK, scatter_dimension=1, tiled=True
        ).astype(jnp.float32),
    )
    summed = attn_sent + ffn_sent
    return (
        result,
        tokens_grad,
        summed[0],
        summed[1],
        summed[2],
        summed[3],
        summed[4],
        summed[5],
        summed[6],
        summed[7],
        summed[8],
    )


def solution(mesh):
    split = Mesh(mesh.devices.reshape(2, 4, 4, mesh.shape["tp"]), ("blk_0", "blk_1", "blk_2", "tp"))
    in_specs = (
        P(BLK, None),
        P(),
        P(None, "tp"),
        P(None, "tp"),
        P(None, "tp"),
        P("tp", None),
        P(),
        P(None, "tp"),
        P(None, "tp"),
        P("tp", None),
        P(BLK, None),
        P(),
    )
    out_specs = (
        P(BLK, None),
        P(BLK, None),
        P(BLK),
        P(BLK, "tp"),
        P(BLK, "tp"),
        P(BLK, "tp"),
        P("tp", BLK),
        P(BLK),
        P(BLK, "tp"),
        P(BLK, "tp"),
        P("tp", BLK),
    )
    return jax.shard_map(local, mesh=split, in_specs=in_specs, out_specs=out_specs, check_vma=False)
```

profile of v0, /device:TPU:0, one launch (start us, length us, event | category | flops | bytes accessed | tf_op | source)
XLA Modules:
  0.0 1331.0 jit_solution(11220053538192675982)
XLA Ops:
  7.3 1.5 fusion.18
  11.6 1.8 convolution_convert_fusion.10
  15.0 2.2 fusion.39
  17.9 151.3 %all-gather.2.cloned.1.call-done = bf16[8192,384]{0,1:T(8,128)(2,1)} async-done(((bf16[256,384]{0,1:T(8,128)(2,1)}), bf16[8192,384]{0,1:T(8,128)(2,1)}) %all-gather.2.cloned.1.call-update) | async-done | bytes 6291472 | tf_op jit(solution)/shard_map/all_gather | solution.py:184
  169.2 6.1 copy.174
  175.9 35.1 %while.31 = (s32[]{:T(128)}, f32[2,2,256]{2,1,0:T(2,128)S(1)}, f32[2,2,256]{2,1,0:T(2,128)S(1)}, f32[2,2,256,96]{2,3,1,0:T(8,128)S(1)}, s32[16]{0:T(128)}, /*ind...) while((s32[]{:T(128)}, f32[2,2,256]{2,1,0:T(2,128)S(1)}, ...), condition=%wide.region_10.11_spmd.clone, body=%wide.region_4.10_spmd.clone.sunk | while | flops 205596416 | bytes 10370415 | solution.py:192
  177.8 3.5 conditional.6
  211.7 1.9 convolution_convert_fusion.6
  213.8 42.1 %all_to_all.20 = bf16[4,256,1536]{2,1,0:T(8,128)(2,1)S(1)} all-to-all(bf16[4,256,1536]{2,1,0:T(8,128)(2,1)S(1)} %broadcast_in_dim.114), channel_id=1, replica_groups=mesh['blk_0'=2,'blk_1'=4,'blk_2'=4,'tp'=4] {'tp'}, dimensions={0} | all-to-all | bytes 6291456 | tf_op jit(solution)/shard_map/all_to_all | solution.py:18
  258.2 1.4 copy-done.19
  262.9 2.2 multiply_convert_fusion.1
  267.1 2.0 broadcast_in_dim.116
  269.1 4.6 all-to-all-start.2
  273.8 2.9 convolution_convert_fusion.5
  276.7 35.6 %all-to-all-done.2 = bf16[4,256,1536]{2,1,0:T(8,128)(2,1)} async-done(((bf16[4,256,1536]{2,1,0:T(8,128)(2,1)}), bf16[4,256,1536]{2,1,0:T(8,128)(2,1)}, u32[]{:S(2)}, u32[]{:S(2)}) %all-to-all-start.2) | async-done | bytes 3145760 | tf_op jit(solution)/shard_map/all_to_all | solution.py:18
  312.3 3.0 broadcast_in_dim.115
  315.3 4.7 all-to-all-start.1
  320.8 2.6 convert_reduce_fusion.3
  325.2 33.3 %all-to-all-done.1 = bf16[4,256,1536]{2,1,0:T(8,128)(2,1)} async-done(((bf16[4,256,1536]{2,1,0:T(8,128)(2,1)}), bf16[4,256,1536]{2,1,0:T(8,128)(2,1)}, u32[]{:S(2)}, u32[]{:S(2)}) %all-to-all-start.1) | async-done | bytes 3145760 | tf_op jit(solution)/shard_map/all_to_all | solution.py:18
  358.5 2.6 convert_reduce_fusion.4
  364.6 42.0 %while.32 = (s32[]{:T(128)}, f32[256,2,2,96]{0,3,2,1:T(8,128)S(1)}, bf16[16,512,384]{2,1,0:T(8,128)(2,1)}, s32[16]{0:T(128)S(1)}, s32[]{:T(128)}, /*index=5*/s32...) while((s32[]{:T(128)}, f32[256,2,2,96]{0,3,2,1:T(8,128)S(1)}, ...), condition=%wide.region_21.22_spmd.clone, body=%wide.region_17.21_spmd.clone.sunk | while | flops 508468992 | bytes 17014660 | solution.py:304
  365.9 4.6 conditional.7
  406.7 6.4 copy.130
  413.1 8.6 copy.131
  421.9 182.8 %reduce-scatter.12.cloned.1.call-done = bf16[8,256,384]{1,2,0:T(8,128)(2,1)} async-done(((bf16[32,256,384]{1,2,0:T(8,128)(2,1)}), bf16[8,256,384]{1,2,0:T(8,128)(2,1)}) %reduce-scatter.12.cloned.1.call-update) | async-done | bytes 1572880 | tf_op jit(solution)/shard_map/reduce_scatter | solution.py:42
  604.8 27.8 %reduce-scatter.14.cloned.1.call-done = bf16[2,256,384]{1,2,0:T(8,128)(2,1)} async-done(((bf16[8,256,384]{1,2,0:T(8,128)(2,1)}), bf16[2,256,384]{1,2,0:T(8,128)(2,1)}) %reduce-scatter.14.cloned.1.call-update) | async-done | bytes 393232 | tf_op jit(solution)/shard_map/reduce_scatter | solution.py:42
  632.7 1.6 convolution_convert_fusion.4
  634.5 2.7 convolution_convert_fusion
  637.3 2.4 convolution_convert_fusion.1
  639.7 2.7 convolution_convert_fusion.2
  642.4 31.4 %concatenate.42 = bf16[1536,2049]{0,1:T(8,128)(2,1)} concatenate(bf16[1536,1]{0,1:T(2,128)(2,1)S(1)} %convert_element_type.264, bf16[1536,1024]{0,1:T(8,128)(2,1)} %convolution_convert_fusion.2, bf16[1536,1024]{0,1:T(8,128)(2,1)S(1)} %convolution_convert_fusion.1), dimensions={1} | concatenate | bytes 12589056 | tf_op jit(solution)/shard_map/concatenate | solution.py:27
  673.8 9.2 copy.150
  686.0 1.5 convolution_add_fusion.3
  687.9 2.0 broadcast_in_dim.119
  689.9 5.0 all-to-all-start.3
  695.0 1.6 convolution_convert_fusion.3
  698.3 38.7 %all-to-all-done.3 = bf16[4,256,1536]{2,1,0:T(8,128)(2,1)} async-done(((bf16[4,256,1536]{2,1,0:T(8,128)(2,1)}), bf16[4,256,1536]{2,1,0:T(8,128)(2,1)}, u32[]{:S(2)}, u32[]{:S(2)}) %all-to-all-start.3) | async-done | bytes 3145760 | tf_op jit(solution)/shard_map/all_to_all | solution.py:18
  737.0 2.5 convert_reduce_fusion.2
  740.0 1.4 copy-done.16
  741.5 2.0 pad_maximum_fusion
  743.5 4.4 copy.148
  747.9 67.4 %reduce-scatter.18.cloned.1.call-done = bf16[384,48]{0,1:T(8,128)(2,1)} async-done(((bf16[384,1536]{0,1:T(8,128)(2,1)}), bf16[384,48]{0,1:T(8,128)(2,1)}) %reduce-scatter.18.cloned.1.call-update) | async-done | bytes 36880 | tf_op jit(solution)/shard_map/reduce_scatter | solution.py:355
  815.4 1.4 convert_element_type.262
  816.8 162.8 %reduce-scatter.20.cloned.1.call-done = bf16[1024,48]{0,1:T(8,128)(2,1)} async-done(((bf16[1024,1536]{0,1:T(8,128)(2,1)}), bf16[1024,48]{0,1:T(8,128)(2,1)}) %reduce-scatter.20.cloned.1.call-update) | async-done | bytes 98320 | tf_op jit(solution)/shard_map/reduce_scatter | solution.py:247
  979.6 1.6 convert_element_type.272
  981.2 173.5 %reduce-scatter.24.cloned.1.call-done = bf16[48,2049]{1,0:T(8,128)(2,1)} async-done(((bf16[1536,2049]{1,0:T(8,128)(2,1)}), bf16[48,2049]{1,0:T(8,128)(2,1)}) %reduce-scatter.24.cloned.1.call-update) | async-done | bytes 196720
  1159.0 3.6 fusion.24
  1162.6 155.9 %reduce-scatter.22.cloned.1.call-done = bf16[48,769]{1,0:T(8,128)(2,1)} async-done(((bf16[1536,769]{1,0:T(8,128)(2,1)}), bf16[48,769]{1,0:T(8,128)(2,1)}) %reduce-scatter.22.cloned.1.call-update) | async-done | bytes 73840
  (387 shorter events, 91.3 us)
Async XLA Ops:
  7.2 255.6 %copy-start = (bf16[1024,1536]{1,0:T(8,128)(2,1)S(1)}, bf16[1024,1536]{1,0:T(8,128)(2,1)}, u32[]{:S(2)}) copy-start(bf16[1024,1536]{1,0:T(8,128)(2,1)} %param.29) | copy-start | bytes 9437188
  7.2 6.2 copy-start.39
  7.2 162.0 %all-gather.2.cloned.1.call-start = ((), (), s32[]{:S(2)}) async-start(), calls=%async_computation.11 | async-start | bytes 6488064 | tf_op jit(solution)/shard_map/all_gather | solution.py:184
  10.2 3.2 copy-start.8
  10.2 3.2 copy-start.36
  11.6 3.4 copy-start.43
  14.2 3.0 copy-start.28
  14.2 3.0 copy-start.30
  177.8 2.1 copy-start.6
  257.1 2.5 copy-start.19
  257.4 3.2 copy-start.4
  258.0 2.6 copy-start.46
  259.6 2.2 copy-start.18
  269.1 43.1 %all-to-all-start.2 = ((bf16[4,256,1536]{2,1,0:T(8,128)(2,1)}), bf16[4,256,1536]{2,1,0:T(8,128)(2,1)}, u32[]{:S(2)}, u32[]{:S(2)}) async-start(bf16[4,256,1536]{2,1,0:T(8,128)(2,1)} %broadcast_in_dim.116), calls=%async_computation.2 | async-start | bytes 6291456 | tf_op jit(solution)/shard_map/all_to_all | solution.py:18
  315.3 43.2 %all-to-all-start.1 = ((bf16[4,256,1536]{2,1,0:T(8,128)(2,1)}), bf16[4,256,1536]{2,1,0:T(8,128)(2,1)}, u32[]{:S(2)}, u32[]{:S(2)}) async-start(bf16[4,256,1536]{2,1,0:T(8,128)(2,1)} %broadcast_in_dim.115), calls=%async_computation.1 | async-start | bytes 6291456 | tf_op jit(solution)/shard_map/all_to_all | solution.py:18
  320.0 284.7 %reduce-scatter.12.cloned.1.call-start = ((), (), s32[]{:S(2)}) async-start(), calls=%async_computation.12 | async-start | bytes 7864320 | tf_op jit(solution)/shard_map/reduce_scatter | solution.py:42
  320.8 2.6 copy-start.5
  320.8 2.6 copy-start.42
  320.8 2.6 copy-start.47
  358.5 2.7 copy-start.15
  358.5 2.7 copy-start.21
  358.5 2.7 copy-start.48
  358.5 2.7 copy-start.51
  358.5 2.7 copy-start.52
  361.2 2.6 copy-start.17
  365.9 2.1 copy-start.7
  365.9 2.1 copy-start.50
  421.8 210.9 %copy-start.3 = (f32[256,1536]{1,0:T(8,128)S(1)}, f32[256,1536]{1,0:T(8,128)}, u32[]{:S(2)}) copy-start(f32[256,1536]{1,0:T(8,128)} %copy-done.2) | copy-start | bytes 4718596
  421.8 210.9 %copy-start.27 = (bf16[256,2,2,96]{0,3,2,1:T(8,128)(2,1)S(1)}, bf16[256,2,2,96]{0,3,2,1:T(8,128)(2,1)}, u32[]{:S(2)}) copy-start(bf16[256,2,2,96]{0,3,2,1:T(8,128)(2,1)} %copy-done.26) | copy-start | bytes 589828
  421.8 210.8 %reduce-scatter.14.cloned.1.call-start = ((), (), s32[]{:S(2)}) async-start(), calls=%async_computation.13 | async-start | bytes 1966080 | tf_op jit(solution)/shard_map/reduce_scatter | solution.py:42
  604.7 80.2 %reduce-scatter.16.cloned.1.call-start = ((), (), s32[]{:S(2)}) async-start(), calls=%async_computation.14 | async-start | bytes 589824 | tf_op jit(solution)/shard_map/reduce_scatter | solution.py:42
  632.7 182.7 %reduce-scatter.18.cloned.1.call-start = ((), (), s32[]{:S(2)}) async-start(), calls=%async_computation.15 | async-start | bytes 1216512 | tf_op jit(solution)/shard_map/reduce_scatter | solution.py:355
  634.4 345.2 %reduce-scatter.20.cloned.1.call-start = ((), (), s32[]{:S(2)}) async-start(), calls=%async_computation.16 | async-start | bytes 3244032 | tf_op jit(solution)/shard_map/reduce_scatter | solution.py:247
  637.2 517.4 %reduce-scatter.24.cloned.1.call-start = ((), (), s32[]{:S(2)}) async-start(), calls=%async_computation.18 | async-start | bytes 6893568
  637.2 2.4 copy-start.12
  637.2 2.4 copy-start.24
  639.7 2.7 copy-start.45
  689.9 5.1 copy-start.10
  689.9 5.1 copy-start.40
  689.9 5.1 copy-start.44
  689.9 47.1 %all-to-all-start.3 = ((bf16[4,256,1536]{2,1,0:T(8,128)(2,1)}), bf16[4,256,1536]{2,1,0:T(8,128)(2,1)}, u32[]{:S(2)}, u32[]{:S(2)}) async-start(bf16[4,256,1536]{2,1,0:T(8,128)(2,1)} %broadcast_in_dim.119), calls=%async_computation.6 | async-start | bytes 6291456 | tf_op jit(solution)/shard_map/all_to_all | solution.py:18
  694.9 2.1 copy-start.38
  694.9 623.6 %reduce-scatter.22.cloned.1.call-start = ((), (), s32[]{:S(2)}) async-start(), calls=%async_computation.17 | async-start | bytes 2838528
  739.5 4.0 copy-start.13
  739.5 1.8 copy-start.16
  739.5 2.0 copy-start.34
  747.9 411.1 %copy-start.49 = (f32[256]{0:T(256)S(1)}, f32[256]{0:T(256)}, u32[]{:S(2)}) copy-start(f32[256]{0:T(256)} %get-tuple-element.660) | copy-start | bytes 3076
  1159.0 165.1 %copy-start.1 = (bf16[1024,1536]{1,0:T(8,128)(2,1)S(1)}, bf16[1024,1536]{1,0:T(8,128)(2,1)}, u32[]{:S(2)}) copy-start(bf16[1024,1536]{1,0:T(8,128)(2,1)} %param.29) | copy-start | bytes 9437188
  (16 other events, 18.9 us)
Sparse Core Ops, SparseCore 0:
  15.1 154.0 all-gather.1
  421.9 182.7 reduce-scatter.11
  607.1 25.4 reduce-scatter.13
  634.8 15.4 reduce-scatter.15
  652.6 162.7 reduce-scatter.17
  817.6 161.9 reduce-scatter.19
  982.1 172.4 reduce-scatter.23
  1157.0 161.4 reduce-scatter.21
where the time goes:
time: 1340 us; the launch traced here: 1330 us
  waiting for transfers between devices  1030 us (77%)
  local copies, waits for them, and re-layouts  140 us (10%)
  blocking collectives  42.1 us (3%)
  matrix products  34.6 us (3%)
  other arithmetic  31.5 us (2%)
  loops' own time  23.2 us (2%)
  between operations  15 us (1%)
  starting transfers between devices  14.8 us (1%)
    unnamed x10, waiting for transfers between devices  329 us
    reduce_scatter x3, waiting for transfers between devices, own_block(): parts = lax.psum_scatter(parts, axes[k], scatter_dimension=0, tiled=True)  211 us
    reduce_scatter x1, waiting for transfers between devices, local(): lax.psum_scatter(down_weight_grad.astype(jnp.bfloat16), BLK, scatter_dime...  163 us
    all_gather x1, waiting for transfers between devices, local(): piece = lax.all_gather(key_value, BLK, axis=0, tiled=True)  151 us
    all_to_all x3, waiting for transfers between devices, sent_to_all(): return lax.all_to_all(copies, axis, split_axis=0, concat_axis=0, tiled=True)  108 us
    reduce_scatter x1, waiting for transfers between devices, local(): lax.psum_scatter(out_weight_grad.astype(jnp.bfloat16), BLK, scatter_dimen...  67.4 us
    all_to_all x1, blocking collectives, sent_to_all(): return lax.all_to_all(copies, axis, split_axis=0, concat_axis=0, tiled=True)  42.1 us
    concatenate x1, local copies, waits for them, and re-layouts, side_by_side(): both = jnp.concatenate(columns, axis=along)  31.4 us
  transfers between devices with their start and end apart: 11, of which 10 were waited for; matrix products, arithmetic and copies ran while one was open for 7% of the time, Pallas kernels for 0%

commit v1 on v0

v1 whole, which is shorter than its diff:
```python
import jax
import jax.numpy as jnp
import numpy as np
from jax import lax
from jax.experimental import pallas as pl
from jax.experimental.pallas import tpu as pltpu
from jax.sharding import Mesh
from jax.sharding import PartitionSpec as P

AXES = ("zl", "x", "y", "zh", "c")
BLK = ("zl", "x", "y")
TP = ("zh", "c")
HEAD = 96
HALF = HEAD // 2
ROWS = 256
WIDTH = 1536
HEADS_LOCAL = 384
PAIRS_LOCAL = 192
FFL = 1024
EPS = 1e-05
THETA = 100000.0
SCALE = HEAD**-0.5
LOG2E = float(np.log2(np.e))
LN2 = float(np.log(2.0))
BIG = 1e30
SEG = 16
MESH = pl.DeviceIdType.MESH
F32 = jnp.float32
BF16 = jnp.bfloat16
VMEM_LIMIT = 60 * 2**20


def dot(a, b, ca=1, cb=0):
    return lax.dot_general(a, b, (((ca,), (cb,)), ((), ())), preferred_element_type=F32)


class Place:
    def __init__(self):
        self.zl, self.x, self.y, self.zh, self.c = (lax.axis_index(a) for a in AXES)

    def at(self, **changes):
        own = dict(zl=self.zl, x=self.x, y=self.y, zh=self.zh, c=self.c)
        own.update(changes)
        return tuple(own[a] for a in AXES)

    def along(self, axis, step):
        return self.at(**{axis: lax.rem(getattr(self, axis) + (step + 4), 4)})

    @property
    def pair(self):
        return dict(zl=1 - self.zl, x=3 - self.x, y=3 - self.y)

    def low_block(self, x, y):
        p = x * 4 + y
        return jnp.where(self.zl == 0, p, 15 - p)


def greet(peers):
    barrier = pltpu.get_barrier_semaphore()
    for peer in peers:
        pl.semaphore_signal(barrier, inc=1, device_id=peer, device_id_type=MESH)
    pl.semaphore_wait(barrier, len(peers))


def remote(src, dst, send, recv, device):
    return pltpu.make_async_remote_copy(
        src_ref=src, dst_ref=dst, send_sem=send, recv_sem=recv, device_id=device, device_id_type=MESH
    )


def seg_rows(ends, base):
    token = base + lax.broadcasted_iota(jnp.int32, (SEG, ROWS), 1)
    row = lax.broadcasted_iota(jnp.int32, (SEG, ROWS), 0)
    inside = jnp.zeros((SEG, ROWS), F32)
    start = 0
    for d in range(5):
        hit = (row == d) & (token >= start) & (token < ends[d])
        inside = jnp.where(hit, 1.0, inside)
        start = ends[d]
    return inside, row


def key_segments(ends, base):
    return seg_rows(ends, base)[0].astype(BF16)


def query_segments(ends, base):
    inside, row = seg_rows(ends, base)
    return jnp.where(row < 5, (inside - 1.0) * BIG, 0.0).astype(BF16)


def ends_of(lengths_ref):
    ends, total = [], 0
    for d in range(5):
        total = total + lengths_ref[d]
        ends.append(total)
    return ends


def rotation(ends, lengths_ref, base, freq):
    token = base + lax.broadcasted_iota(jnp.int32, (1, ROWS), 1)
    begin = jnp.zeros((1, ROWS), jnp.int32)
    for d in range(5):
        begin = begin + jnp.where(token >= ends[d], lengths_ref[d], 0)
    angle = (token - begin).astype(F32) * freq
    return jnp.cos(angle), jnp.sin(angle)


class RingSum:
    def __init__(self, place, axis, half, bufs, out, send, recv, add2, add3):
        self.half, self.bufs, self.out, self.add2, self.add3 = half, bufs, out, add2, add3
        me = getattr(place, axis)
        self.me = me
        self.r, self.l, self.o = (lax.rem(me + k, 4) for k in (1, 3, 2))
        self.right, self.left = place.along(axis, 1), place.along(axis, -1)
        self.send, self.recv = send, recv

    def cp(self, k):
        src = (
            lambda: self.half(self.o, 0),
            lambda: self.half(self.o, 1),
            lambda: self.half(self.r, 1),
            lambda: self.half(self.l, 0),
            lambda: self.bufs(0),
            lambda: self.bufs(1),
        )[k]()
        return remote(
            src, self.bufs(k), self.send(k), self.recv(k), (self.right, self.left)[k % 2]
        )

    def start(self):
        for k in range(4):
            self.cp(k).start()

    def mid(self):
        self.cp(0).wait_recv()
        self.cp(0).wait_send()
        self.add2(self.bufs(0), self.half(self.r, 0))
        self.cp(4).start()
        self.cp(1).wait_recv()
        self.cp(1).wait_send()
        self.add2(self.bufs(1), self.half(self.l, 1))
        self.cp(5).start()

    def fin(self):
        self.cp(4).wait_recv()
        self.cp(3).wait_recv()
        self.add3(self.out(0), self.half(self.me, 0), self.bufs(4), self.bufs(3))
        self.cp(5).wait_recv()
        self.cp(2).wait_recv()
        self.add3(self.out(1), self.half(self.me, 1), self.bufs(5), self.bufs(2))

    def end(self):
        for k in range(2, 6):
            self.cp(k).wait_send()


def add2_lead(dst, src):
    for i in range(dst.shape[0]):
        dst[i] = dst[i] + src[i]


def add3_lead(out, a, b, d):
    for i in range(out.shape[0]):
        out[i] = (a[i].astype(F32) + b[i].astype(F32) + d[i].astype(F32)).astype(BF16)


def add2_flat(dst, src):
    dst[...] = dst[...] + src[...]


def add3_flat(out, a, b, d):
    out[...] = (a[...].astype(F32) + b[...].astype(F32) + d[...].astype(F32)).astype(BF16)


class GradSum:
    def __init__(self, place, first, lo, w, g, bufs, sems, n):
        b1, r1, b2, r2, zb = bufs
        send, recv = sems
        self.place, self.cols, self.r2, self.zb, self.n = place, pl.ds(lo, w), r2, zb, n
        self.send, self.recv = send, recv
        cols = self.cols
        second = "y" if first == "x" else "x"
        if first == "x":
            half1 = lambda d, h: g.at[h, d, :, :, cols]
        else:
            half1 = lambda d, h: g.at[h, :, d, :, cols]
        self.one = RingSum(
            place, first, half1, lambda k: b1.at[k, :, :, cols], lambda h: r1.at[h, :, :, cols],
            lambda k: send.at[n, k], lambda k: recv.at[n, k], add2_lead, add3_lead,
        )
        self.two = RingSum(
            place, second, lambda d, h: r1.at[h, d, :, cols], lambda k: b2.at[k, :, cols],
            lambda h: r2.at[h, :, cols], lambda k: send.at[n, 6 + k], lambda k: recv.at[n, 6 + k],
            add2_flat, add3_flat,
        )

    def zcp(self):
        other = 1 - self.place.zl
        return remote(
            self.r2.at[other, :, self.cols], self.zb.at[:, self.cols], self.send.at[self.n, 12],
            self.recv.at[self.n, 12], self.place.at(zl=other),
        )

    def total(self):
        self.zcp().wait_recv()
        own = self.r2[self.place.zl, :, self.cols].astype(F32)
        return own + self.zb[:, self.cols].astype(F32)

    def end(self):
        self.one.end()
        self.two.end()
        self.zcp().wait_send()


def grad_scratch(width, pieces):
    return [
        pltpu.VMEM((6, 4, 48, width), BF16),
        pltpu.VMEM((2, 4, 48, width), BF16),
        pltpu.VMEM((6, 48, width), BF16),
        pltpu.VMEM((2, 48, width), BF16),
        pltpu.VMEM((48, width), BF16),
        pltpu.SemaphoreType.DMA((pieces, 13)),
        pltpu.SemaphoreType.DMA((pieces, 13)),
    ]


AR_PIECES = 4
AR_ROWS = ROWS // 2 // AR_PIECES


class TpSum:
    def __init__(self, place, part, total, buf, sems):
        self.place, self.part, self.total, self.buf = place, part, total, buf
        self.send, self.recv = sems
        self.core = place.at(c=1 - place.c)
        self.far = place.at(zh=1 - place.zh)

    def a(self, k):
        return remote(
            self.part.at[1 - self.place.c, k], self.buf.at[0, k], self.send.at[0, k], self.recv.at[0, k], self.core
        )

    def b(self, k):
        return remote(self.buf.at[0, k], self.buf.at[1, k], self.send.at[1, k], self.recv.at[1, k], self.far)

    def d(self, k):
        rows = self.total.at[self.place.c, k]
        return remote(rows, rows, self.send.at[2, k], self.recv.at[2, k], self.core)

    def start(self):
        for k in range(AR_PIECES):
            self.a(k).start()

    def mid(self):
        for k in range(AR_PIECES):
            self.a(k).wait_recv()
            self.buf[0, k] = self.buf[0, k] + self.part[self.place.c, k]
            self.b(k).start()

    def fin(self):
        for k in range(AR_PIECES):
            self.b(k).wait_recv()
            self.total[self.place.c, k] = self.buf[0, k] + self.buf[1, k]
            self.d(k).start()

    def landed(self):
        for k in range(AR_PIECES):
            rows = self.total.at[1 - self.place.c, k]
            remote(rows, rows, self.send.at[2, k], self.recv.at[2, k], self.core).wait_recv()

    def end(self):
        for k in range(AR_PIECES):
            self.a(k).wait_send()
            self.b(k).wait_send()
            self.d(k).wait_send()


def tp_scratch():
    return [
        pltpu.VMEM((2, AR_PIECES, AR_ROWS, WIDTH), BF16),
        pltpu.SemaphoreType.DMA((3, AR_PIECES)),
        pltpu.SemaphoreType.DMA((3, AR_PIECES)),
    ]


def ar_view(value):
    return value.reshape(2, AR_PIECES, AR_ROWS, WIDTH)


def ar_load(ref):
    return ref[...].reshape(ROWS, WIDTH)


def front_kernel(
    lengths, freq, tokens, gain, wq, wk, wv, wo,
    normed_out, qkv, kvall, att, o_out, lse_out, wo_full,
    grp, qaug, acc, peak, total, mine,
    pair_sem, ag_send, ag_recv, o_send, o_recv, w_send, w_recv, loc_sem,
):
    place = Place()
    zl, x, y, zh, c = place.zl, place.x, place.y, place.zh, place.c
    partner = place.at(**place.pair)
    far_partner = place.at(**place.pair, zh=1 - zh)
    far = place.at(zh=1 - zh)
    core = place.at(c=1 - c)
    xr, xl, yr, yl = place.along("x", 1), place.along("x", -1), place.along("y", 1), place.along("y", -1)
    greet([partner, far_partner, far, core, xr, xl, yr, yl])
    ends = ends_of(lengths)
    block = zl * 16 + x * 4 + y
    cosine, sine = rotation(ends, lengths, block * ROWS, freq[...])
    source = tokens[...].astype(F32)
    inverse = lax.rsqrt(jnp.mean(source * source, -1, keepdims=True) + EPS)
    normed = (source * inverse * gain[...]).astype(BF16)
    normed_out[...] = normed

    def turned(u, factor):
        a, b = u[:HALF], u[HALF:]
        if factor is None:
            return a * cosine - b * sine, b * cosine + a * sine
        return (a * cosine - b * sine) * factor, (b * cosine + a * sine) * factor

    qt = dot(normed, wq[...]).T
    kt = dot(normed, wk[...]).T
    vt = dot(normed, wv[...]).T
    for g in range(2):
        for h in range(2):
            a, b = turned(qt[(2 * g + h) * HEAD : (2 * g + h + 1) * HEAD], SCALE * LOG2E)
            grp[g, h * HEAD : h * HEAD + HALF] = a.astype(BF16)
            grp[g, h * HEAD + HALF : (h + 1) * HEAD] = b.astype(BF16)
        a, b = turned(kt[g * HEAD : (g + 1) * HEAD], None)
        grp[g, 2 * HEAD : 2 * HEAD + HALF] = a.astype(BF16)
        grp[g, 2 * HEAD + HALF : 3 * HEAD] = b.astype(BF16)
        grp[g, 3 * HEAD :] = vt[g * HEAD : (g + 1) * HEAD].astype(BF16)

    pair_cp = remote(grp.at[1 - zl], qkv.at[zl], pair_sem.at[0], pair_sem.at[1], partner)
    pair_cp.start()
    qkv[zl] = grp[zl]
    kvall[x, y, zl] = grp[zl, 2 * HEAD :]
    me_t = zh * 2 + c
    wo_local = pltpu.make_async_copy(wo, wo_full.at[me_t], loc_sem.at[0])
    wo_local.start()
    pair_cp.wait_recv()
    kvall[x, y, 1 - zl] = qkv[1 - zl, 2 * HEAD :]

    def gather(slot, first):
        swap = first == "y"
        me1, me2 = (y, x) if swap else (x, y)
        r1, l1, r2, l2 = (yr, yl, xr, xl) if swap else (xr, xl, yr, yl)

        def ref(i, j, part=None):
            i, j = lax.rem(i + 4, 4), lax.rem(j + 4, 4)
            v = kvall.at[j, i, slot] if swap else kvall.at[i, j, slot]
            return v if part is None else v.at[pl.ds(part * HEAD, HEAD)]

        def cp(n, view, dev):
            return remote(view, view, ag_send.at[slot, n], ag_recv.at[slot, n], dev)

        def stage(base, i, j, di, dj, r, l):
            own = (i, j)
            return dict(
                right=cp(base, ref(i, j), r),
                left=cp(base + 1, ref(i, j), l),
                from_left=cp(base, ref(i - di, j - dj), r),
                from_right=cp(base + 1, ref(i + di, j + dj), l),
                on_right=cp(base + 2, ref(i - di, j - dj, 0), r),
                on_left=cp(base + 3, ref(i + di, j + dj, 1), l),
                from_left2=cp(base + 2, ref(i + 2 * di, j + 2 * dj, 0), r),
                from_right2=cp(base + 3, ref(i + 2 * di, j + 2 * dj, 1), l),
            )

        s1 = stage(0, me1, me2, 1, 0, r1, l1)
        s2 = [stage(4 + 4 * k, me1 + k, me2, 0, 1, r2, l2) for k in range(4)]
        return s1, s2

    ga, gb = gather(0, "x"), gather(1, "y")
    both = (ga, gb)
    for s1, s2 in both:
        s1["right"].start()
        s1["left"].start()
    for s1, s2 in both:
        s2[0]["right"].start()
        s2[0]["left"].start()
    wo_cps = [
        remote(wo, wo_full.at[me_t], w_send.at[0], w_recv.at[0], far),
        remote(wo, wo_full.at[me_t], w_send.at[1], w_recv.at[1], core),
    ]
    for cp in wo_cps:
        cp.start()
    for s1, s2 in both:
        s1["from_left"].wait_recv()
        s1["on_right"].start()
        s1["from_right"].wait_recv()
        s1["on_left"].start()
    for k in (3, 1):
        for s1, s2 in both:
            s2[k]["right"].start()
            s2[k]["left"].start()
    for s1, s2 in both:
        s2[0]["from_left"].wait_recv()
        s2[0]["on_right"].start()
        s2[0]["from_right"].wait_recv()
        s2[0]["on_left"].start()
    for s1, s2 in both:
        s1["from_left2"].wait_recv()
        s1["from_right2"].wait_recv()
        s2[2]["right"].start()
        s2[2]["left"].start()
    for k in (3, 1, 2):
        for s1, s2 in both:
            s2[k]["from_left"].wait_recv()
            s2[k]["on_right"].start()
            s2[k]["from_right"].wait_recv()
            s2[k]["on_left"].start()
    for k in (0, 3, 1, 2):
        for s1, s2 in both:
            s2[k]["from_left2"].wait_recv()
            s2[k]["from_right2"].wait_recv()

    low = place.low_block(x, y)
    for s in range(2):
        base = jnp.where(s == 0, low, 31 - low) * ROWS
        segs = query_segments(ends, base)
        for h in range(2):
            qaug[s, :HEAD, h * ROWS : (h + 1) * ROWS] = qkv[s, h * HEAD : (h + 1) * HEAD]
            qaug[s, HEAD:, h * ROWS : (h + 1) * ROWS] = segs
    peak[...] = jnp.full(peak.shape, -BIG, F32)
    total[...] = jnp.zeros(total.shape, F32)
    acc[...] = jnp.zeros(acc.shape, F32)

    def unit(qs, kx, ky, ks, kbase, causal):
        kv = kvall[kx, ky, ks]
        ka = jnp.concatenate([kv[:HEAD], key_segments(ends, kbase)], 0)
        s = dot(ka, qaug[qs], 0, 0)
        if causal:
            key = lax.broadcasted_iota(jnp.int32, (ROWS, 2 * ROWS), 0)
            query = lax.broadcasted_iota(jnp.int32, (ROWS, 2 * ROWS), 1)
            s = jnp.where(key <= jnp.where(query >= ROWS, query - ROWS, query), s, -BIG)
        old = peak[qs]
        new = jnp.maximum(old, jnp.max(s, 0, keepdims=True))
        p = jnp.exp2(s - new)
        fade = jnp.exp2(old - new)
        peak[qs] = new
        total[qs] = total[qs] * fade + jnp.sum(p, 0, keepdims=True)
        acc[qs] = acc[qs] * fade + dot(kv[HEAD:], p.astype(BF16))

    unit(0, x, y, 0, low * ROWS, True)
    unit(1, x, y, 1, (31 - low) * ROWS, True)
    unit(1, x, y, 0, low * ROWS, False)

    def step(i, carry):
        kx, ky = lax.rem(x + i // 4, 4), lax.rem(y + i % 4, 4)
        there = place.low_block(kx, ky)
        unit(1, kx, ky, 0, there * ROWS, False)
        sel = jnp.where(there < low, 0, 1)
        unit(sel, kx, ky, sel, jnp.where(there < low, there, 31 - there) * ROWS, False)
        return carry

    lax.fori_loop(1, 16, step, 0)
    for s in range(2):
        out = acc[s] / total[s]
        lse_out[s] = peak[s] + jnp.log2(total[s])
        for h in range(2):
            part = out[:, h * ROWS : (h + 1) * ROWS]
            o_out[s, h * HEAD : (h + 1) * HEAD] = part
            mine[s, h * HEAD : (h + 1) * HEAD] = part.astype(BF16)

    group = me_t * 2 + zl
    att[group] = mine[zl]
    sends = [
        remote(mine.at[1 - zl], att.at[group], o_send.at[0], o_recv.at[0], partner),
        remote(mine.at[1 - zl], att.at[group], o_send.at[1], o_recv.at[1], far_partner),
        remote(mine.at[zl], att.at[group], o_send.at[2], o_recv.at[2], far),
    ]
    for cp in sends:
        cp.start()
    there_t = (1 - zh) * 2 + c
    order = [
        (None, group), (0, me_t * 2 + 1 - zl), (1, there_t * 2 + 1 - zl), (2, there_t * 2 + zl),
    ]
    relays = []
    for n, (sem, which) in enumerate(order):
        if sem is not None:
            remote(att.at[which], att.at[which], o_send.at[sem], o_recv.at[sem], far).wait_recv()
        cp = remote(att.at[which], att.at[which], o_send.at[3 + n], o_recv.at[3 + n], core)
        cp.start()
        relays.append(cp)
    wo_far = wo_full.at[there_t]
    remote(wo_far, wo_far, w_send.at[0], w_recv.at[0], far).wait_recv()
    wo_relay = remote(wo_far, wo_far, w_send.at[2], w_recv.at[2], core)
    wo_relay.start()
    mine_t, other_t = zh * 2 + (1 - c), (1 - zh) * 2 + (1 - c)
    for n, which in enumerate([mine_t * 2 + zl, mine_t * 2 + 1 - zl, other_t * 2 + 1 - zl, other_t * 2 + zl]):
        remote(att.at[which], att.at[which], o_send.at[3 + n], o_recv.at[3 + n], core).wait_recv()
    w1, w2 = wo_full.at[mine_t], wo_full.at[other_t]
    remote(w1, w1, w_send.at[1], w_recv.at[1], core).wait_recv()
    remote(w2, w2, w_send.at[2], w_recv.at[2], core).wait_recv()
    wo_local.wait()
    pair_cp.wait_send()
    for s1, s2 in both:
        for st in [s1, *s2]:
            for name in ("right", "left", "on_right", "on_left"):
                st[name].wait_send()
    for cp in [*wo_cps, wo_relay, *sends, *relays]:
        cp.wait_send()


def front(lengths, freq, tokens, gain, wq, wk, wv, wo):
    vm = pl.BlockSpec(memory_space=pltpu.VMEM)
    anywhere = pl.BlockSpec(memory_space=pl.ANY)
    dma = pltpu.SemaphoreType.DMA
    return pl.pallas_call(
        front_kernel,
        out_shape=(
            jax.ShapeDtypeStruct((ROWS, WIDTH), BF16),
            jax.ShapeDtypeStruct((2, 4 * HEAD, ROWS), BF16),
            jax.ShapeDtypeStruct((4, 4, 2, 2 * HEAD, ROWS), BF16),
            jax.ShapeDtypeStruct((8, 2 * HEAD, ROWS), BF16),
            jax.ShapeDtypeStruct((2, 2 * HEAD, ROWS), F32),
            jax.ShapeDtypeStruct((2, 1, 2 * ROWS), F32),
            jax.ShapeDtypeStruct((4, HEADS_LOCAL, WIDTH), BF16),
        ),
        in_specs=[pl.BlockSpec(memory_space=pltpu.SMEM), vm, vm, vm, vm, vm, vm, anywhere],
        out_specs=(vm, vm, vm, vm, vm, vm, anywhere),
        scratch_shapes=[
            pltpu.VMEM((2, 4 * HEAD, ROWS), BF16),
            pltpu.VMEM((2, HEAD + SEG, 2 * ROWS), BF16),
            pltpu.VMEM((2, HEAD, 2 * ROWS), F32),
            pltpu.VMEM((2, 1, 2 * ROWS), F32),
            pltpu.VMEM((2, 1, 2 * ROWS), F32),
            pltpu.VMEM((2, 2 * HEAD, ROWS), BF16),
            dma((2,)),
            dma((2, 20)),
            dma((2, 20)),
            dma((7,)),
            dma((7,)),
            dma((3,)),
            dma((3,)),
            dma((1,)),
        ],
        compiler_params=pltpu.CompilerParams(
            collective_id=0, has_side_effects=True, vmem_limit_bytes=VMEM_LIMIT
        ),
        name="front",
    )(lengths, freq, tokens, gain, wq, wk, wv, wo)


W_FFN = 3 * FFL
W_MID = W_FFN + HEADS_LOCAL


def norm_back(source, inverse, gain, grad):
    scaled = grad * gain
    gain_grad = jnp.sum(grad * source * inverse, 0, keepdims=True)
    mean = jnp.mean(scaled * source, -1, keepdims=True)
    return inverse * scaled - source * (inverse * inverse * inverse) * mean, gain_grad


def middle_kernel(
    tokens, cot, att, wo, gain, wg, wu, wd,
    result, grads, mixed_grad_out, dout, gain_grad_out,
    gate_s, upper_s, left, part3, part2, tot3, tot2, buf3, s3, r3, buf2, s2, r2, dgrp, pair_sem,
):
    place = Place()
    partner = place.at(**place.pair)
    greet([partner, place.at(zh=1 - place.zh), place.at(c=1 - place.c)])
    zl = place.zl
    mixed = tokens[...].astype(F32)
    mixed = mixed + dot(att[...].reshape(WIDTH, ROWS), wo[...].reshape(WIDTH, WIDTH), 0, 0)
    inverse = lax.rsqrt(jnp.mean(mixed * mixed, -1, keepdims=True) + EPS)
    normed = (mixed * inverse * gain[...]).astype(BF16)
    gate_s[...] = dot(normed, wg[...])
    upper_s[...] = dot(normed, wu[...])
    hidden_grad = dot(cot[...], wd[...], 1, 1)
    gate, upper = gate_s[...], upper_s[...]
    sig = jax.nn.sigmoid(gate)
    silu = gate * sig
    hidden = (silu * upper).astype(BF16)
    gate_grad = (hidden_grad * upper * sig * (1.0 + gate * (1.0 - sig))).astype(BF16)
    upper_grad = (hidden_grad * silu).astype(BF16)
    back = dot(gate_grad, wg[...], 1, 1) + dot(upper_grad, wu[...], 1, 1)
    part3[...] = ar_view(back.astype(BF16))
    sum3 = TpSum(place, part3, tot3, buf3, (s3, r3))
    sum3.start()
    part2[...] = ar_view(dot(hidden, wd[...]).astype(BF16))
    sum3.mid()
    sum2 = TpSum(place, part2, tot2, buf2, (s2, r2))
    sum2.start()

    def weight_grad(lhs, rhs, lo, cb=0):
        left[...] = lhs.T
        w = rhs.shape[1 - cb]

        def rows(i, carry):
            piece = dot(left[pl.ds(pl.multiple_of(i * 192, 192), 192)], rhs, 1, cb)
            grads[i // 4, i % 4, :, :, lo : lo + w] = piece.astype(BF16).reshape(4, 48, w)
            return carry

        lax.fori_loop(0, 8, rows, 0)

    weight_grad(normed, gate_grad, 0)
    weight_grad(normed, upper_grad, FFL)
    sum2.mid()
    weight_grad(cot[...], hidden, 2 * FFL)
    sum3.fin()
    sum3.landed()
    grad = ar_load(tot3).astype(F32)
    mixed_part, gain_grad = norm_back(mixed, inverse, gain[...], grad)
    gain_grad_out[...] = gain_grad
    mixed_grad = cot[...].astype(F32) + mixed_part
    mixed_grad_out[...] = mixed_grad
    branch = mixed_grad.astype(BF16)
    me_t = place.zh * 2 + place.c
    own = dot(wo[me_t], branch, 1, 1).astype(BF16)
    dgrp[0] = own[: 2 * HEAD]
    dgrp[1] = own[2 * HEAD :]
    pair_cp = remote(dgrp.at[1 - zl], dout.at[zl], pair_sem.at[0], pair_sem.at[1], partner)
    pair_cp.start()
    dout[zl] = dgrp[zl]
    heads = att[pl.ds(me_t * 2, 2)].reshape(HEADS_LOCAL, ROWS)
    weight_grad(branch, heads, W_FFN, 1)
    sum2.fin()
    sum2.landed()
    result[...] = (mixed + ar_load(tot2).astype(F32)).astype(BF16)
    pair_cp.wait_recv()
    pair_cp.wait_send()
    sum3.end()
    sum2.end()


def middle(tokens, cot, att, wo, gain, wg, wu, wd):
    vm = pl.BlockSpec(memory_space=pltpu.VMEM)
    shape = (2, AR_PIECES, AR_ROWS, WIDTH)
    return pl.pallas_call(
        middle_kernel,
        out_shape=(
            jax.ShapeDtypeStruct((ROWS, WIDTH), BF16),
            jax.ShapeDtypeStruct((2, 4, 4, 48, W_MID), BF16),
            jax.ShapeDtypeStruct((ROWS, WIDTH), F32),
            jax.ShapeDtypeStruct((2, 2 * HEAD, ROWS), BF16),
            jax.ShapeDtypeStruct((1, WIDTH), F32),
        ),
        in_specs=[vm] * 8,
        out_specs=(vm,) * 5,
        scratch_shapes=[
            pltpu.VMEM((ROWS, FFL), F32),
            pltpu.VMEM((ROWS, FFL), F32),
            pltpu.VMEM((WIDTH, ROWS), BF16),
            pltpu.VMEM(shape, BF16),
            pltpu.VMEM(shape, BF16),
            pltpu.VMEM(shape, BF16),
            pltpu.VMEM(shape, BF16),
            *tp_scratch(),
            *tp_scratch(),
            pltpu.VMEM((2, 2 * HEAD, ROWS), BF16),
            pltpu.SemaphoreType.DMA((2,)),
        ],
        compiler_params=pltpu.CompilerParams(
            collective_id=1, has_side_effects=True, vmem_limit_bytes=VMEM_LIMIT
        ),
        name="middle",
    )(tokens, cot, att, wo, gain, wg, wu, wd)


def cut(width, first="x", sizes=(3, 4)):
    pieces, lo, n = [], 0, 0
    order = ("x", "y") if first == "x" else ("y", "x")
    while lo < width:
        w = min(sizes[n % len(sizes)] * 128, width - lo)
        pieces.append((order[n % 2], lo, w))
        lo += w
        n += 1
    return pieces


MID_PIECES = cut(W_MID, "x", (3, 4))


def back_kernel(
    lengths, qkv, kvall, o_in, lse, dout, grads,
    dqkv, sums,
    qaug, dot_t, delta, dq, dkv, mine,
    kb1, kr1, kb2, kr2, ksend, krecv,
    b1, r1, b2, r2, zb, gsend, grecv, pair_sem,
):
    place = Place()
    zl, x, y = place.zl, place.x, place.y
    partner = place.at(**place.pair)
    greet(
        [partner, place.at(zl=1 - zl)]
        + [place.along(a, s) for a in ("x", "y") for s in (1, -1)]
    )
    pieces = [
        GradSum(place, first, lo, w, grads, (b1, r1, b2, r2, zb), (gsend, grecv), n)
        for n, (first, lo, w) in enumerate(MID_PIECES)
    ]
    for piece in pieces:
        piece.one.start()
    ends = ends_of(lengths)
    low = place.low_block(x, y)
    for s in range(2):
        segs = query_segments(ends, jnp.where(s == 0, low, 31 - low) * ROWS)
        for h in range(2):
            lanes, feats = slice(h * ROWS, (h + 1) * ROWS), slice(h * HEAD, (h + 1) * HEAD)
            qaug[s, :HEAD, lanes] = qkv[s, feats]
            qaug[s, HEAD:, lanes] = segs
            d = dout[s, feats]
            dot_t[s, :, lanes] = d
            delta[s, :, lanes] = jnp.sum(d.astype(F32) * o_in[s, feats], 0, keepdims=True)
    dq[...] = jnp.zeros(dq.shape, F32)

    def unit(qs, kx, ky, ks, kbase, causal):
        kv = kvall[kx, ky, ks]
        q = qaug[qs]
        do = dot_t[qs]
        ka = jnp.concatenate([kv[:HEAD], key_segments(ends, kbase)], 0)
        s = dot(ka, q, 0, 0)
        p = jnp.exp2(s - lse[qs])
        if causal:
            key = lax.broadcasted_iota(jnp.int32, (ROWS, 2 * ROWS), 0)
            query = lax.broadcasted_iota(jnp.int32, (ROWS, 2 * ROWS), 1)
            p = jnp.where(key <= jnp.where(query >= ROWS, query - ROWS, query), p, 0.0)
        dp = dot(kv[HEAD:], do, 0, 0)
        ds = (p * (dp - delta[qs])).astype(BF16)
        dq[qs] = dq[qs] + dot(kv[:HEAD], ds)
        dk = dot(q[:HEAD], ds, 1, 1)
        dv = dot(do, p.astype(BF16), 1, 1)
        return jnp.concatenate([dk, dv], 0)

    first = unit(0, x, y, 0, low * ROWS, True) + unit(1, x, y, 0, low * ROWS, False)
    dkv[x, y, 0] = first.astype(BF16)
    dkv[x, y, 1] = unit(1, x, y, 1, (31 - low) * ROWS, True).astype(BF16)

    def step(i, carry):
        kx, ky = lax.rem(x + i // 4, 4), lax.rem(y + i % 4, 4)
        there = place.low_block(kx, ky)
        one = unit(1, kx, ky, 0, there * ROWS, False)
        before = there < low
        sel = jnp.where(before, 0, 1)
        two = unit(sel, kx, ky, sel, jnp.where(before, there, 31 - there) * ROWS, False)
        share = jnp.where(before, 1.0, 0.0)
        dkv[kx, ky, 0] = (one + two * share).astype(BF16)
        dkv[kx, ky, 1] = (two * (1.0 - share)).astype(BF16)
        return carry

    lax.fori_loop(1, 6, step, 0)
    for piece in pieces:
        piece.one.mid()
    lax.fori_loop(6, 16, step, 0)

    def key_sum(slot, axis):
        other = "y" if axis == "x" else "x"
        if axis == "x":
            half = lambda d, h: dkv.at[d, :, slot, pl.ds(h * HEAD, HEAD)]
        else:
            half = lambda d, h: dkv.at[:, d, slot, pl.ds(h * HEAD, HEAD)]
        one = RingSum(
            place, axis, half, lambda k: kb1.at[slot, k], lambda h: kr1.at[slot, h],
            lambda k: ksend.at[slot, k], lambda k: krecv.at[slot, k], add2_lead, add3_lead,
        )
        two = RingSum(
            place, other, lambda d, h: kr1.at[slot, h, d], lambda k: kb2.at[slot, k],
            lambda h: kr2.at[slot, h], lambda k: ksend.at[slot, 6 + k], lambda k: krecv.at[slot, 6 + k],
            add2_flat, add3_flat,
        )
        return one, two

    ka, kb = key_sum(0, "x"), key_sum(1, "y")
    ka[0].start()
    kb[0].start()
    for piece in pieces:
        piece.one.fin()
        piece.two.start()
    ka[0].mid()
    kb[0].mid()
    for piece in pieces:
        piece.two.mid()
    ka[0].fin()
    kb[0].fin()
    ka[1].start()
    kb[1].start()
    for piece in pieces:
        piece.two.fin()
        piece.zcp().start()
    ka[1].mid()
    kb[1].mid()
    ka[1].fin()
    kb[1].fin()
    for s in range(2):
        for h in range(2):
            mine[s, h * HEAD : (h + 1) * HEAD] = (dq[s, :, h * ROWS : (h + 1) * ROWS] * SCALE).astype(BF16)
            mine[s, (2 + h) * HEAD : (3 + h) * HEAD] = kr2[s, h]
    pair_cp = remote(mine.at[1 - zl], dqkv.at[zl], pair_sem.at[0], pair_sem.at[1], partner)
    pair_cp.start()
    dqkv[zl] = mine[zl]
    for piece, (_, lo, w) in zip(pieces, MID_PIECES):
        sums[:, lo : lo + w] = piece.total()
    landing = dqkv.at[1 - zl]
    pair_cp.wait_send()
    remote(landing, landing, pair_sem.at[0], pair_sem.at[1], partner).wait_recv()
    for piece in pieces:
        piece.end()
    for one, two in (ka, kb):
        one.end()
        two.end()


def back(lengths, qkv, kvall, o_in, lse, dout, grads):
    vm = pl.BlockSpec(memory_space=pltpu.VMEM)
    dma = pltpu.SemaphoreType.DMA
    return pl.pallas_call(
        back_kernel,
        out_shape=(
            jax.ShapeDtypeStruct((2, 4 * HEAD, ROWS), BF16),
            jax.ShapeDtypeStruct((48, W_MID), F32),
        ),
        in_specs=[pl.BlockSpec(memory_space=pltpu.SMEM)] + [vm] * 6,
        out_specs=(vm,) * 2,
        scratch_shapes=[
            pltpu.VMEM((2, HEAD + SEG, 2 * ROWS), BF16),
            pltpu.VMEM((2, HEAD, 2 * ROWS), BF16),
            pltpu.VMEM((2, 1, 2 * ROWS), F32),
            pltpu.VMEM((2, HEAD, 2 * ROWS), F32),
            pltpu.VMEM((4, 4, 2, 2 * HEAD, ROWS), BF16),
            pltpu.VMEM((2, 4 * HEAD, ROWS), BF16),
            pltpu.VMEM((2, 6, 4, HEAD, ROWS), BF16),
            pltpu.VMEM((2, 2, 4, HEAD, ROWS), BF16),
            pltpu.VMEM((2, 6, HEAD, ROWS), BF16),
            pltpu.VMEM((2, 2, HEAD, ROWS), BF16),
            dma((2, 12)),
            dma((2, 12)),
            *grad_scratch(W_MID, len(MID_PIECES)),
            dma((2,)),
        ],
        compiler_params=pltpu.CompilerParams(
            collective_id=2, has_side_effects=True, vmem_limit_bytes=VMEM_LIMIT
        ),
        name="back",
    )(lengths, qkv, kvall, o_in, lse, dout, grads)


W_TAIL = HEADS_LOCAL + 2 * PAIRS_LOCAL
TAIL_PIECES = cut(W_TAIL, "x", (1, 1, 2, 2))
GAIN_ROWS = 2 * WIDTH // 128


def tail_kernel(
    lengths, freq, tokens, gain, normed, dqkv, wq, wk, wv, mixed_grad, ffn_gain_grad,
    tokens_grad, sums, gains,
    rows, left, grads, part, total, buf, s4, r4,
    b1, r1, b2, r2, zb, gsend, grecv, gain_buf, gain_sum, gn_send, gn_recv,
):
    place = Place()
    zl, x, y = place.zl, place.x, place.y
    others = [place.along(a, s) for a in ("x", "y") for s in (1, 2, 3)]
    greet(others + [place.at(zl=1 - zl), place.at(zh=1 - place.zh), place.at(c=1 - place.c)])
    ends = ends_of(lengths)
    block = zl * 16 + x * 4 + y
    cosine, sine = rotation(ends, lengths, block * ROWS, freq[...])
    for g in range(2):
        for h in range(3):
            a = dqkv[g, h * HEAD : h * HEAD + HALF].astype(F32)
            b = dqkv[g, h * HEAD + HALF : (h + 1) * HEAD].astype(F32)
            if h == 2:
                a, b = a * LN2, b * LN2
            at = (2 * g + h) * HEAD if h < 2 else HEADS_LOCAL + g * HEAD
            rows[at : at + HALF] = (a * cosine + b * sine).astype(BF16)
            rows[at + HALF : at + HEAD] = (b * cosine - a * sine).astype(BF16)
        at = HEADS_LOCAL + PAIRS_LOCAL + g * HEAD
        rows[at : at + HEAD] = dqkv[g, 3 * HEAD :]
    back = dot(rows[:HEADS_LOCAL], wq[...], 0, 1)
    back = back + dot(rows[HEADS_LOCAL : HEADS_LOCAL + PAIRS_LOCAL], wk[...], 0, 1)
    back = back + dot(rows[HEADS_LOCAL + PAIRS_LOCAL :], wv[...], 0, 1)
    part[...] = ar_view(back.astype(BF16))
    sum4 = TpSum(place, part, total, buf, (s4, r4))
    sum4.start()
    left[...] = normed[...].T

    def weight_rows(i, carry):
        piece = dot(left[pl.ds(pl.multiple_of(i * 192, 192), 192)], rows[...], 1, 1)
        grads[i // 4, i % 4] = piece.astype(BF16).reshape(4, 48, W_TAIL)
        return carry

    lax.fori_loop(0, 8, weight_rows, 0)
    pieces = [
        GradSum(place, first, lo, w, grads, (b1, r1, b2, r2, zb), (gsend, grecv), n)
        for n, (first, lo, w) in enumerate(TAIL_PIECES)
    ]
    for piece in pieces:
        piece.one.start()
    sum4.mid()
    for piece in pieces:
        piece.one.mid()
    sum4.fin()
    sum4.landed()
    source = tokens[...].astype(F32)
    inverse = lax.rsqrt(jnp.mean(source * source, -1, keepdims=True) + EPS)
    grad = ar_load(total).astype(F32)
    source_part, gain_grad = norm_back(source, inverse, gain[...], grad)
    tokens_grad[...] = (mixed_grad[...] + source_part).astype(BF16)
    gain_sum[0, 0:1] = gain_grad
    gain_sum[0, 1:2] = ffn_gain_grad[...]

    def gain_copies(stage, axis):
        if axis == "zl":
            peers = [place.at(zl=1 - zl)]
        else:
            peers = [place.along(axis, s) for s in (1, 2, 3)]
        return [
            remote(gain_sum.at[stage], gain_buf.at[stage, k], gn_send.at[stage, k], gn_recv.at[stage, k], peer)
            for k, peer in enumerate(peers)
        ]

    sent = gain_copies(0, "x")
    for cp in sent:
        cp.start()
    for piece in pieces:
        piece.one.fin()
        piece.two.start()
    for cp in sent:
        cp.wait_recv()
    gain_sum[1] = gain_sum[0] + gain_buf[0, 0] + gain_buf[0, 1] + gain_buf[0, 2]
    sent_y = gain_copies(1, "y")
    for cp in sent_y:
        cp.start()
    for piece in pieces:
        piece.two.mid()
    for cp in sent_y:
        cp.wait_recv()
    gain_sum[2] = gain_sum[1] + gain_buf[1, 0] + gain_buf[1, 1] + gain_buf[1, 2]
    sent_z = gain_copies(2, "zl")
    for cp in sent_z:
        cp.start()
    for piece in pieces:
        piece.two.fin()
        piece.zcp().start()
    for cp in sent_z:
        cp.wait_recv()
    gains[...] = gain_sum[2] + gain_buf[2, 0]
    for piece, (_, lo, w) in zip(pieces, TAIL_PIECES):
        sums[:, lo : lo + w] = piece.total()
    for cp in [*sent, *sent_y, *sent_z]:
        cp.wait_send()
    for piece in pieces:
        piece.end()
    sum4.end()


def tail(lengths, freq, tokens, gain, normed, dqkv, wq, wk, wv, mixed_grad, ffn_gain_grad):
    vm = pl.BlockSpec(memory_space=pltpu.VMEM)
    dma = pltpu.SemaphoreType.DMA
    shape = (2, AR_PIECES, AR_ROWS, WIDTH)
    return pl.pallas_call(
        tail_kernel,
        out_shape=(
            jax.ShapeDtypeStruct((ROWS, WIDTH), BF16),
            jax.ShapeDtypeStruct((48, W_TAIL), F32),
            jax.ShapeDtypeStruct((2, WIDTH), F32),
        ),
        in_specs=[pl.BlockSpec(memory_space=pltpu.SMEM)] + [vm] * 10,
        out_specs=(vm,) * 3,
        scratch_shapes=[
            pltpu.VMEM((W_TAIL, ROWS), BF16),
            pltpu.VMEM((WIDTH, ROWS), BF16),
            pltpu.VMEM((2, 4, 4, 48, W_TAIL), BF16),
            pltpu.VMEM(shape, BF16),
            pltpu.VMEM(shape, BF16),
            *tp_scratch(),
            *grad_scratch(W_TAIL, len(TAIL_PIECES)),
            pltpu.VMEM((3, 3, 2, WIDTH), F32),
            pltpu.VMEM((3, 2, WIDTH), F32),
            dma((3, 3)),
            dma((3, 3)),
        ],
        compiler_params=pltpu.CompilerParams(
            collective_id=3, has_side_effects=True, vmem_limit_bytes=VMEM_LIMIT
        ),
        name="tail",
    )(lengths, freq, tokens, gain, normed, dqkv, wq, wk, wv, mixed_grad, ffn_gain_grad)


def local(
    tokens, norm_gain, query_weight, key_matrix, value_matrix, out_weight,
    ffn_gain, gate_weight, up_weight, down_weight, cotangent, lengths,
):
    freq = jnp.asarray(
        (THETA ** (-2.0 * np.arange(HALF) / HEAD)).astype(np.float32).reshape(HALF, 1)
    )
    gain1, gain2 = norm_gain.reshape(1, WIDTH), ffn_gain.reshape(1, WIDTH)
    normed, qkv, kvall, att, o, lse, wo_full = front(
        lengths, freq, tokens, gain1, query_weight, key_matrix, value_matrix, out_weight
    )
    result, grads, mixed_grad, dout, ffn_gain_grad = middle(
        tokens, cotangent, att, wo_full, gain2, gate_weight, up_weight, down_weight
    )
    dqkv, mid_sums = back(lengths, qkv, kvall, o, lse, dout, grads)
    tokens_grad, sums, gains = tail(
        lengths, freq, tokens, gain1, normed, dqkv, query_weight, key_matrix, value_matrix,
        mixed_grad, ffn_gain_grad,
    )
    block = (lax.axis_index("zl") * 4 + lax.axis_index("x")) * 4 + lax.axis_index("y")
    own = lax.dynamic_slice(gains, (0, block * 48), (2, 48))
    return (
        result,
        tokens_grad,
        own[0],
        sums[:, :HEADS_LOCAL],
        sums[:, HEADS_LOCAL : HEADS_LOCAL + PAIRS_LOCAL],
        sums[:, HEADS_LOCAL + PAIRS_LOCAL :],
        mid_sums[:, W_FFN:].T,
        own[1],
        mid_sums[:, :FFL],
        mid_sums[:, FFL : 2 * FFL],
        mid_sums[:, 2 * FFL : W_FFN].T,
    )


def solution(mesh):
    split = Mesh(mesh.devices.reshape(2, 4, 4, 2, 2), AXES)
    in_specs = (
        P(BLK, None),
        P(),
        P(None, TP),
        P(None, TP),
        P(None, TP),
        P(TP, None),
        P(),
        P(None, TP),
        P(None, TP),
        P(TP, None),
        P(BLK, None),
        P(),
    )
    out_specs = (
        P(BLK, None),
        P(BLK, None),
        P(BLK),
        P(BLK, TP),
        P(BLK, TP),
        P(BLK, TP),
        P(TP, BLK),
        P(BLK),
        P(BLK, TP),
        P(BLK, TP),
        P(TP, BLK),
    )
    return jax.shard_map(local, mesh=split, in_specs=in_specs, out_specs=out_specs, check_vma=False)
```

time: 1340 us -> 255 us (0.19)
  waiting for transfers between devices: 1030 us -> 0 us
  Pallas kernels: 0 us -> 239 us
  local copies, waits for them, and re-layouts: 140 us -> 13.9 us
  blocking collectives: 42.1 us -> 0 us
  matrix products: 34.6 us -> 0 us
  other arithmetic: 31.5 us -> 0 us
  loops' own time: 23.2 us -> 0 us
  starting transfers between devices: 14.8 us -> 0 us
  between operations: 15 us -> 0.71 us
    reduce_scatter x5 -> x0, waiting for transfers between devices: 441 us -> none  [the longest x3 211 us: own_block(): parts = lax.psum_scatter(parts, axes[k], scatter_dimension=0, tiled=True)]
    unnamed x10 -> x0, waiting for transfers between devices: 329 us -> none
    pallas_call x0 -> x4, Pallas kernels: none -> 239 us  [the longest x1 96.2 us: back(): pl.pallas_call(back_kernel, out_shape=(jax.ShapeDtypeStruct((2, 4 * HEAD,...]
    all_gather x1 -> x0, waiting for transfers between devices: 151 us -> none  [local(): piece = lax.all_gather(key_value, BLK, axis=0, tiled=True)]
    all_to_all x3 -> x0, waiting for transfers between devices: 108 us -> none  [sent_to_all(): return lax.all_to_all(copies, axis, split_axis=0, concat_axis=0, tiled=True)]
    all_to_all x1 -> x0, blocking collectives: 42.1 us -> none  [sent_to_all(): return lax.all_to_all(copies, axis, split_axis=0, concat_axis=0, tiled=True)]
    dot_general x28 -> x0, matrix products: 34.6 us -> none  [the longest x1 2.9 us: local(): jnp.dot(hidden, down_weight, preferred_element_type=jnp.float32)]
    concatenate x1 -> x0, local copies, waits for them, and re-layouts: 31.4 us -> none  [side_by_side(): both = jnp.concatenate(columns, axis=along)]
  transfers between devices with their start and end apart: 11 -> 0, of which waited for: 10 -> 0; matrix products, arithmetic and copies ran while one was open for 7% -> 0% of each run, Pallas kernels for 0% -> 0%
where the time goes in v1:
time: 255 us; the launch traced here: 254 us
  Pallas kernels  239 us (94%)
  local copies, waits for them, and re-layouts  13.9 us (5%)
    pallas_call x1, Pallas kernels, back(): pl.pallas_call(back_kernel, out_shape=(jax.ShapeDtypeStruct((2, 4 * HEAD,...  96.2 us
    pallas_call x1, Pallas kernels, front(): pl.pallas_call(front_kernel, out_shape=(jax.ShapeDtypeStruct((ROWS, WIDTH...  66.2 us
    pallas_call x1, Pallas kernels, middle(): pl.pallas_call(middle_kernel, out_shape=(jax.ShapeDtypeStruct((ROWS, WIDT...  43.6 us
    pallas_call x1, Pallas kernels, tail(): pl.pallas_call(tail_kernel, out_shape=(jax.ShapeDtypeStruct((ROWS, WIDTH)...  33.3 us
    unnamed x12, local copies, waits for them, and re-layouts  6.22 us

profile of v1, /device:TPU:0, one launch (start us, length us, event | category | flops | bytes accessed | tf_op | source)
XLA Modules:
  0.0 254.0 jit_solution(3009507594579540682)
XLA Ops:
  0.6 2.2 copy.24.wk
  2.9 0.0 copy-start.3
  2.9 2.2 copy.25.wv
  5.1 1.3 reshape.28.gain
  6.4 66.2 %front.1 = (bf16[256,1536]{1,0:T(8,128)(2,1)}, bf16[2,384,256]{2,1,0:T(8,128)(2,1)}, bf16[4,4,2,192,256]{4,3,2,1,0:T(8,128)(2,1)}, bf16[8,192,256]{2,1,0:T(8,128...) custom-call(s32[5]{0:T(128)} %lengths.5, f32[48,1]{1,0:T(8,128)} %constant.25.clone.freq, ...), custom_call_target="tpu_custom_call" | custom-call | tf_op jit(solution)/shard_map/front/pallas_call | solution.py:512
  72.6 0.0 copy-done.3
  72.6 0.6 reshape.29.gain
  73.2 43.6 %middle.1 = (bf16[256,1536]{1,0:T(8,128)(2,1)}, bf16[2,4,4,48,3456]{4,3,2,1,0:T(8,128)(2,1)}, f32[256,1536]{1,0:T(8,128)}, bf16[2,192,256]{2,1,0:T(8,128)(2,1)}, f32[1,1536]{1,0:T(1,128)}) custom-call(bf16[256,1536]{1,0:T(8,128)(2,1)} %tokens.5, bf16[256,1536]{1,0:T(8,128)(2,1)} %cot.1, bf16[8,192,256]{2,1,0:T(8,128)(2,1)} %get-tuple-element.28.att, ...), custom_call_target="tpu_custom_call" | custom-call | tf_op jit(solution)/shard_map/middle/pallas_call | solution.py:634
  116.8 96.2 %back.1 = (bf16[2,384,256]{2,1,0:T(8,128)(2,1)}, f32[48,3456]{1,0:T(8,128)}) custom-call(s32[5]{0:T(128)} %lengths.5, bf16[2,384,256]{2,1,0:T(8,128)(2,1)} %get-tuple-element.32.qkv, bf16[4,4,2,192,256]{4,3,2,1,0:T(8,128)(2,1)} %get-tuple-element.33.kvall, f32[2,192,256]{2,1,0:T(8,128)} %get-tuple-element.34.o_in, f32[2,1,512]{2,1,0:T(1,128)} %get-tuple-element.35.lse, ...), custom_call_target="tpu_custom_call" | custom-call | tf_op jit(solution)/shard_map/back/pallas_call | solution.py:811
  213.0 0.0 copy-start.2
  213.0 0.0 copy-start
  213.0 33.3 %tail.1 = (bf16[256,1536]{1,0:T(8,128)(2,1)}, f32[48,768]{1,0:T(8,128)}, f32[2,1536]{1,0:T(2,128)}) custom-call(s32[5]{0:T(128)} %lengths.5, f32[48,1]{1,0:T(8,128)} %constant.25.clone.freq, bf16[256,1536]{1,0:T(8,128)(2,1)} %tokens.5, f32[1,1536]{1,0:T(1,128)} %reshape.28.gain, bf16[256,1536]{1,0:T(8,128)(2,1)} %get-tuple-element.31.normed, ...), custom_call_target="tpu_custom_call" | custom-call | tf_op jit(solution)/shard_map/tail/pallas_call | solution.py:953
  246.4 0.0 copy-start.1
  246.4 1.6 fusion
  248.0 1.5 slice.28
  249.5 0.7 constant_dynamic-slice_fusion
  250.2 0.5 slice_bitcast_fusion.2
  250.8 0.0 copy-done.2
  250.8 0.8 slice_bitcast_fusion
  251.6 0.6 slice_bitcast_fusion.1
  252.2 0.0 copy-done
  252.2 0.9 copy.30
  253.1 0.0 copy-done.1
  253.1 0.9 copy.31
Async XLA Ops:
  2.9 69.7 %copy-start.3 = (f32[1536]{0:T(1024)S(1)}, f32[1536]{0:T(1024)}, u32[]{:S(2)}) copy-start(f32[1536]{0:T(1024)} %param.19) | copy-start | bytes 18436
  213.0 37.8 %copy-start.2 = (f32[48,3456]{1,0:T(8,128)S(1)}, f32[48,3456]{1,0:T(8,128)}, u32[]{:S(2)}) copy-start(f32[48,3456]{1,0:T(8,128)} %get-tuple-element.44) | copy-start | bytes 1990660
  213.0 39.2 %copy-start = (bf16[256,1536]{1,0:T(8,128)(2,1)S(1)}, bf16[256,1536]{1,0:T(8,128)(2,1)}, u32[]{:S(2)}) copy-start(bf16[256,1536]{1,0:T(8,128)(2,1)} %get-tuple-element.63) | copy-start | bytes 2359300
  246.4 6.7 %copy-start.1 = (bf16[256,1536]{1,0:T(8,128)(2,1)S(1)}, bf16[256,1536]{1,0:T(8,128)(2,1)}, u32[]{:S(2)}) copy-start(bf16[256,1536]{1,0:T(8,128)(2,1)} %get-tuple-element.64) | copy-start | bytes 2359300

commit v2 on v1

--- a/solution.py
+++ b/solution.py
@@ -55,11 +55,14 @@
         return jnp.where(self.zl == 0, p, 15 - p)
 
 
-def greet(peers):
+def call(peers):
     barrier = pltpu.get_barrier_semaphore()
     for peer in peers:
         pl.semaphore_signal(barrier, inc=1, device_id=peer, device_id_type=MESH)
-    pl.semaphore_wait(barrier, len(peers))
+
+
+def answer(peers):
+    pl.semaphore_wait(pltpu.get_barrier_semaphore(), len(peers))
 
 
 def remote(src, dst, send, recv, device):
@@ -293,10 +296,10 @@
 
 
 def front_kernel(
-    lengths, freq, tokens, gain, wq, wk, wv, wo,
+    lengths, freq, tokens, gain, wq, wkt, wvt, wo,
     normed_out, qkv, kvall, att, o_out, lse_out, wo_full,
     grp, qaug, acc, peak, total, mine,
-    pair_sem, ag_send, ag_recv, o_send, o_recv, w_send, w_recv, loc_sem,
+    pair_sem, ag_send, ag_recv, o_send, o_recv, w_send, w_recv,
 ):
     place = Place()
     zl, x, y, zh, c = place.zl, place.x, place.y, place.zh, place.c
@@ -305,13 +308,14 @@
     far = place.at(zh=1 - zh)
     core = place.at(c=1 - c)
     xr, xl, yr, yl = place.along("x", 1), place.along("x", -1), place.along("y", 1), place.along("y", -1)
-    greet([partner, far_partner, far, core, xr, xl, yr, yl])
+    peers = [partner, far_partner, far, core, xr, xl, yr, yl]
+    call(peers)
     ends = ends_of(lengths)
     block = zl * 16 + x * 4 + y
     cosine, sine = rotation(ends, lengths, block * ROWS, freq[...])
     source = tokens[...].astype(F32)
     inverse = lax.rsqrt(jnp.mean(source * source, -1, keepdims=True) + EPS)
-    normed = (source * inverse * gain[...]).astype(BF16)
+    normed = (source * inverse * gain[...].reshape(1, WIDTH)).astype(BF16)
     normed_out[...] = normed
 
     def turned(u, factor):
@@ -321,8 +325,8 @@
         return (a * cosine - b * sine) * factor, (b * cosine + a * sine) * factor
 
     qt = dot(normed, wq[...]).T
-    kt = dot(normed, wk[...]).T
-    vt = dot(normed, wv[...]).T
+    kt = dot(wkt[...], normed, 1, 1)
+    vt = dot(wvt[...], normed, 1, 1)
     for g in range(2):
         for h in range(2):
             a, b = turned(qt[(2 * g + h) * HEAD : (2 * g + h + 1) * HEAD], SCALE * LOG2E)
@@ -333,18 +337,13 @@
         grp[g, 2 * HEAD + HALF : 3 * HEAD] = b.astype(BF16)
         grp[g, 3 * HEAD :] = vt[g * HEAD : (g + 1) * HEAD].astype(BF16)
 
+    answer(peers)
     pair_cp = remote(grp.at[1 - zl], qkv.at[zl], pair_sem.at[0], pair_sem.at[1], partner)
     pair_cp.start()
     qkv[zl] = grp[zl]
     kvall[x, y, zl] = grp[zl, 2 * HEAD :]
-    me_t = zh * 2 + c
-    wo_local = pltpu.make_async_copy(wo, wo_full.at[me_t], loc_sem.at[0])
-    wo_local.start()
-    pair_cp.wait_recv()
-    kvall[x, y, 1 - zl] = qkv[1 - zl, 2 * HEAD :]
-
-    def gather(slot, first):
-        swap = first == "y"
+
+    def gather(n, slot, swap):
         me1, me2 = (y, x) if swap else (x, y)
         r1, l1, r2, l2 = (yr, yl, xr, xl) if swap else (xr, xl, yr, yl)
 
@@ -353,11 +352,10 @@
             v = kvall.at[j, i, slot] if swap else kvall.at[i, j, slot]
             return v if part is None else v.at[pl.ds(part * HEAD, HEAD)]
 
-        def cp(n, view, dev):
-            return remote(view, view, ag_send.at[slot, n], ag_recv.at[slot, n], dev)
+        def cp(k, view, dev):
+            return remote(view, view, ag_send.at[n, k], ag_recv.at[n, k], dev)
 
         def stage(base, i, j, di, dj, r, l):
-            own = (i, j)
             return dict(
                 right=cp(base, ref(i, j), r),
                 left=cp(base + 1, ref(i, j), l),
@@ -373,49 +371,35 @@
         s2 = [stage(4 + 4 * k, me1 + k, me2, 0, 1, r2, l2) for k in range(4)]
         return s1, s2
 
-    ga, gb = gather(0, "x"), gather(1, "y")
-    both = (ga, gb)
-    for s1, s2 in both:
-        s1["right"].start()
-        s1["left"].start()
-    for s1, s2 in both:
-        s2[0]["right"].start()
-        s2[0]["left"].start()
+    def begin(st):
+        st["right"].start()
+        st["left"].start()
+
+    def hand_on(st):
+        st["from_left"].wait_recv()
+        st["on_right"].start()
+        st["from_right"].wait_recv()
+        st["on_left"].start()
+
+    def complete(st):
+        st["from_left2"].wait_recv()
+        st["from_right2"].wait_recv()
+
+    own, other = gather(0, zl, False), gather(1, 1 - zl, True)
+    both = (own, other)
+    begin(own[0])
+    begin(own[1][0])
+    pair_cp.wait_recv()
+    kvall[x, y, 1 - zl] = qkv[1 - zl, 2 * HEAD :]
+    begin(other[0])
+    begin(other[1][0])
+    me_t = zh * 2 + c
     wo_cps = [
         remote(wo, wo_full.at[me_t], w_send.at[0], w_recv.at[0], far),
         remote(wo, wo_full.at[me_t], w_send.at[1], w_recv.at[1], core),
     ]
     for cp in wo_cps:
         cp.start()
-    for s1, s2 in both:
-        s1["from_left"].wait_recv()
-        s1["on_right"].start()
-        s1["from_right"].wait_recv()
-        s1["on_left"].start()
-    for k in (3, 1):
-        for s1, s2 in both:
-            s2[k]["right"].start()
-            s2[k]["left"].start()
-    for s1, s2 in both:
-        s2[0]["from_left"].wait_recv()
-        s2[0]["on_right"].start()
-        s2[0]["from_right"].wait_recv()
-        s2[0]["on_left"].start()
-    for s1, s2 in both:
-        s1["from_left2"].wait_recv()
-        s1["from_right2"].wait_recv()
-        s2[2]["right"].start()
-        s2[2]["left"].start()
-    for k in (3, 1, 2):
-        for s1, s2 in both:
-            s2[k]["from_left"].wait_recv()
-            s2[k]["on_right"].start()
-            s2[k]["from_right"].wait_recv()
-            s2[k]["on_left"].start()
-    for k in (0, 3, 1, 2):
-        for s1, s2 in both:
-            s2[k]["from_left2"].wait_recv()
-            s2[k]["from_right2"].wait_recv()
 
     low = place.low_block(x, y)
     for s in range(2):
@@ -444,19 +428,48 @@
         total[qs] = total[qs] * fade + jnp.sum(p, 0, keepdims=True)
         acc[qs] = acc[qs] * fade + dot(kv[HEAD:], p.astype(BF16))
 
-    unit(0, x, y, 0, low * ROWS, True)
-    unit(1, x, y, 1, (31 - low) * ROWS, True)
-    unit(1, x, y, 0, low * ROWS, False)
-
-    def step(i, carry):
-        kx, ky = lax.rem(x + i // 4, 4), lax.rem(y + i % 4, 4)
+    def shard(dx, dy):
+        kx, ky = lax.rem(x + dx, 4), lax.rem(y + dy, 4)
         there = place.low_block(kx, ky)
         unit(1, kx, ky, 0, there * ROWS, False)
         sel = jnp.where(there < low, 0, 1)
         unit(sel, kx, ky, sel, jnp.where(there < low, there, 31 - there) * ROWS, False)
-        return carry
-
-    lax.fori_loop(1, 16, step, 0)
+
+    def shards(count, offsets):
+        def step(i, carry):
+            shard(*offsets(i))
+            return carry
+
+        lax.fori_loop(0, count, step, 0)
+
+    unit(0, x, y, 0, low * ROWS, True)
+    unit(1, x, y, 1, (31 - low) * ROWS, True)
+    unit(1, x, y, 0, low * ROWS, False)
+    for s1, s2 in both:
+        hand_on(s1)
+        begin(s2[3])
+        begin(s2[1])
+    for s1, s2 in both:
+        hand_on(s2[0])
+    shards(4, lambda i: ((1 - i // 2) * (2 * i + 1), (i // 2) * (2 * i - 3)))
+    for s1, s2 in both:
+        complete(s1)
+        begin(s2[2])
+    for s1, s2 in both:
+        hand_on(s2[3])
+        hand_on(s2[1])
+    shards(4, lambda i: (2 * (i // 2) + 1, 2 * lax.rem(i, 2) + 1))
+    for s1, s2 in both:
+        complete(s2[0])
+        hand_on(s2[2])
+    shards(2, lambda i: (2 * i, 2 - 2 * i))
+    for s1, s2 in both:
+        complete(s2[3])
+        complete(s2[1])
+    shards(4, lambda i: ((1 - i // 2) * (2 * i + 1) + 2 * (i // 2), (i // 2) * (2 * i - 3) + 2 * (1 - i // 2)))
+    for s1, s2 in both:
+        complete(s2[2])
+    shard(2, 2)
     for s in range(2):
         out = acc[s] / total[s]
         lse_out[s] = peak[s] + jnp.log2(total[s])
@@ -475,6 +488,10 @@
     for cp in sends:
         cp.start()
     there_t = (1 - zh) * 2 + c
+    wo_far = wo_full.at[there_t]
+    remote(wo_far, wo_far, w_send.at[0], w_recv.at[0], far).wait_recv()
+    wo_relay = remote(wo_far, wo_far, w_send.at[2], w_recv.at[2], core)
+    wo_relay.start()
     order = [
         (None, group), (0, me_t * 2 + 1 - zl), (1, there_t * 2 + 1 - zl), (2, there_t * 2 + zl),
     ]
@@ -485,17 +502,12 @@
         cp = remote(att.at[which], att.at[which], o_send.at[3 + n], o_recv.at[3 + n], core)
         cp.start()
         relays.append(cp)
-    wo_far = wo_full.at[there_t]
-    remote(wo_far, wo_far, w_send.at[0], w_recv.at[0], far).wait_recv()
-    wo_relay = remote(wo_far, wo_far, w_send.at[2], w_recv.at[2], core)
-    wo_relay.start()
     mine_t, other_t = zh * 2 + (1 - c), (1 - zh) * 2 + (1 - c)
     for n, which in enumerate([mine_t * 2 + zl, mine_t * 2 + 1 - zl, other_t * 2 + 1 - zl, other_t * 2 + zl]):
         remote(att.at[which], att.at[which], o_send.at[3 + n], o_recv.at[3 + n], core).wait_recv()
     w1, w2 = wo_full.at[mine_t], wo_full.at[other_t]
     remote(w1, w1, w_send.at[1], w_recv.at[1], core).wait_recv()
     remote(w2, w2, w_send.at[2], w_recv.at[2], core).wait_recv()
-    wo_local.wait()
     pair_cp.wait_send()
     for s1, s2 in both:
         for st in [s1, *s2]:
@@ -505,7 +517,7 @@
         cp.wait_send()
 
 
-def front(lengths, freq, tokens, gain, wq, wk, wv, wo):
+def front(lengths, freq, tokens, gain, wq, wkt, wvt, wo):
     vm = pl.BlockSpec(memory_space=pltpu.VMEM)
     anywhere = pl.BlockSpec(memory_space=pl.ANY)
     dma = pltpu.SemaphoreType.DMA
@@ -536,17 +548,18 @@
             dma((7,)),
             dma((3,)),
             dma((3,)),
-            dma((1,)),
         ],
         compiler_params=pltpu.CompilerParams(
             collective_id=0, has_side_effects=True, vmem_limit_bytes=VMEM_LIMIT
         ),
         name="front",
-    )(lengths, freq, tokens, gain, wq, wk, wv, wo)
+    )(lengths, freq, tokens, gain, wq, wkt, wvt, wo)
 
 
 W_FFN = 3 * FFL
 W_MID = W_FFN + HEADS_LOCAL
+FF_CHUNKS = 4
+FF_CHUNK = FFL // FF_CHUNKS
 
 
 def norm_back(source, inverse, gain, grad):
@@ -556,180 +569,209 @@
     return inverse * scaled - source * (inverse * inverse * inverse) * mean, gain_grad
 
 
+def cut(lo, width, sizes, order):
+    pieces, end, n = [], lo + width, 0
+    while lo < end:
+        w = min(sizes[n % len(sizes)] * 128, end - lo)
+        pieces.append((order[n % len(order)], lo, w))
+        lo += w
+        n += 1
+    return pieces
+
+
+DOWN_PIECES = cut(2 * FFL, FFL, (4, 4), "xy")
+GATE_PIECES = cut(0, FFL, (4, 4), "xy")
+UP_PIECES = cut(FFL, FFL, (4, 4), "xy")
+OUT_PIECES = cut(W_FFN, HEADS_LOCAL, (1, 2), "xy")
+MID_PIECES = DOWN_PIECES + GATE_PIECES + UP_PIECES + OUT_PIECES
+
+
 def middle_kernel(
-    tokens, cot, att, wo, gain, wg, wu, wd,
-    result, grads, mixed_grad_out, dout, gain_grad_out,
-    gate_s, upper_s, left, part3, part2, tot3, tot2, buf3, s3, r3, buf2, s2, r2, dgrp, pair_sem,
+    lengths, tokens, cot, att, wo_full, wo_own, gain1, wg, wu, wd, qkv, kv_hbm, o_in, lse,
+    mixed_out, feed_out, mixed_grad_out, gain_grad_out, dqkv, sums,
+    wo_buf, gu_buf, d_buf, mixed, back, feed, normed, hidden, gate_grad, upper_grad, left, grads,
+    part3, tot3, buf3, s3, r3, part2, buf2, s2, r2,
+    kv, qaug, dot_t, delta, dq, dgrp, dout, mine,
+    kb1, kr1, kb2, kr2, ksend, krecv,
+    b1, r1, b2, r2_, zb, gsend, grecv, pair_sem, load_sem, ff_sem, wo_sem,
 ):
     place = Place()
+    zl, x, y = place.zl, place.x, place.y
     partner = place.at(**place.pair)
-    greet([partner, place.at(zh=1 - place.zh), place.at(c=1 - place.c)])
-    zl = place.zl
-    mixed = tokens[...].astype(F32)
-    mixed = mixed + dot(att[...].reshape(WIDTH, ROWS), wo[...].reshape(WIDTH, WIDTH), 0, 0)
-    inverse = lax.rsqrt(jnp.mean(mixed * mixed, -1, keepdims=True) + EPS)
-    normed = (mixed * inverse * gain[...]).astype(BF16)
-    gate_s[...] = dot(normed, wg[...])
-    upper_s[...] = dot(normed, wu[...])
-    hidden_grad = dot(cot[...], wd[...], 1, 1)
-    gate, upper = gate_s[...], upper_s[...]
-    sig = jax.nn.sigmoid(gate)
-    silu = gate * sig
-    hidden = (silu * upper).astype(BF16)
-    gate_grad = (hidden_grad * upper * sig * (1.0 + gate * (1.0 - sig))).astype(BF16)
-    upper_grad = (hidden_grad * silu).astype(BF16)
-    back = dot(gate_grad, wg[...], 1, 1) + dot(upper_grad, wu[...], 1, 1)
-    part3[...] = ar_view(back.astype(BF16))
+    peers = [partner, place.at(zl=1 - zl), place.at(zh=1 - place.zh), place.at(c=1 - place.c)]
+    peers += [place.along(a, s) for a in ("x", "y") for s in (1, -1)]
+    call(peers)
+    me_t = place.zh * 2 + place.c
+
+    def load_wo(t, slot, own=False):
+        if own:
+            pltpu.make_async_copy(wo_own, wo_buf.at[slot], wo_sem.at[slot]).start()
+            return
+
+        @pl.when(me_t == t)
+        def _():
+            pltpu.make_async_copy(wo_own, wo_buf.at[slot], wo_sem.at[slot]).start()
+
+        @pl.when(me_t != t)
+        def _():
+            pltpu.make_async_copy(wo_full.at[t], wo_buf.at[slot], wo_sem.at[slot]).start()
+
+    def wo_ready(slot):
+        pltpu.make_async_copy(wo_own, wo_buf.at[slot], wo_sem.at[slot]).wait()
+
+    def ff_loads(k):
+        slot, cols = k % 2, pl.ds(k * FF_CHUNK, FF_CHUNK)
+        return [
+            pltpu.make_async_copy(wg.at[:, cols], gu_buf.at[slot, :, pl.ds(0, FF_CHUNK)], ff_sem.at[slot, 0]),
+            pltpu.make_async_copy(wu.at[:, cols], gu_buf.at[slot, :, pl.ds(FF_CHUNK, FF_CHUNK)], ff_sem.at[slot, 1]),
+            pltpu.make_async_copy(wd.at[cols], d_buf.at[slot], ff_sem.at[slot, 2]),
+        ]
+
+    load_wo(0, 0)
+    load_wo(1, 1)
+    for k in range(2):
+        for cp in ff_loads(k):
+            cp.start()
+    kv_load = pltpu.make_async_copy(kv_hbm, kv, load_sem.at[0])
+    kv_load.start()
+
+    mixed[...] = tokens[...].astype(F32)
+    for t in range(4):
+        wo_ready(t % 2)
+        heads = att[2 * t : 2 * t + 2].reshape(HEADS_LOCAL, ROWS)
+        mixed[...] = mixed[...] + dot(heads, wo_buf[t % 2], 0, 0)
+        if t < 2:
+            load_wo(t + 2, t % 2)
+        elif t == 2:
+            load_wo(0, 0, own=True)
+    gain = gain1[...].reshape(1, WIDTH)
+    inverse = lax.rsqrt(jnp.mean(mixed[...] * mixed[...], -1, keepdims=True) + EPS)
+    normed[...] = (mixed[...] * inverse * gain).astype(BF16)
+    mixed_save = pltpu.make_async_copy(mixed, mixed_out, load_sem.at[1])
+    mixed_save.start()
+
+    for k in range(FF_CHUNKS):
+        slot, cols = k % 2, slice(k * FF_CHUNK, (k + 1) * FF_CHUNK)
+        for cp in ff_loads(k):
+            cp.wait()
+        both = dot(normed[...], gu_buf[slot])
+        gate, upper = both[:, :FF_CHUNK], both[:, FF_CHUNK:]
+        hidden_grad = dot(cot[...], d_buf[slot], 1, 1)
+        sig = jax.nn.sigmoid(gate)
+        silu = gate * sig
+        hid = (silu * upper).astype(BF16)
+        gg = (hidden_grad * upper * sig * (1.0 + gate * (1.0 - sig))).astype(BF16)
+        ug = (hidden_grad * silu).astype(BF16)
+        hidden[:, cols], gate_grad[:, cols], upper_grad[:, cols] = hid, gg, ug
+        add_back = dot(jnp.concatenate([gg, ug], 1), gu_buf[slot], 1, 1)
+        add_feed = dot(hid, d_buf[slot])
+        if k == 0:
+            back[...], feed[...] = add_back, add_feed
+        else:
+            back[...] = back[...] + add_back
+            feed[...] = feed[...] + add_feed
+        if k + 2 < FF_CHUNKS:
+            for cp in ff_loads(k + 2):
+                cp.start()
+    part3[...] = ar_view(back[...].astype(BF16))
+    answer(peers)
     sum3 = TpSum(place, part3, tot3, buf3, (s3, r3))
     sum3.start()
-    part2[...] = ar_view(dot(hidden, wd[...]).astype(BF16))
-    sum3.mid()
-    sum2 = TpSum(place, part2, tot2, buf2, (s2, r2))
-    sum2.start()
+    part2[...] = ar_view(feed[...].astype(BF16))
 
     def weight_grad(lhs, rhs, lo, cb=0):
         left[...] = lhs.T
         w = rhs.shape[1 - cb]
 
         def rows(i, carry):
-            piece = dot(left[pl.ds(pl.multiple_of(i * 192, 192), 192)], rhs, 1, cb)
+            piece = dot(left[pl.ds(pl.multiple_of(i * 192, 192), 192)], rhs[...], 1, cb)
             grads[i // 4, i % 4, :, :, lo : lo + w] = piece.astype(BF16).reshape(4, 48, w)
             return carry
 
         lax.fori_loop(0, 8, rows, 0)
 
-    weight_grad(normed, gate_grad, 0)
-    weight_grad(normed, upper_grad, FFL)
-    sum2.mid()
+    pieces = [
+        GradSum(place, first, lo, w, grads, (b1, r1, b2, r2_, zb), (gsend, grecv), n)
+        for n, (first, lo, w) in enumerate(MID_PIECES)
+    ]
+    n_down, n_gate, n_up = len(DOWN_PIECES), len(GATE_PIECES), len(UP_PIECES)
+    ready = 0
+
+    def start_pieces(count):
+        nonlocal ready
+        for piece in pieces[ready : ready + count]:
+            piece.one.start()
+        ready += count
+
+    sum3.mid()
     weight_grad(cot[...], hidden, 2 * FFL)
+    start_pieces(n_down)
+    weight_grad(normed[...], gate_grad, 0)
+    start_pieces(n_gate)
+    weight_grad(normed[...], upper_grad, FFL)
+    start_pieces(n_up)
+    sum2 = TpSum(place, part2, feed_out, buf2, (s2, r2))
+    sum2.start()
+    ends = ends_of(lengths)
+    low = place.low_block(x, y)
+    for s in range(2):
+        segs = query_segments(ends, jnp.where(s == 0, low, 31 - low) * ROWS)
+        for h in range(2):
+            lanes = slice(h * ROWS, (h + 1) * ROWS)
+            qaug[s, :HEAD, lanes] = qkv[s, h * HEAD : (h + 1) * HEAD]
+            qaug[s, HEAD:, lanes] = segs
+    dq[...] = jnp.zeros(dq.shape, F32)
     sum3.fin()
     sum3.landed()
-    grad = ar_load(tot3).astype(F32)
-    mixed_part, gain_grad = norm_back(mixed, inverse, gain[...], grad)
+    mixed_part, gain_grad = norm_back(mixed[...], inverse, gain, ar_load(tot3).astype(F32))
     gain_grad_out[...] = gain_grad
-    mixed_grad = cot[...].astype(F32) + mixed_part
-    mixed_grad_out[...] = mixed_grad
-    branch = mixed_grad.astype(BF16)
-    me_t = place.zh * 2 + place.c
-    own = dot(wo[me_t], branch, 1, 1).astype(BF16)
+    back[...] = cot[...].astype(F32) + mixed_part
+    mixed_grad_save = pltpu.make_async_copy(back, mixed_grad_out, load_sem.at[2])
+    mixed_grad_save.start()
+    branch = back[...].astype(BF16)
+    wo_ready(0)
+    own = dot(wo_buf[0], branch, 1, 1).astype(BF16)
     dgrp[0] = own[: 2 * HEAD]
     dgrp[1] = own[2 * HEAD :]
     pair_cp = remote(dgrp.at[1 - zl], dout.at[zl], pair_sem.at[0], pair_sem.at[1], partner)
     pair_cp.start()
     dout[zl] = dgrp[zl]
-    heads = att[pl.ds(me_t * 2, 2)].reshape(HEADS_LOCAL, ROWS)
-    weight_grad(branch, heads, W_FFN, 1)
-    sum2.fin()
-    sum2.landed()
-    result[...] = (mixed + ar_load(tot2).astype(F32)).astype(BF16)
+    normed[...] = branch
+    weight_grad(normed[...], att.at[pl.ds(me_t * 2, 2)][...].reshape(HEADS_LOCAL, ROWS), W_FFN, 1)
+    start_pieces(len(OUT_PIECES))
+    sum2.mid()
+    kv_load.wait()
+    for piece in pieces[:2]:
+        piece.one.mid()
     pair_cp.wait_recv()
-    pair_cp.wait_send()
-    sum3.end()
-    sum2.end()
-
-
-def middle(tokens, cot, att, wo, gain, wg, wu, wd):
-    vm = pl.BlockSpec(memory_space=pltpu.VMEM)
-    shape = (2, AR_PIECES, AR_ROWS, WIDTH)
-    return pl.pallas_call(
-        middle_kernel,
-        out_shape=(
-            jax.ShapeDtypeStruct((ROWS, WIDTH), BF16),
-            jax.ShapeDtypeStruct((2, 4, 4, 48, W_MID), BF16),
-            jax.ShapeDtypeStruct((ROWS, WIDTH), F32),
-            jax.ShapeDtypeStruct((2, 2 * HEAD, ROWS), BF16),
-            jax.ShapeDtypeStruct((1, WIDTH), F32),
-        ),
-        in_specs=[vm] * 8,
-        out_specs=(vm,) * 5,
-        scratch_shapes=[
-            pltpu.VMEM((ROWS, FFL), F32),
-            pltpu.VMEM((ROWS, FFL), F32),
-            pltpu.VMEM((WIDTH, ROWS), BF16),
-            pltpu.VMEM(shape, BF16),
-            pltpu.VMEM(shape, BF16),
-            pltpu.VMEM(shape, BF16),
-            pltpu.VMEM(shape, BF16),
-            *tp_scratch(),
-            *tp_scratch(),
-            pltpu.VMEM((2, 2 * HEAD, ROWS), BF16),
-            pltpu.SemaphoreType.DMA((2,)),
-        ],
-        compiler_params=pltpu.CompilerParams(
-            collective_id=1, has_side_effects=True, vmem_limit_bytes=VMEM_LIMIT
-        ),
-        name="middle",
-    )(tokens, cot, att, wo, gain, wg, wu, wd)
-
-
-def cut(width, first="x", sizes=(3, 4)):
-    pieces, lo, n = [], 0, 0
-    order = ("x", "y") if first == "x" else ("y", "x")
-    while lo < width:
-        w = min(sizes[n % len(sizes)] * 128, width - lo)
-        pieces.append((order[n % 2], lo, w))
-        lo += w
-        n += 1
-    return pieces
-
-
-MID_PIECES = cut(W_MID, "x", (3, 4))
-
-
-def back_kernel(
-    lengths, qkv, kvall, o_in, lse, dout, grads,
-    dqkv, sums,
-    qaug, dot_t, delta, dq, dkv, mine,
-    kb1, kr1, kb2, kr2, ksend, krecv,
-    b1, r1, b2, r2, zb, gsend, grecv, pair_sem,
-):
-    place = Place()
-    zl, x, y = place.zl, place.x, place.y
-    partner = place.at(**place.pair)
-    greet(
-        [partner, place.at(zl=1 - zl)]
-        + [place.along(a, s) for a in ("x", "y") for s in (1, -1)]
-    )
-    pieces = [
-        GradSum(place, first, lo, w, grads, (b1, r1, b2, r2, zb), (gsend, grecv), n)
-        for n, (first, lo, w) in enumerate(MID_PIECES)
-    ]
-    for piece in pieces:
-        piece.one.start()
-    ends = ends_of(lengths)
-    low = place.low_block(x, y)
     for s in range(2):
-        segs = query_segments(ends, jnp.where(s == 0, low, 31 - low) * ROWS)
         for h in range(2):
             lanes, feats = slice(h * ROWS, (h + 1) * ROWS), slice(h * HEAD, (h + 1) * HEAD)
-            qaug[s, :HEAD, lanes] = qkv[s, feats]
-            qaug[s, HEAD:, lanes] = segs
             d = dout[s, feats]
             dot_t[s, :, lanes] = d
             delta[s, :, lanes] = jnp.sum(d.astype(F32) * o_in[s, feats], 0, keepdims=True)
-    dq[...] = jnp.zeros(dq.shape, F32)
 
     def unit(qs, kx, ky, ks, kbase, causal):
-        kv = kvall[kx, ky, ks]
+        pair = kv[kx, ky, ks]
         q = qaug[qs]
         do = dot_t[qs]
-        ka = jnp.concatenate([kv[:HEAD], key_segments(ends, kbase)], 0)
+        ka = jnp.concatenate([pair[:HEAD], key_segments(ends, kbase)], 0)
         s = dot(ka, q, 0, 0)
         p = jnp.exp2(s - lse[qs])
         if causal:
             key = lax.broadcasted_iota(jnp.int32, (ROWS, 2 * ROWS), 0)
             query = lax.broadcasted_iota(jnp.int32, (ROWS, 2 * ROWS), 1)
             p = jnp.where(key <= jnp.where(query >= ROWS, query - ROWS, query), p, 0.0)
-        dp = dot(kv[HEAD:], do, 0, 0)
+        dp = dot(pair[HEAD:], do, 0, 0)
         ds = (p * (dp - delta[qs])).astype(BF16)
-        dq[qs] = dq[qs] + dot(kv[:HEAD], ds)
+        dq[qs] = dq[qs] + dot(pair[:HEAD], ds)
         dk = dot(q[:HEAD], ds, 1, 1)
         dv = dot(do, p.astype(BF16), 1, 1)
         return jnp.concatenate([dk, dv], 0)
 
     first = unit(0, x, y, 0, low * ROWS, True) + unit(1, x, y, 0, low * ROWS, False)
-    dkv[x, y, 0] = first.astype(BF16)
-    dkv[x, y, 1] = unit(1, x, y, 1, (31 - low) * ROWS, True).astype(BF16)
+    kv[x, y, 0] = first.astype(BF16)
+    kv[x, y, 1] = unit(1, x, y, 1, (31 - low) * ROWS, True).astype(BF16)
 
     def step(i, carry):
         kx, ky = lax.rem(x + i // 4, 4), lax.rem(y + i % 4, 4)
@@ -739,21 +781,33 @@
         sel = jnp.where(before, 0, 1)
         two = unit(sel, kx, ky, sel, jnp.where(before, there, 31 - there) * ROWS, False)
         share = jnp.where(before, 1.0, 0.0)
-        dkv[kx, ky, 0] = (one + two * share).astype(BF16)
-        dkv[kx, ky, 1] = (two * (1.0 - share)).astype(BF16)
+        kv[kx, ky, 0] = (one + two * share).astype(BF16)
+        kv[kx, ky, 1] = (two * (1.0 - share)).astype(BF16)
         return carry
 
-    lax.fori_loop(1, 6, step, 0)
-    for piece in pieces:
+    def fin(group):
+        for piece in group:
+            piece.one.fin()
+            piece.two.start()
+
+    lax.fori_loop(1, 4, step, 0)
+    for piece in pieces[2:4]:
         piece.one.mid()
-    lax.fori_loop(6, 16, step, 0)
+    lax.fori_loop(4, 7, step, 0)
+    for piece in pieces[4:]:
+        piece.one.mid()
+    lax.fori_loop(7, 10, step, 0)
+    fin(pieces[:2])
+    lax.fori_loop(10, 13, step, 0)
+    fin(pieces[2:4])
+    lax.fori_loop(13, 16, step, 0)
 
     def key_sum(slot, axis):
         other = "y" if axis == "x" else "x"
         if axis == "x":
-            half = lambda d, h: dkv.at[d, :, slot, pl.ds(h * HEAD, HEAD)]
+            half = lambda d, h: kv.at[d, :, slot, pl.ds(h * HEAD, HEAD)]
         else:
-            half = lambda d, h: dkv.at[:, d, slot, pl.ds(h * HEAD, HEAD)]
+            half = lambda d, h: kv.at[:, d, slot, pl.ds(h * HEAD, HEAD)]
         one = RingSum(
             place, axis, half, lambda k: kb1.at[slot, k], lambda h: kr1.at[slot, h],
             lambda k: ksend.at[slot, k], lambda k: krecv.at[slot, k], add2_lead, add3_lead,
@@ -768,9 +822,8 @@
     ka, kb = key_sum(0, "x"), key_sum(1, "y")
     ka[0].start()
     kb[0].start()
-    for piece in pieces:
-        piece.one.fin()
-        piece.two.start()
+    fin(pieces[4:])
+    sum2.fin()
     ka[0].mid()
     kb[0].mid()
     for piece in pieces:
@@ -790,14 +843,20 @@
         for h in range(2):
             mine[s, h * HEAD : (h + 1) * HEAD] = (dq[s, :, h * ROWS : (h + 1) * ROWS] * SCALE).astype(BF16)
             mine[s, (2 + h) * HEAD : (3 + h) * HEAD] = kr2[s, h]
-    pair_cp = remote(mine.at[1 - zl], dqkv.at[zl], pair_sem.at[0], pair_sem.at[1], partner)
-    pair_cp.start()
+    back_cp = remote(mine.at[1 - zl], dqkv.at[zl], pair_sem.at[2], pair_sem.at[3], partner)
+    back_cp.start()
     dqkv[zl] = mine[zl]
     for piece, (_, lo, w) in zip(pieces, MID_PIECES):
         sums[:, lo : lo + w] = piece.total()
     landing = dqkv.at[1 - zl]
+    remote(landing, landing, pair_sem.at[2], pair_sem.at[3], partner).wait_recv()
+    sum2.landed()
+    mixed_save.wait()
+    mixed_grad_save.wait()
     pair_cp.wait_send()
-    remote(landing, landing, pair_sem.at[0], pair_sem.at[1], partner).wait_recv()
+    back_cp.wait_send()
+    sum3.end()
+    sum2.end()
     for piece in pieces:
         piece.end()
     for one, two in (ka, kb):
@@ -805,23 +864,49 @@
         two.end()
 
 
-def back(lengths, qkv, kvall, o_in, lse, dout, grads):
+def middle(lengths, tokens, cot, att, wo_full, wo_own, gain, wg, wu, wd, qkv, kvall, o, lse):
     vm = pl.BlockSpec(memory_space=pltpu.VMEM)
+    hbm = pl.BlockSpec(memory_space=pl.ANY)
     dma = pltpu.SemaphoreType.DMA
+    shape = (2, AR_PIECES, AR_ROWS, WIDTH)
+    wide = pltpu.VMEM((ROWS, WIDTH), F32)
     return pl.pallas_call(
-        back_kernel,
+        middle_kernel,
         out_shape=(
+            jax.ShapeDtypeStruct((ROWS, WIDTH), F32),
+            jax.ShapeDtypeStruct(shape, BF16),
+            jax.ShapeDtypeStruct((ROWS, WIDTH), F32),
+            jax.ShapeDtypeStruct((1, WIDTH), F32),
             jax.ShapeDtypeStruct((2, 4 * HEAD, ROWS), BF16),
             jax.ShapeDtypeStruct((48, W_MID), F32),
         ),
-        in_specs=[pl.BlockSpec(memory_space=pltpu.SMEM)] + [vm] * 6,
-        out_specs=(vm,) * 2,
+        in_specs=[pl.BlockSpec(memory_space=pltpu.SMEM), vm, vm, vm, hbm, hbm, vm, hbm, hbm, hbm, vm, hbm, vm, vm],
+        out_specs=(hbm, vm, hbm, vm, vm, vm),
         scratch_shapes=[
+            pltpu.VMEM((2, HEADS_LOCAL, WIDTH), BF16),
+            pltpu.VMEM((2, WIDTH, 2 * FF_CHUNK), BF16),
+            pltpu.VMEM((2, FF_CHUNK, WIDTH), BF16),
+            wide,
+            wide,
+            wide,
+            pltpu.VMEM((ROWS, WIDTH), BF16),
+            pltpu.VMEM((ROWS, FFL), BF16),
+            pltpu.VMEM((ROWS, FFL), BF16),
+            pltpu.VMEM((ROWS, FFL), BF16),
+            pltpu.VMEM((WIDTH, ROWS), BF16),
+            pltpu.VMEM((2, 4, 4, 48, W_MID), BF16),
+            pltpu.VMEM(shape, BF16),
+            pltpu.VMEM(shape, BF16),
+            *tp_scratch(),
+            pltpu.VMEM(shape, BF16),
+            *tp_scratch(),
+            pltpu.VMEM((4, 4, 2, 2 * HEAD, ROWS), BF16),
             pltpu.VMEM((2, HEAD + SEG, 2 * ROWS), BF16),
             pltpu.VMEM((2, HEAD, 2 * ROWS), BF16),
             pltpu.VMEM((2, 1, 2 * ROWS), F32),
             pltpu.VMEM((2, HEAD, 2 * ROWS), F32),
-            pltpu.VMEM((4, 4, 2, 2 * HEAD, ROWS), BF16),
+            pltpu.VMEM((2, 2 * HEAD, ROWS), BF16),
+            pltpu.VMEM((2, 2 * HEAD, ROWS), BF16),
             pltpu.VMEM((2, 4 * HEAD, ROWS), BF16),
             pltpu.VMEM((2, 6, 4, HEAD, ROWS), BF16),
             pltpu.VMEM((2, 2, 4, HEAD, ROWS), BF16),
@@ -830,22 +915,25 @@
             dma((2, 12)),
             dma((2, 12)),
             *grad_scratch(W_MID, len(MID_PIECES)),
+            dma((4,)),
+            dma((3,)),
+            dma((2, 3)),
             dma((2,)),
         ],
         compiler_params=pltpu.CompilerParams(
-            collective_id=2, has_side_effects=True, vmem_limit_bytes=VMEM_LIMIT
+            collective_id=1, has_side_effects=True, vmem_limit_bytes=VMEM_LIMIT
         ),
-        name="back",
-    )(lengths, qkv, kvall, o_in, lse, dout, grads)
+        name="middle",
+    )(lengths, tokens, cot, att, wo_full, wo_own, gain, wg, wu, wd, qkv, kvall, o, lse)
 
 
 W_TAIL = HEADS_LOCAL + 2 * PAIRS_LOCAL
-TAIL_PIECES = cut(W_TAIL, "x", (1, 1, 2, 2))
+TAIL_PIECES = cut(0, W_TAIL, (1, 1, 2, 2), "xy")
 GAIN_ROWS = 2 * WIDTH // 128
 
 
 def tail_kernel(
-    lengths, freq, tokens, gain, normed, dqkv, wq, wk, wv, mixed_grad, ffn_gain_grad,
+    lengths, freq, tokens, gain, normed, dqkv, wq, wkt, wvt, mixed_grad, ffn_gain_grad,
     tokens_grad, sums, gains,
     rows, left, grads, part, total, buf, s4, r4,
     b1, r1, b2, r2, zb, gsend, grecv, gain_buf, gain_sum, gn_send, gn_recv,
@@ -853,7 +941,9 @@
     place = Place()
     zl, x, y = place.zl, place.x, place.y
     others = [place.along(a, s) for a in ("x", "y") for s in (1, 2, 3)]
-    greet(others + [place.at(zl=1 - zl), place.at(zh=1 - place.zh), place.at(c=1 - place.c)])
+    peers = others + [place.at(zl=1 - zl), place.at(zh=1 - place.zh), place.at(c=1 - place.c)]
+    call(peers)
+    answer(peers)
     ends = ends_of(lengths)
     block = zl * 16 + x * 4 + y
     cosine, sine = rotation(ends, lengths, block * ROWS, freq[...])
@@ -869,8 +959,8 @@
         at = HEADS_LOCAL + PAIRS_LOCAL + g * HEAD
         rows[at : at + HEAD] = dqkv[g, 3 * HEAD :]
     back = dot(rows[:HEADS_LOCAL], wq[...], 0, 1)
-    back = back + dot(rows[HEADS_LOCAL : HEADS_LOCAL + PAIRS_LOCAL], wk[...], 0, 1)
-    back = back + dot(rows[HEADS_LOCAL + PAIRS_LOCAL :], wv[...], 0, 1)
+    back = back + dot(rows[HEADS_LOCAL : HEADS_LOCAL + PAIRS_LOCAL], wkt[...], 0, 0)
+    back = back + dot(rows[HEADS_LOCAL + PAIRS_LOCAL :], wvt[...], 0, 0)
     part[...] = ar_view(back.astype(BF16))
     sum4 = TpSum(place, part, total, buf, (s4, r4))
     sum4.start()
@@ -896,7 +986,7 @@
     source = tokens[...].astype(F32)
     inverse = lax.rsqrt(jnp.mean(source * source, -1, keepdims=True) + EPS)
     grad = ar_load(total).astype(F32)
-    source_part, gain_grad = norm_back(source, inverse, gain[...], grad)
+    source_part, gain_grad = norm_back(source, inverse, gain[...].reshape(1, WIDTH), grad)
     tokens_grad[...] = (mixed_grad[...] + source_part).astype(BF16)
     gain_sum[0, 0:1] = gain_grad
     gain_sum[0, 1:2] = ffn_gain_grad[...]
@@ -946,7 +1036,7 @@
     sum4.end()
 
 
-def tail(lengths, freq, tokens, gain, normed, dqkv, wq, wk, wv, mixed_grad, ffn_gain_grad):
+def tail(lengths, freq, tokens, gain, normed, dqkv, wq, wkt, wvt, mixed_grad, ffn_gain_grad):
     vm = pl.BlockSpec(memory_space=pltpu.VMEM)
     dma = pltpu.SemaphoreType.DMA
     shape = (2, AR_PIECES, AR_ROWS, WIDTH)
@@ -973,10 +1063,10 @@
             dma((3, 3)),
         ],
         compiler_params=pltpu.CompilerParams(
-            collective_id=3, has_side_effects=True, vmem_limit_bytes=VMEM_LIMIT
+            collective_id=2, has_side_effects=True, vmem_limit_bytes=VMEM_LIMIT
         ),
         name="tail",
-    )(lengths, freq, tokens, gain, normed, dqkv, wq, wk, wv, mixed_grad, ffn_gain_grad)
+    )(lengths, freq, tokens, gain, normed, dqkv, wq, wkt, wvt, mixed_grad, ffn_gain_grad)
 
 
 def local(
@@ -986,16 +1076,17 @@
     freq = jnp.asarray(
         (THETA ** (-2.0 * np.arange(HALF) / HEAD)).astype(np.float32).reshape(HALF, 1)
     )
-    gain1, gain2 = norm_gain.reshape(1, WIDTH), ffn_gain.reshape(1, WIDTH)
+    key_t, value_t = key_matrix.T, value_matrix.T
     normed, qkv, kvall, att, o, lse, wo_full = front(
-        lengths, freq, tokens, gain1, query_weight, key_matrix, value_matrix, out_weight
+        lengths, freq, tokens, norm_gain, query_weight, key_t, value_t, out_weight
     )
-    result, grads, mixed_grad, dout, ffn_gain_grad = middle(
-        tokens, cotangent, att, wo_full, gain2, gate_weight, up_weight, down_weight
+    mixed, feed, mixed_grad, ffn_gain_grad, dqkv, mid_sums = middle(
+        lengths, tokens, cotangent, att, wo_full, out_weight, ffn_gain, gate_weight, up_weight, down_weight,
+        qkv, kvall, o, lse,
     )
-    dqkv, mid_sums = back(lengths, qkv, kvall, o, lse, dout, grads)
+    result = (mixed + feed.reshape(ROWS, WIDTH).astype(F32)).astype(BF16)
     tokens_grad, sums, gains = tail(
-        lengths, freq, tokens, gain1, normed, dqkv, query_weight, key_matrix, value_matrix,
+        lengths, freq, tokens, norm_gain, normed, dqkv, query_weight, key_t, value_t,
         mixed_grad, ffn_gain_grad,
     )
     block = (lax.axis_index("zl") * 4 + lax.axis_index("x")) * 4 + lax.axis_index("y")

time: 255 us -> 207 us (0.81)
  Pallas kernels: 239 us -> 198 us
  local copies, waits for them, and re-layouts: 13.9 us -> 6.73 us
    pallas_call x1 -> x0, Pallas kernels: 96.2 us -> none  [back(): pl.pallas_call(back_kernel, out_shape=(jax.ShapeDtypeStruct((2, 4 * HEAD,...]
    pallas_call x1, Pallas kernels: 43.6 us -> 111 us  [middle(): pl.pallas_call(middle_kernel, out_shape=(jax.ShapeDtypeStruct((ROWS, WIDT...]
    pallas_call x1, Pallas kernels: 66.2 us -> 54.3 us  [front(): pl.pallas_call(front_kernel, out_shape=(jax.ShapeDtypeStruct((ROWS, WIDTH...]
    unnamed x12 -> x9, local copies, waits for them, and re-layouts: 6.22 us -> 0.9 us
where the time goes in v2:
time: 207 us; the launch traced here: 206 us
  Pallas kernels  198 us (96%)
  local copies, waits for them, and re-layouts  6.73 us (3%)
    pallas_call x1, Pallas kernels, middle(): pl.pallas_call(middle_kernel, out_shape=(jax.ShapeDtypeStruct((ROWS, WIDT...  111 us
    pallas_call x1, Pallas kernels, front(): pl.pallas_call(front_kernel, out_shape=(jax.ShapeDtypeStruct((ROWS, WIDTH...  54.3 us
    pallas_call x1, Pallas kernels, tail(): pl.pallas_call(tail_kernel, out_shape=(jax.ShapeDtypeStruct((ROWS, WIDTH)...  32.1 us

profile of v2, /device:TPU:0, one launch (start us, length us, event | category | flops | bytes accessed | tf_op | source)
XLA Modules:
  0.0 206.2 jit_solution(11772924163730785342)
XLA Ops:
  0.6 54.3 %front.1 = (bf16[256,1536]{1,0:T(8,128)(2,1)}, bf16[2,384,256]{2,1,0:T(8,128)(2,1)}, bf16[4,4,2,192,256]{4,3,2,1,0:T(8,128)(2,1)}, bf16[8,192,256]{2,1,0:T(8,128...) custom-call(s32[5]{0:T(128)} %lengths.5, f32[48,1]{1,0:T(8,128)} %constant.25.clone.freq, ...), custom_call_target="tpu_custom_call" | custom-call | tf_op jit(solution)/shard_map/front/pallas_call | solution.py:524
  54.9 111.3 %middle.1 = (f32[256,1536]{1,0:T(8,128)}, bf16[2,4,32,1536]{3,2,1,0:T(8,128)(2,1)}, f32[256,1536]{1,0:T(8,128)}, f32[1,1536]{1,0:T(1,128)}, bf16[2,384,256]{2,1,0:T(8,128)(2,1)}, /*index=5*/f32[48,3456]{1,0:T(8,128)}) custom-call(s32[5]{0:T(128)} %lengths.5, bf16[256,1536]{1,0:T(8,128)(2,1)} %tokens.5, bf16[256,1536]{1,0:T(8,128)(2,1)} %cot.1, ...), custom_call_target="tpu_custom_call" | custom-call | tf_op jit(solution)/shard_map/middle/pallas_call | solution.py:873
  166.2 0.0 copy-start
  166.2 0.0 copy-start.2
  166.2 32.1 %tail.1 = (bf16[256,1536]{1,0:T(8,128)(2,1)}, f32[48,768]{1,0:T(8,128)}, f32[2,1536]{1,0:T(2,128)}) custom-call(s32[5]{0:T(128)} %lengths.5, f32[48,1]{1,0:T(8,128)} %constant.25.clone.freq, bf16[256,1536]{1,0:T(8,128)(2,1)} %tokens.5, f32[1536]{0:T(1024)} %gain.3, bf16[256,1536]{1,0:T(8,128)(2,1)} %get-tuple-element.35.normed, ...), custom_call_target="tpu_custom_call" | custom-call | tf_op jit(solution)/shard_map/tail/pallas_call | solution.py:1043
  198.4 1.6 fusion.1
  199.9 1.5 slice.28
  201.5 0.8 constant_dynamic-slice_fusion
  202.2 0.5 slice_bitcast_fusion.2
  202.7 0.0 copy-done
  202.7 0.0 copy-done.2
  202.7 0.0 copy-start.3
  202.7 0.0 copy-start.1
  202.8 1.1 fusion
  203.9 0.0 copy-done.3
  203.9 0.8 slice_bitcast_fusion
  204.7 0.6 slice_bitcast_fusion.1
  205.3 0.0 copy-done.1
  205.3 0.9 copy.25
Async XLA Ops:
  166.2 36.5 %copy-start = (f32[256,1536]{1,0:T(8,128)S(1)}, f32[256,1536]{1,0:T(8,128)}, u32[]{:S(2)}) copy-start(f32[256,1536]{1,0:T(8,128)} %get-tuple-element.33) | copy-start | bytes 4718596
  166.2 36.5 %copy-start.2 = (bf16[2,4,32,1536]{3,2,1,0:T(8,128)(2,1)S(1)}, bf16[2,4,32,1536]{3,2,1,0:T(8,128)(2,1)}, u32[]{:S(2)}) copy-start(bf16[2,4,32,1536]{3,2,1,0:T(8,128)(2,1)} %get-tuple-element.34) | copy-start | bytes 2359300
  202.7 1.1 copy-start.3
  202.7 2.6 %copy-start.1 = (bf16[256,1536]{1,0:T(8,128)(2,1)S(1)}, bf16[256,1536]{1,0:T(8,128)(2,1)}, u32[]{:S(2)}) copy-start(bf16[256,1536]{1,0:T(8,128)(2,1)} %get-tuple-element.62) | copy-start | bytes 2359300

commit v3 on v2

v3 whole, which is shorter than its diff:
```python
import jax
import jax.numpy as jnp
import numpy as np
from jax import lax
from jax.experimental import pallas as pl
from jax.experimental.pallas import tpu as pltpu
from jax.sharding import Mesh
from jax.sharding import PartitionSpec as P

AXES = ("zl", "x", "y", "zh", "c")
BLK = ("zl", "x", "y")
TP = ("zh", "c")
HEAD = 96
HALF = HEAD // 2
ROWS = 256
WIDTH = 1536
HEADS_LOCAL = 384
PAIRS_LOCAL = 192
FFL = 1024
EPS = 1e-05
THETA = 100000.0
SCALE = HEAD**-0.5
LOG2E = float(np.log2(np.e))
LN2 = float(np.log(2.0))
BIG = 1e30
SEG = 16
MESH = pl.DeviceIdType.MESH
F32 = jnp.float32
BF16 = jnp.bfloat16
VMEM_LIMIT = 63 * 2**20


def dot(a, b, ca=1, cb=0):
    return lax.dot_general(a, b, (((ca,), (cb,)), ((), ())), preferred_element_type=F32)


class Place:
    def __init__(self):
        self.zl, self.x, self.y, self.zh, self.c = (lax.axis_index(a) for a in AXES)

    def at(self, **changes):
        own = dict(zl=self.zl, x=self.x, y=self.y, zh=self.zh, c=self.c)
        own.update(changes)
        return tuple(own[a] for a in AXES)

    def along(self, axis, step):
        return self.at(**{axis: lax.rem(getattr(self, axis) + (step + 4), 4)})

    @property
    def pair(self):
        return dict(zl=1 - self.zl, x=3 - self.x, y=3 - self.y)

    def low_block(self, x, y):
        p = x * 4 + y
        return jnp.where(self.zl == 0, p, 15 - p)


def call(peers):
    barrier = pltpu.get_barrier_semaphore()
    for peer in peers:
        pl.semaphore_signal(barrier, inc=1, device_id=peer, device_id_type=MESH)


def answer(peers):
    pl.semaphore_wait(pltpu.get_barrier_semaphore(), len(peers))


def remote(src, dst, send, recv, device):
    return pltpu.make_async_remote_copy(
        src_ref=src, dst_ref=dst, send_sem=send, recv_sem=recv, device_id=device, device_id_type=MESH
    )


def seg_rows(ends, base):
    token = base + lax.broadcasted_iota(jnp.int32, (SEG, ROWS), 1)
    row = lax.broadcasted_iota(jnp.int32, (SEG, ROWS), 0)
    inside = jnp.zeros((SEG, ROWS), F32)
    start = 0
    for d in range(5):
        hit = (row == d) & (token >= start) & (token < ends[d])
        inside = jnp.where(hit, 1.0, inside)
        start = ends[d]
    return inside, row


def key_segments(ends, base):
    return seg_rows(ends, base)[0].astype(BF16)


def query_segments(ends, base):
    inside, row = seg_rows(ends, base)
    return jnp.where(row < 5, (inside - 1.0) * BIG, 0.0).astype(BF16)


def ends_of(lengths_ref):
    ends, total = [], 0
    for d in range(5):
        total = total + lengths_ref[d]
        ends.append(total)
    return ends


def rotation(ends, lengths_ref, base, freq):
    token = base + lax.broadcasted_iota(jnp.int32, (1, ROWS), 1)
    begin = jnp.zeros((1, ROWS), jnp.int32)
    for d in range(5):
        begin = begin + jnp.where(token >= ends[d], lengths_ref[d], 0)
    angle = (token - begin).astype(F32) * freq
    return jnp.cos(angle), jnp.sin(angle)


class RingSum:
    def __init__(self, place, axis, half, bufs, out, send, recv):
        self.half, self.bufs, self.out = half, bufs, out
        me = getattr(place, axis)
        self.me = me
        self.r, self.l, self.o = (lax.rem(me + k, 4) for k in (1, 3, 2))
        self.right, self.left = place.along(axis, 1), place.along(axis, -1)
        self.send, self.recv = send, recv
        self.ended = False

    def cp(self, k):
        src = (
            lambda: self.half(self.o, 0),
            lambda: self.half(self.o, 1),
            lambda: self.half(self.r, 1),
            lambda: self.half(self.l, 0),
            lambda: self.bufs(0),
            lambda: self.bufs(1),
        )[k]()
        return remote(src, self.bufs(k), self.send(k), self.recv(k), (self.right, self.left)[k % 2])

    def start(self):
        for k in range(4):
            self.cp(k).start()

    def mid(self):
        self.cp(0).wait_recv()
        add_two(self.bufs(0), self.half(self.r, 0))
        self.cp(4).start()
        self.cp(1).wait_recv()
        add_two(self.bufs(1), self.half(self.l, 1))
        self.cp(5).start()

    def fin(self):
        self.cp(4).wait_recv()
        self.cp(3).wait_recv()
        add_three(self.out(0), self.half(self.me, 0), self.bufs(4), self.bufs(3))
        self.cp(5).wait_recv()
        self.cp(2).wait_recv()
        add_three(self.out(1), self.half(self.me, 1), self.bufs(5), self.bufs(2))

    def end(self):
        if not self.ended:
            self.ended = True
            for k in range(6):
                self.cp(k).wait_send()


def add_two(dst, src):
    if len(dst.shape) == 3:
        for i in range(dst.shape[0]):
            dst[i] = dst[i] + src[i]
    else:
        dst[...] = dst[...] + src[...]


def add_three(out, a, b, d):
    if len(out.shape) == 3:
        for i in range(out.shape[0]):
            out[i] = (a[i].astype(F32) + b[i].astype(F32) + d[i].astype(F32)).astype(out.dtype)
    else:
        out[...] = (a[...].astype(F32) + b[...].astype(F32) + d[...].astype(F32)).astype(out.dtype)


class Steps:
    at = 0

    def next(self):
        self.steps[self.at]()
        self.at += 1


class PlaneSum(Steps):
    def __init__(self, place, first, g, glo, blo, slo, w, bufs, sems, n, sums):
        b1, r1, b2, r2, zb = bufs
        send, recv = sems
        gc, bc = pl.ds(glo, w), pl.ds(blo, w)
        self.place, self.r2, self.zb, self.bc, self.sc = place, r2, zb, bc, slice(slo, slo + w)
        self.send, self.recv, self.n, self.sums = send, recv, n, sums
        if first == "x":
            half1 = lambda d, h: g.at[h, d, :, :, gc]
        else:
            half1 = lambda d, h: g.at[h, :, d, :, gc]
        self.one = RingSum(
            place, first, half1, lambda k: b1.at[k, :, :, bc], lambda h: r1.at[h, :, :, bc],
            lambda k: send.at[n, k], lambda k: recv.at[n, k],
        )
        self.two = RingSum(
            place, "y" if first == "x" else "x", lambda d, h: r1.at[h, d, :, bc], lambda k: b2.at[k, :, bc],
            lambda h: r2.at[h, :, bc], lambda k: send.at[n, 6 + k], lambda k: recv.at[n, 6 + k],
        )
        self.steps = [self.one.start, self.one.mid, self.turn, self.two.mid, self.cross, self.total]

    def zcp(self):
        other = 1 - self.place.zl
        return remote(
            self.r2.at[other, :, self.bc], self.zb.at[:, self.bc], self.send.at[self.n, 12],
            self.recv.at[self.n, 12], self.place.at(zl=other),
        )

    def turn(self):
        self.one.fin()
        self.two.start()

    def cross(self):
        self.two.fin()
        self.zcp().start()

    def total(self):
        self.zcp().wait_recv()
        own = self.r2[self.place.zl, :, self.bc].astype(F32)
        self.sums[:, self.sc] = own + self.zb[:, self.bc].astype(F32)

    def end(self):
        self.one.end()
        self.two.end()
        self.zcp().wait_send()


class DepthSum(Steps):
    def __init__(self, place, first, g, glo, blo, slo, w, bufs, sems, n, sums):
        z0, b1, r1, b2 = bufs
        send, recv = sems
        h_w = w // 2
        self.place, self.g, self.z0 = place, g, z0
        self.gc, self.zc = pl.ds(glo, w), pl.ds(blo, w)
        self.send, self.recv, self.n = send, recv, n
        zl = place.zl
        part = lambda lo, h: pl.ds(lo + h * h_w, h_w)
        if first == "x":
            half1 = lambda d, h: g.at[zl, d, :, :, part(glo, h)]
        else:
            half1 = lambda d, h: g.at[zl, :, d, :, part(glo, h)]
        bc = pl.ds(blo // 2, h_w)
        self.one = RingSum(
            place, first, half1, lambda k: b1.at[k, :, :, bc], lambda h: r1.at[:, :, part(blo, h)],
            lambda k: send.at[n, k], lambda k: recv.at[n, k],
        )
        self.two = RingSum(
            place, "y" if first == "x" else "x", lambda d, h: r1.at[d, :, part(blo, h)], lambda k: b2.at[k, :, bc],
            lambda h: sums.at[:, part(slo, h)], lambda k: send.at[n, 6 + k], lambda k: recv.at[n, 6 + k],
        )
        self.steps = [self.cross, self.join, self.one.mid, self.turn, self.two.mid, self.two.fin]

    def zcp(self):
        other = 1 - self.place.zl
        return remote(
            self.g.at[other, :, :, :, self.gc], self.z0.at[:, :, :, self.zc], self.send.at[self.n, 12],
            self.recv.at[self.n, 12], self.place.at(zl=other),
        )

    def cross(self):
        self.zcp().start()

    def join(self):
        self.zcp().wait_recv()
        mine = self.g.at[self.place.zl, :, :, :, self.gc]
        came = self.z0.at[:, :, :, self.zc]

        def add(i, carry):
            for j in range(4):
                mine[i, j] = mine[i, j] + came[i, j]
            return carry

        lax.fori_loop(0, 4, add, 0)
        self.one.start()

    def turn(self):
        self.one.fin()
        self.two.start()

    def end(self):
        self.one.end()
        self.two.end()
        self.zcp().wait_send()


AR_PIECES = 4
AR_ROWS = ROWS // 2 // AR_PIECES


class TpSum:
    def __init__(self, place, part, buf, sems):
        self.place, self.part, self.buf = place, part, buf
        self.send, self.recv = sems
        self.core = place.at(c=1 - place.c)
        self.far = place.at(zh=1 - place.zh)

    def a(self, k):
        return remote(
            self.part.at[1 - self.place.c, k], self.buf.at[0, k], self.send.at[0, k], self.recv.at[0, k], self.core
        )

    def b(self, k):
        return remote(self.buf.at[0, k], self.buf.at[1, k], self.send.at[1, k], self.recv.at[1, k], self.far)

    def d(self, k):
        return remote(
            self.part.at[self.place.c, k], self.buf.at[2, k], self.send.at[2, k], self.recv.at[2, k], self.core
        )

    def start(self):
        for k in range(AR_PIECES):
            self.a(k).start()

    def mid(self):
        for k in range(AR_PIECES):
            self.a(k).wait_recv()
            self.buf[0, k] = self.buf[0, k] + self.part[self.place.c, k]
            self.b(k).start()

    def fin(self):
        for k in range(AR_PIECES):
            self.b(k).wait_recv()
            self.part[self.place.c, k] = self.buf[0, k] + self.buf[1, k]
            self.d(k).start()

    def landed(self):
        for k in range(AR_PIECES):
            self.a(k).wait_send()
            self.d(k).wait_recv()
            self.part[1 - self.place.c, k] = self.buf[2, k]

    def end(self):
        for k in range(AR_PIECES):
            self.b(k).wait_send()
            self.d(k).wait_send()


def tp_scratch():
    return [
        pltpu.VMEM((3, AR_PIECES, AR_ROWS, WIDTH), BF16),
        pltpu.SemaphoreType.DMA((3, AR_PIECES)),
        pltpu.SemaphoreType.DMA((3, AR_PIECES)),
    ]


def ar_view(value):
    return value.reshape(2, AR_PIECES, AR_ROWS, WIDTH)


def ar_load(ref):
    return ref[...].reshape(ROWS, WIDTH)


def norm_back(source, inverse, gain, grad):
    scaled = grad * gain
    gain_grad = jnp.sum(grad * source * inverse, 0, keepdims=True)
    mean = jnp.mean(scaled * source, -1, keepdims=True)
    return inverse * scaled - source * (inverse * inverse * inverse) * mean, gain_grad


W_FFN = 3 * FFL
W_MID = W_FFN + HEADS_LOCAL
W_TAIL = HEADS_LOCAL + 2 * PAIRS_LOCAL
W_ALL = W_MID + W_TAIL
FF_CHUNKS = 4
FF_CHUNK = FFL // FF_CHUNKS

PLAN = [
    ("down", "plane", "x", 2048, 256, 2048),
    ("down", "plane", "y", 2304, 256, 2304),
    ("down_z", "depth", "x", 2560, 256, 2560),
    ("down_z", "depth", "y", 2816, 256, 2816),
    ("gate", "plane", "x", 0, 384, 0),
    ("gate", "plane", "y", 384, 384, 384),
    ("gate_z", "depth", "x", 768, 256, 768),
    ("up", "plane", "x", 1024, 384, 1024),
    ("up", "plane", "y", 1408, 384, 1408),
    ("up_z", "depth", "y", 1792, 256, 1792),
    ("out", "plane", "x", 3072, 128, 3072),
    ("out", "plane", "y", 3200, 256, 3200),
    ("query", "plane", "x", 3456, 256, 2048),
    ("query", "plane", "y", 3712, 128, 2304),
    ("pair", "plane", "x", 3840, 128, 0),
    ("pair", "plane", "y", 3968, 256, 128),
]
W_PLANE = sum(p[4] for p in PLAN if p[1] == "plane")
W_DEPTH = sum(p[4] for p in PLAN if p[1] == "depth")


def layer_kernel(
    lengths, freq, tokens, cot, gain1, gain2, wq, wkt, wvt, wo, wg, wu, wd,
    mixed_out, normed_out, wo_full, feed_out, tokens_grad, sums, gains,
    wo_buf, gu_buf, d_buf, mixed, back, normed, hidden, gate_grad, upper_grad, left, grads,
    b1, r1, b2, r2, zb, z0, b1z, r1z, b2z, gsend, grecv,
    part3, buf3, send3, recv3, buf2, send2, recv2, buf4, send4, recv4,
    kv, kb1, kr1, kb2, kr2, ksend, krecv,
    grp, qkv, att, o, lse, qaug, acc, peak, total, mine, dgrp, dout, dot_t, delta, dqkv, rows,
    gain_sum, gain_buf, gn_send, gn_recv,
    pair_send, pair_recv, ag_send, ag_recv, o_send, o_recv, w_send, w_recv, load_sem, ff_sem, wo_sem,
):
    place = Place()
    zl, x, y, zh, c = place.zl, place.x, place.y, place.zh, place.c
    partner = place.at(**place.pair)
    far_partner = place.at(**place.pair, zh=1 - zh)
    far = place.at(zh=1 - zh)
    core = place.at(c=1 - c)
    diagonal = place.at(zl=1 - zl, zh=1 - zh)
    xr, xl, yr, yl = place.along("x", 1), place.along("x", -1), place.along("y", 1), place.along("y", -1)
    peers = [partner, far_partner, far, core, diagonal, place.at(zl=1 - zl), xr, xl, yr, yl]
    peers += [place.along("x", 2), place.along("y", 2)]
    call(peers)
    me_t = zh * 2 + c
    there_t = (1 - zh) * 2 + c
    mine_t, other_t = zh * 2 + (1 - c), (1 - zh) * 2 + (1 - c)

    def projections():
        return [
            pltpu.make_async_copy(wq, gu_buf.at[0, :, pl.ds(0, HEADS_LOCAL)], ff_sem.at[0, 0]),
            pltpu.make_async_copy(wkt, d_buf.at[0, pl.ds(0, PAIRS_LOCAL)], ff_sem.at[0, 1]),
            pltpu.make_async_copy(wvt, d_buf.at[1, pl.ds(0, PAIRS_LOCAL)], ff_sem.at[0, 2]),
        ]

    def ff_loads(k):
        slot, cols = k % 2, pl.ds(k * FF_CHUNK, FF_CHUNK)
        return [
            pltpu.make_async_copy(wg.at[:, cols], gu_buf.at[slot, :, pl.ds(0, FF_CHUNK)], ff_sem.at[slot, 0]),
            pltpu.make_async_copy(wu.at[:, cols], gu_buf.at[slot, :, pl.ds(FF_CHUNK, FF_CHUNK)], ff_sem.at[slot, 1]),
            pltpu.make_async_copy(wd.at[cols], d_buf.at[slot], ff_sem.at[slot, 2]),
        ]

    for cp in projections():
        cp.start()
    ends = ends_of(lengths)
    block = zl * 16 + x * 4 + y
    source = tokens[...].astype(F32)
    inverse = lax.rsqrt(jnp.mean(source * source, -1, keepdims=True) + EPS)
    normed[...] = (source * inverse * gain1[...].reshape(1, WIDTH)).astype(BF16)
    normed_save = pltpu.make_async_copy(normed, normed_out, load_sem.at[0])
    normed_save.start()
    cosine, sine = rotation(ends, lengths, block * ROWS, freq[...])
    answer(peers)
    wo_cps = [
        remote(wo, wo_full.at[me_t], w_send.at[0], w_recv.at[0], diagonal),
        remote(wo, wo_full.at[me_t], w_send.at[1], w_recv.at[1], core),
    ]
    for cp in wo_cps:
        cp.start()

    def turned(u, factor):
        a, b = u[:HALF], u[HALF:]
        if factor is None:
            return a * cosine - b * sine, b * cosine + a * sine
        return (a * cosine - b * sine) * factor, (b * cosine + a * sine) * factor

    for cp in projections():
        cp.wait()
    kt = dot(d_buf[0, :PAIRS_LOCAL], normed[...], 1, 1)
    vt = dot(d_buf[1, :PAIRS_LOCAL], normed[...], 1, 1)
    qt = dot(normed[...], gu_buf[0, :, :HEADS_LOCAL]).T
    for g in range(2):
        for h in range(2):
            a, b = turned(qt[(2 * g + h) * HEAD : (2 * g + h + 1) * HEAD], SCALE * LOG2E)
            grp[g, h * HEAD : h * HEAD + HALF] = a.astype(BF16)
            grp[g, h * HEAD + HALF : (h + 1) * HEAD] = b.astype(BF16)
        a, b = turned(kt[g * HEAD : (g + 1) * HEAD], None)
        grp[g, 2 * HEAD : 2 * HEAD + HALF] = a.astype(BF16)
        grp[g, 2 * HEAD + HALF : 3 * HEAD] = b.astype(BF16)
        grp[g, 3 * HEAD :] = vt[g * HEAD : (g + 1) * HEAD].astype(BF16)
    pair_cp = remote(grp.at[1 - zl], qkv.at[zl], pair_send.at[0], pair_recv.at[0], partner)
    pair_cp.start()
    for k in range(2):
        for cp in ff_loads(k):
            cp.start()
    qkv[zl] = grp[zl]
    kv[x, y, zl] = grp[zl, 2 * HEAD :]

    def gather(n, slot, swap):
        me1, me2 = (y, x) if swap else (x, y)
        r1, l1, r2, l2 = (yr, yl, xr, xl) if swap else (xr, xl, yr, yl)

        def ref(i, j, part=None):
            i, j = lax.rem(i + 4, 4), lax.rem(j + 4, 4)
            v = kv.at[j, i, slot] if swap else kv.at[i, j, slot]
            return v if part is None else v.at[pl.ds(part * HEAD, HEAD)]

        def cp(k, view, dev):
            return remote(view, view, ag_send.at[n, k], ag_recv.at[n, k], dev)

        def stage(base, i, j, di, dj, r, l):
            return dict(
                right=cp(base, ref(i, j), r),
                left=cp(base + 1, ref(i, j), l),
                from_left=cp(base, ref(i - di, j - dj), r),
                from_right=cp(base + 1, ref(i + di, j + dj), l),
                on_right=cp(base + 2, ref(i - di, j - dj, 0), r),
                on_left=cp(base + 3, ref(i + di, j + dj, 1), l),
                from_left2=cp(base + 2, ref(i + 2 * di, j + 2 * dj, 0), r),
                from_right2=cp(base + 3, ref(i + 2 * di, j + 2 * dj, 1), l),
            )

        s1 = stage(0, me1, me2, 1, 0, r1, l1)
        s2 = [stage(4 + 4 * k, me1 + k, me2, 0, 1, r2, l2) for k in range(4)]
        return s1, s2

    def begin(st):
        st["right"].start()
        st["left"].start()

    def hand_on(st):
        st["from_left"].wait_recv()
        st["on_right"].start()
        st["from_right"].wait_recv()
        st["on_left"].start()

    def complete(st):
        st["from_left2"].wait_recv()
        st["from_right2"].wait_recv()

    own, other = gather(0, zl, False), gather(1, 1 - zl, True)
    both = (own, other)
    begin(own[0])
    begin(own[1][0])
    pair_cp.wait_recv()
    kv[x, y, 1 - zl] = qkv[1 - zl, 2 * HEAD :]
    begin(other[0])
    begin(other[1][0])
    low = place.low_block(x, y)
    for s in range(2):
        base = jnp.where(s == 0, low, 31 - low) * ROWS
        segs = query_segments(ends, base)
        for h in range(2):
            qaug[s, :HEAD, h * ROWS : (h + 1) * ROWS] = qkv[s, h * HEAD : (h + 1) * HEAD]
            qaug[s, HEAD:, h * ROWS : (h + 1) * ROWS] = segs
    peak[...] = jnp.full(peak.shape, -BIG, F32)
    total[...] = jnp.zeros(total.shape, F32)
    acc[...] = jnp.zeros(acc.shape, F32)

    def attend(qs, kx, ky, ks, kbase, causal):
        pair = kv[kx, ky, ks]
        ka = jnp.concatenate([pair[:HEAD], key_segments(ends, kbase)], 0)
        s = dot(ka, qaug[qs], 0, 0)
        if causal:
            key = lax.broadcasted_iota(jnp.int32, (ROWS, 2 * ROWS), 0)
            query = lax.broadcasted_iota(jnp.int32, (ROWS, 2 * ROWS), 1)
            s = jnp.where(key <= jnp.where(query >= ROWS, query - ROWS, query), s, -BIG)
        old = peak[qs]
        new = jnp.maximum(old, jnp.max(s, 0, keepdims=True))
        p = jnp.exp2(s - new)
        fade = jnp.exp2(old - new)
        peak[qs] = new
        total[qs] = total[qs] * fade + jnp.sum(p, 0, keepdims=True)
        acc[qs] = acc[qs] * fade + dot(pair[HEAD:], p.astype(BF16))

    def shard(dx, dy):
        kx, ky = lax.rem(x + dx, 4), lax.rem(y + dy, 4)
        there = place.low_block(kx, ky)
        attend(1, kx, ky, 0, there * ROWS, False)
        sel = jnp.where(there < low, 0, 1)
        attend(sel, kx, ky, sel, jnp.where(there < low, there, 31 - there) * ROWS, False)

    def shards(count, offsets):
        def step(i, carry):
            shard(*offsets(i))
            return carry

        lax.fori_loop(0, count, step, 0)

    attend(0, x, y, 0, low * ROWS, True)
    attend(1, x, y, 1, (31 - low) * ROWS, True)
    attend(1, x, y, 0, low * ROWS, False)
    for s1, s2 in both:
        hand_on(s1)
        begin(s2[3])
        begin(s2[1])
    for s1, s2 in both:
        hand_on(s2[0])
    shards(4, lambda i: ((1 - i // 2) * (2 * i + 1), (i // 2) * (2 * i - 3)))
    for s1, s2 in both:
        complete(s1)
        begin(s2[2])
    for s1, s2 in both:
        hand_on(s2[3])
        hand_on(s2[1])
    shards(4, lambda i: (2 * (i // 2) + 1, 2 * lax.rem(i, 2) + 1))
    for s1, s2 in both:
        complete(s2[0])
        hand_on(s2[2])
    shards(2, lambda i: (2 * i, 2 - 2 * i))
    for s1, s2 in both:
        complete(s2[3])
        complete(s2[1])
    shards(4, lambda i: ((1 - i // 2) * (2 * i + 1) + 2 * (i // 2), (i // 2) * (2 * i - 3) + 2 * (1 - i // 2)))
    for s1, s2 in both:
        complete(s2[2])
    shard(2, 2)
    for s in range(2):
        out = acc[s] / total[s]
        lse[s] = peak[s] + jnp.log2(total[s])
        for h in range(2):
            part = out[:, h * ROWS : (h + 1) * ROWS]
            o[s, h * HEAD : (h + 1) * HEAD] = part
            mine[s, h * HEAD : (h + 1) * HEAD] = part.astype(BF16)

    for s1, s2 in both:
        for st in [s1, *s2]:
            for name in ("right", "left", "on_right", "on_left"):
                st[name].wait_send()
    pair_cp.wait_send()

    group = me_t * 2 + zl
    att[group] = mine[zl]
    sends = [
        remote(mine.at[1 - zl], att.at[group], o_send.at[0], o_recv.at[0], partner),
        remote(mine.at[1 - zl], att.at[group], o_send.at[1], o_recv.at[1], far_partner),
        remote(mine.at[zl], att.at[group], o_send.at[2], o_recv.at[2], far),
    ]
    for cp in sends:
        cp.start()
    wo_far = wo_full.at[there_t]
    remote(wo_far, wo_far, w_send.at[0], w_recv.at[0], far).wait_recv()
    wo_relay = remote(wo_far, wo_far, w_send.at[2], w_recv.at[2], core)
    wo_relay.start()
    order = [
        (None, group), (0, me_t * 2 + 1 - zl), (1, there_t * 2 + 1 - zl), (2, there_t * 2 + zl),
    ]
    relays = []
    for n, (sem, which) in enumerate(order):
        if sem is not None:
            remote(att.at[which], att.at[which], o_send.at[sem], o_recv.at[sem], far).wait_recv()
        cp = remote(att.at[which], att.at[which], o_send.at[3 + n], o_recv.at[3 + n], core)
        cp.start()
        relays.append(cp)

    def load_wo(t, slot, own=False):
        if own:
            pltpu.make_async_copy(wo, wo_buf.at[slot], wo_sem.at[slot]).start()
            return

        @pl.when(me_t == t)
        def _():
            pltpu.make_async_copy(wo, wo_buf.at[slot], wo_sem.at[slot]).start()

        @pl.when(me_t != t)
        def _():
            pltpu.make_async_copy(wo_full.at[t], wo_buf.at[slot], wo_sem.at[slot]).start()

    def wo_ready(slot):
        pltpu.make_async_copy(wo, wo_buf.at[slot], wo_sem.at[slot]).wait()

    w1, w2 = wo_full.at[mine_t], wo_full.at[other_t]
    remote(w1, w1, w_send.at[1], w_recv.at[1], core).wait_recv()
    remote(w2, w2, w_send.at[2], w_recv.at[2], core).wait_recv()
    load_wo(0, 0)
    load_wo(1, 1)
    mixed[...] = tokens[...].astype(F32)
    for n, which in enumerate([mine_t * 2 + zl, mine_t * 2 + 1 - zl, other_t * 2 + 1 - zl, other_t * 2 + zl]):
        remote(att.at[which], att.at[which], o_send.at[3 + n], o_recv.at[3 + n], core).wait_recv()

    for t in range(4):
        wo_ready(t % 2)
        heads = att[2 * t : 2 * t + 2].reshape(HEADS_LOCAL, ROWS)
        mixed[...] = mixed[...] + dot(heads, wo_buf[t % 2], 0, 0)
        if t < 2:
            load_wo(t + 2, t % 2)
        elif t == 2:
            load_wo(0, 0, own=True)
    normed_save.wait()
    gain = gain2[...].reshape(1, WIDTH)
    inverse_two = lax.rsqrt(jnp.mean(mixed[...] * mixed[...], -1, keepdims=True) + EPS)
    normed[...] = (mixed[...] * inverse_two * gain).astype(BF16)
    mixed_save = pltpu.make_async_copy(mixed, mixed_out, load_sem.at[1])
    mixed_save.start()

    for k in range(FF_CHUNKS):
        slot, cols = k % 2, slice(k * FF_CHUNK, (k + 1) * FF_CHUNK)
        for cp in ff_loads(k):
            cp.wait()
        both_ff = dot(normed[...], gu_buf[slot])
        gate, upper = both_ff[:, :FF_CHUNK], both_ff[:, FF_CHUNK:]
        hidden_grad = dot(cot[...], d_buf[slot], 1, 1)
        sig = jax.nn.sigmoid(gate)
        silu = gate * sig
        hid = (silu * upper).astype(BF16)
        gg = (hidden_grad * upper * sig * (1.0 + gate * (1.0 - sig))).astype(BF16)
        ug = (hidden_grad * silu).astype(BF16)
        hidden[:, cols], gate_grad[:, cols], upper_grad[:, cols] = hid, gg, ug
        add_back = dot(jnp.concatenate([gg, ug], 1), gu_buf[slot], 1, 1)
        add_feed = dot(hid, d_buf[slot])
        if k == 0:
            mixed_save.wait()
            back[...], mixed[...] = add_back, add_feed
        else:
            back[...] = back[...] + add_back
            mixed[...] = mixed[...] + add_feed
        if k + 2 < FF_CHUNKS:
            for cp in ff_loads(k + 2):
                cp.start()
    part3[...] = ar_view(back[...].astype(BF16))
    sum3 = TpSum(place, part3, buf3, (send3, recv3))
    sum3.start()
    feed_out[...] = ar_view(mixed[...].astype(BF16))
    mixed_load = pltpu.make_async_copy(mixed_out, mixed, load_sem.at[1])
    mixed_load.start()

    def weight_grad(rhs, lo, cb=0):
        w = rhs.shape[1 - cb]

        def slab(i, carry):
            piece = dot(left[pl.ds(pl.multiple_of(i * 192, 192), 192)], rhs[...], 1, cb)
            grads[i // 4, i % 4, :, :, lo : lo + w] = piece.astype(BF16).reshape(4, 48, w)
            return carry

        lax.fori_loop(0, 8, slab, 0)

    groups, blo = {}, dict(plane=0, depth=0)
    for n, (name, kind, first, slo, w, glo) in enumerate(PLAN):
        if kind == "plane":
            piece = PlaneSum(place, first, grads, glo, blo[kind], slo, w, (b1, r1, b2, r2, zb), (gsend, grecv), n, sums)
        else:
            piece = DepthSum(place, first, grads, glo, blo[kind], slo, w, (z0, b1z, r1z, b2z), (gsend, grecv), n, sums)
        blo[kind] += w
        groups.setdefault(name, []).append(piece)
    pieces = [p for group_ in groups.values() for p in group_]

    def go(*names):
        for name in names:
            for piece in groups[name]:
                piece.next()

    left[...] = cot[...].T
    weight_grad(hidden, 2 * FFL)
    go("down")
    sum3.mid()
    left[...] = normed[...].T
    weight_grad(gate_grad, 0)
    go("gate")
    weight_grad(upper_grad, FFL)
    go("up")
    sum2 = TpSum(place, feed_out, buf2, (send2, recv2))
    sum2.start()
    for s in range(2):
        for h in range(2):
            dot_t[s, :, h * ROWS : (h + 1) * ROWS] = jnp.zeros((HEAD, ROWS), BF16)
    acc[...] = jnp.zeros(acc.shape, F32)
    dq = acc
    mixed_load.wait()
    sum3.fin()
    go("down_z", "gate_z", "up_z")
    sum3.landed()
    mixed_part, ffn_gain_grad = norm_back(mixed[...], inverse_two, gain, ar_load(part3).astype(F32))
    gain_sum[0, 1:2] = ffn_gain_grad
    back[...] = cot[...].astype(F32) + mixed_part
    normed[...] = back[...].astype(BF16)
    wo_ready(0)
    own_grad = dot(wo_buf[0], normed[...], 1, 1).astype(BF16)
    dgrp[0] = own_grad[: 2 * HEAD]
    dgrp[1] = own_grad[2 * HEAD :]
    grad_cp = remote(dgrp.at[1 - zl], dout.at[zl], pair_send.at[1], pair_recv.at[1], partner)
    grad_cp.start()
    dout[zl] = dgrp[zl]
    left[...] = normed[...].T
    weight_grad(att.at[pl.ds(me_t * 2, 2)][...].reshape(HEADS_LOCAL, ROWS), W_FFN, 1)
    go("out")
    normed_load = pltpu.make_async_copy(normed_out, normed, load_sem.at[0])
    normed_load.start()
    for cp in projections():
        cp.start()
    go("down")
    grad_cp.wait_recv()
    for s in range(2):
        for h in range(2):
            lanes, feats = slice(h * ROWS, (h + 1) * ROWS), slice(h * HEAD, (h + 1) * HEAD)
            d = dout[s, feats]
            dot_t[s, :, lanes] = d
            delta[s, :, lanes] = jnp.sum(d.astype(F32) * o[s, feats], 0, keepdims=True)

    def attend_back(qs, kx, ky, ks, kbase, causal):
        pair = kv[kx, ky, ks]
        q = qaug[qs]
        do = dot_t[qs]
        ka = jnp.concatenate([pair[:HEAD], key_segments(ends, kbase)], 0)
        s = dot(ka, q, 0, 0)
        p = jnp.exp2(s - lse[qs])
        if causal:
            key = lax.broadcasted_iota(jnp.int32, (ROWS, 2 * ROWS), 0)
            query = lax.broadcasted_iota(jnp.int32, (ROWS, 2 * ROWS), 1)
            p = jnp.where(key <= jnp.where(query >= ROWS, query - ROWS, query), p, 0.0)
        dp = dot(pair[HEAD:], do, 0, 0)
        ds = (p * (dp - delta[qs])).astype(BF16)
        dq[qs] = dq[qs] + dot(pair[:HEAD], ds)
        dk = dot(q[:HEAD], ds, 1, 1)
        dv = dot(do, p.astype(BF16), 1, 1)
        return jnp.concatenate([dk, dv], 0)

    first = attend_back(0, x, y, 0, low * ROWS, True) + attend_back(1, x, y, 0, low * ROWS, False)
    kv[x, y, 0] = first.astype(BF16)
    kv[x, y, 1] = attend_back(1, x, y, 1, (31 - low) * ROWS, True).astype(BF16)

    def step(i, carry):
        kx, ky = lax.rem(x + i // 4, 4), lax.rem(y + i % 4, 4)
        there = place.low_block(kx, ky)
        one = attend_back(1, kx, ky, 0, there * ROWS, False)
        before = there < low
        sel = jnp.where(before, 0, 1)
        two = attend_back(sel, kx, ky, sel, jnp.where(before, there, 31 - there) * ROWS, False)
        share = jnp.where(before, 1.0, 0.0)
        kv[kx, ky, 0] = (one + two * share).astype(BF16)
        kv[kx, ky, 1] = (two * (1.0 - share)).astype(BF16)
        return carry

    lax.fori_loop(1, 4, step, 0)
    go("gate")
    lax.fori_loop(4, 7, step, 0)
    go("up", "out", "down_z")
    lax.fori_loop(7, 10, step, 0)
    go("down")
    lax.fori_loop(10, 13, step, 0)
    go("gate", "gate_z")
    lax.fori_loop(13, 16, step, 0)

    for s in range(2):
        for h in range(2):
            grp[s, h * HEAD : (h + 1) * HEAD] = (dq[s, :, h * ROWS : (h + 1) * ROWS] * SCALE).astype(BF16)
    q_rows, k_rows = pl.ds(0, 2 * HEAD), pl.ds(2 * HEAD, 2 * HEAD)
    dq_cp = remote(grp.at[1 - zl, q_rows], dqkv.at[zl, q_rows], pair_send.at[2], pair_recv.at[2], partner)
    dq_cp.start()
    dqkv[zl, : 2 * HEAD] = grp[zl, : 2 * HEAD]

    def key_sum(slot, axis):
        other_axis = "y" if axis == "x" else "x"
        if axis == "x":
            half = lambda d, h: kv.at[d, :, slot, pl.ds(h * HEAD, HEAD)]
        else:
            half = lambda d, h: kv.at[:, d, slot, pl.ds(h * HEAD, HEAD)]
        one = RingSum(
            place, axis, half, lambda k: kb1.at[slot, k], lambda h: kr1.at[slot, h],
            lambda k: ksend.at[slot, k], lambda k: krecv.at[slot, k],
        )
        two = RingSum(
            place, other_axis, lambda d, h: kr1.at[slot, h, d], lambda k: kb2.at[slot, k],
            lambda h: kr2.at[slot, h], lambda k: ksend.at[slot, 6 + k], lambda k: krecv.at[slot, 6 + k],
        )
        return one, two

    ka, kb = key_sum(0, "x"), key_sum(1, "y")
    ka[0].start()
    kb[0].start()
    go("up", "out", "up_z", "down_z")
    sum2.mid()
    ka[0].mid()
    kb[0].mid()
    go("down", "gate", "gate_z", "down_z")

    def unturned(g, h, at):
        a = dqkv[g, h * HEAD : h * HEAD + HALF].astype(F32)
        b = dqkv[g, h * HEAD + HALF : (h + 1) * HEAD].astype(F32)
        if h == 2:
            a, b = a * LN2, b * LN2
        rows[at : at + HALF] = (a * cosine + b * sine).astype(BF16)
        rows[at + HALF : at + HEAD] = (b * cosine - a * sine).astype(BF16)

    dq_there = dqkv.at[1 - zl, q_rows]
    remote(dq_there, dq_there, pair_send.at[2], pair_recv.at[2], partner).wait_recv()
    for g in range(2):
        for h in range(2):
            unturned(g, h, (2 * g + h) * HEAD)
    normed_load.wait()
    for piece in groups["down"]:
        piece.one.end()
    left[...] = normed[...].T
    weight_grad(rows.at[pl.ds(0, HEADS_LOCAL)], 2 * FFL, 1)
    go("query")
    ka[0].fin()
    kb[0].fin()
    ka[1].start()
    kb[1].start()
    for cp in projections():
        cp.wait()
    mixed[...] = dot(rows[:HEADS_LOCAL], gu_buf[0, :, :HEADS_LOCAL], 0, 1)
    go("up", "out", "up_z", "gate_z", "down_z")
    ka[1].mid()
    kb[1].mid()
    go("down", "gate")
    sum2.fin()
    ka[1].fin()
    kb[1].fin()
    for s in range(2):
        for h in range(2):
            grp[s, (2 + h) * HEAD : (3 + h) * HEAD] = kr2[s, h]
    dk_cp = remote(grp.at[1 - zl, k_rows], dqkv.at[zl, k_rows], pair_send.at[3], pair_recv.at[3], partner)
    dk_cp.start()
    dqkv[zl, 2 * HEAD :] = grp[zl, 2 * HEAD :]
    go("query", "up", "out", "up_z", "gate_z", "down_z")
    go("down", "gate")
    for piece in groups["gate"]:
        piece.one.end()
    sum3.end()
    dk_there = dqkv.at[1 - zl, k_rows]
    remote(dk_there, dk_there, pair_send.at[3], pair_recv.at[3], partner).wait_recv()
    for g in range(2):
        unturned(g, 2, HEADS_LOCAL + g * HEAD)
        at = HEADS_LOCAL + PAIRS_LOCAL + g * HEAD
        rows[at : at + HEAD] = dqkv[g, 3 * HEAD :]
    grad_in = mixed[...] + dot(rows[HEADS_LOCAL : HEADS_LOCAL + PAIRS_LOCAL], d_buf[0, :PAIRS_LOCAL], 0, 0)
    grad_in = grad_in + dot(rows[HEADS_LOCAL + PAIRS_LOCAL :], d_buf[1, :PAIRS_LOCAL], 0, 0)
    part3[...] = ar_view(grad_in.astype(BF16))
    sum4 = TpSum(place, part3, buf4, (send4, recv4))
    sum4.start()
    weight_grad(rows.at[pl.ds(HEADS_LOCAL, 2 * PAIRS_LOCAL)], 0, 1)
    go("pair")
    sum4.mid()
    go("query", "up", "out", "up_z", "gate_z")
    go("pair")
    go("query")
    sum4.fin()
    sum4.landed()
    source = tokens[...].astype(F32)
    source_part, gain_grad = norm_back(source, inverse, gain1[...].reshape(1, WIDTH), ar_load(part3).astype(F32))
    tokens_grad[...] = (back[...] + source_part).astype(BF16)
    gain_sum[0, 0:1] = gain_grad

    def gain_copies(stage, axis):
        if axis == "zl":
            there = [place.at(zl=1 - zl)]
        else:
            there = [place.along(axis, s) for s in (1, 2, 3)]
        return [
            remote(gain_sum.at[stage], gain_buf.at[stage, k], gn_send.at[stage, k], gn_recv.at[stage, k], peer)
            for k, peer in enumerate(there)
        ]

    sent_x = gain_copies(0, "x")
    for cp in sent_x:
        cp.start()
    go("pair")
    go("query", "up_z")
    for cp in sent_x:
        cp.wait_recv()
    gain_sum[1] = gain_sum[0] + gain_buf[0, 0] + gain_buf[0, 1] + gain_buf[0, 2]
    sent_y = gain_copies(1, "y")
    for cp in sent_y:
        cp.start()
    go("pair")
    for cp in sent_y:
        cp.wait_recv()
    gain_sum[2] = gain_sum[1] + gain_buf[1, 0] + gain_buf[1, 1] + gain_buf[1, 2]
    sent_z = gain_copies(2, "zl")
    for cp in sent_z:
        cp.start()
    go("pair")
    go("query")
    for cp in sent_z:
        cp.wait_recv()
    gains[...] = gain_sum[2] + gain_buf[2, 0]
    go("pair")
    sum2.landed()
    for cp in [grad_cp, dq_cp, dk_cp, *wo_cps, wo_relay, *sends, *relays, *sent_x, *sent_y, *sent_z]:
        cp.wait_send()
    sum2.end()
    sum4.end()
    for piece in pieces:
        assert piece.at == len(piece.steps)
        piece.end()
    for one, two in (ka, kb):
        one.end()
        two.end()


def layer(lengths, freq, tokens, cot, gain1, gain2, wq, wkt, wvt, wo, wg, wu, wd):
    vm = pl.BlockSpec(memory_space=pltpu.VMEM)
    hbm = pl.BlockSpec(memory_space=pl.ANY)
    dma = pltpu.SemaphoreType.DMA
    shape = (2, AR_PIECES, AR_ROWS, WIDTH)
    group = pltpu.VMEM((2, 4 * HEAD, ROWS), BF16)
    two_heads = pltpu.VMEM((2, 2 * HEAD, ROWS), BF16)
    line = pltpu.VMEM((2, 1, 2 * ROWS), F32)
    return pl.pallas_call(
        layer_kernel,
        out_shape=(
            jax.ShapeDtypeStruct((ROWS, WIDTH), F32),
            jax.ShapeDtypeStruct((ROWS, WIDTH), BF16),
            jax.ShapeDtypeStruct((4, HEADS_LOCAL, WIDTH), BF16),
            jax.ShapeDtypeStruct(shape, BF16),
            jax.ShapeDtypeStruct((ROWS, WIDTH), BF16),
            jax.ShapeDtypeStruct((48, W_ALL), F32),
            jax.ShapeDtypeStruct((2, WIDTH), F32),
        ),
        in_specs=[pl.BlockSpec(memory_space=pltpu.SMEM)] + [vm] * 5 + [hbm] * 7,
        out_specs=(hbm, hbm, hbm, vm, vm, vm, vm),
        scratch_shapes=[
            pltpu.VMEM((2, HEADS_LOCAL, WIDTH), BF16),
            pltpu.VMEM((2, WIDTH, 2 * FF_CHUNK), BF16),
            pltpu.VMEM((2, FF_CHUNK, WIDTH), BF16),
            pltpu.VMEM((ROWS, WIDTH), F32),
            pltpu.VMEM((ROWS, WIDTH), F32),
            pltpu.VMEM((ROWS, WIDTH), BF16),
            pltpu.VMEM((ROWS, FFL), BF16),
            pltpu.VMEM((ROWS, FFL), BF16),
            pltpu.VMEM((ROWS, FFL), BF16),
            pltpu.VMEM((WIDTH, ROWS), BF16),
            pltpu.VMEM((2, 4, 4, 48, W_MID), BF16),
            pltpu.VMEM((6, 4, 48, W_PLANE), BF16),
            pltpu.VMEM((2, 4, 48, W_PLANE), BF16),
            pltpu.VMEM((6, 48, W_PLANE), BF16),
            pltpu.VMEM((2, 48, W_PLANE), BF16),
            pltpu.VMEM((48, W_PLANE), BF16),
            pltpu.VMEM((4, 4, 48, W_DEPTH), BF16),
            pltpu.VMEM((6, 4, 48, W_DEPTH // 2), BF16),
            pltpu.VMEM((4, 48, W_DEPTH), BF16),
            pltpu.VMEM((6, 48, W_DEPTH // 2), BF16),
            dma((len(PLAN), 13)),
            dma((len(PLAN), 13)),
            pltpu.VMEM(shape, BF16),
            *tp_scratch(),
            *tp_scratch(),
            *tp_scratch(),
            pltpu.VMEM((4, 4, 2, 2 * HEAD, ROWS), BF16),
            pltpu.VMEM((2, 6, 4, HEAD, ROWS), BF16),
            pltpu.VMEM((2, 2, 4, HEAD, ROWS), BF16),
            pltpu.VMEM((2, 6, HEAD, ROWS), BF16),
            pltpu.VMEM((2, 2, HEAD, ROWS), BF16),
            dma((2, 12)),
            dma((2, 12)),
            group,
            group,
            pltpu.VMEM((8, 2 * HEAD, ROWS), BF16),
            pltpu.VMEM((2, 2 * HEAD, ROWS), F32),
            line,
            pltpu.VMEM((2, HEAD + SEG, 2 * ROWS), BF16),
            pltpu.VMEM((2, HEAD, 2 * ROWS), F32),
            line,
            line,
            two_heads,
            two_heads,
            two_heads,
            pltpu.VMEM((2, HEAD, 2 * ROWS), BF16),
            line,
            group,
            pltpu.VMEM((W_TAIL, ROWS), BF16),
            pltpu.VMEM((3, 2, WIDTH), F32),
            pltpu.VMEM((3, 3, 2, WIDTH), F32),
            dma((3, 3)),
            dma((3, 3)),
            dma((4,)),
            dma((4,)),
            dma((2, 20)),
            dma((2, 20)),
            dma((7,)),
            dma((7,)),
            dma((3,)),
            dma((3,)),
            dma((2,)),
            dma((2, 3)),
            dma((2,)),
        ],
        compiler_params=pltpu.CompilerParams(
            collective_id=0, has_side_effects=True, vmem_limit_bytes=VMEM_LIMIT
        ),
        name="layer",
    )(lengths, freq, tokens, cot, gain1, gain2, wq, wkt, wvt, wo, wg, wu, wd)


def finish_kernel(
    mixed, feed, tokens_grad, sums, gains,
    result, tokens_grad_out, norm_gain, query, key, value, out, ffn_gain, gate, up, down,
):
    result[...] = (mixed[...] + ar_load(feed).astype(F32)).astype(BF16)
    tokens_grad_out[...] = tokens_grad[...]
    block = (lax.axis_index("zl") * 4 + lax.axis_index("x")) * 4 + lax.axis_index("y")
    own = jnp.zeros((2, 48), F32)
    for b in range(32):
        own = own + jnp.where(block == b, gains[:, 48 * b : 48 * b + 48], 0.0)
    norm_gain[...] = own[0:1]
    ffn_gain[...] = own[1:2]
    gate[...] = sums[:, :FFL]
    up[...] = sums[:, FFL : 2 * FFL]
    down[...] = sums[:, 2 * FFL : W_FFN]
    out[...] = sums[:, W_FFN:W_MID]
    query[...] = sums[:, W_MID : W_MID + HEADS_LOCAL]
    key[...] = sums[:, W_MID + HEADS_LOCAL : W_MID + HEADS_LOCAL + PAIRS_LOCAL]
    value[...] = sums[:, W_MID + HEADS_LOCAL + PAIRS_LOCAL :]


def finish(mixed, feed, tokens_grad, sums, gains):
    vm = pl.BlockSpec(memory_space=pltpu.VMEM)
    shapes = [(ROWS, WIDTH)] * 2 + [
        (1, 48), (48, HEADS_LOCAL), (48, PAIRS_LOCAL), (48, PAIRS_LOCAL), (48, HEADS_LOCAL), (1, 48),
        (48, FFL), (48, FFL), (48, FFL),
    ]
    return pl.pallas_call(
        finish_kernel,
        out_shape=[jax.ShapeDtypeStruct(s, BF16 if n < 2 else F32) for n, s in enumerate(shapes)],
        in_specs=[vm] * 5,
        out_specs=[vm] * len(shapes),
        compiler_params=pltpu.CompilerParams(vmem_limit_bytes=VMEM_LIMIT),
        name="finish",
    )(mixed, feed, tokens_grad, sums, gains)


def local(
    tokens, norm_gain, query_weight, key_matrix, value_matrix, out_weight,
    ffn_gain, gate_weight, up_weight, down_weight, cotangent, lengths,
):
    freq = jnp.asarray(
        (THETA ** (-2.0 * np.arange(HALF) / HEAD)).astype(np.float32).reshape(HALF, 1)
    )
    mixed, _, _, feed, tokens_grad, sums, gains = layer(
        lengths, freq, tokens, cotangent, norm_gain, ffn_gain, query_weight, key_matrix.T, value_matrix.T,
        out_weight, gate_weight, up_weight, down_weight,
    )
    result, tokens_grad, norm_gain_grad, query, key, value, out, ffn_gain_grad, gate, up, down = finish(
        mixed, feed, tokens_grad, sums, gains
    )
    return (
        result, tokens_grad, norm_gain_grad.reshape(48), query, key, value, out.T,
        ffn_gain_grad.reshape(48), gate, up, down.T,
    )


def solution(mesh):
    split = Mesh(mesh.devices.reshape(2, 4, 4, 2, 2), AXES)
    in_specs = (
        P(BLK, None),
        P(),
        P(None, TP),
        P(None, TP),
        P(None, TP),
        P(TP, None),
        P(),
        P(None, TP),
        P(None, TP),
        P(TP, None),
        P(BLK, None),
        P(),
    )
    out_specs = (
        P(BLK, None),
        P(BLK, None),
        P(BLK),
        P(BLK, TP),
        P(BLK, TP),
        P(BLK, TP),
        P(TP, BLK),
        P(BLK),
        P(BLK, TP),
        P(BLK, TP),
        P(TP, BLK),
    )
    return jax.shard_map(local, mesh=split, in_specs=in_specs, out_specs=out_specs, check_vma=False)
```

time: 207 us -> 183 us (0.88)
  Pallas kernels: 198 us -> 181 us
  local copies, waits for them, and re-layouts: 6.73 us -> 0 us
    pallas_call x3 -> x2, Pallas kernels: 198 us -> 181 us  [the longest x1 178 us: layer(): pl.pallas_call(layer_kernel, out_shape=(jax.ShapeDtypeStruct((ROWS, WIDTH...]
    slice x2 -> x0, local copies, waits for them, and re-layouts: 3.1 us -> none  [the longest x1 1.58 us: local(): sums[:, HEADS_LOCAL + PAIRS_LOCAL:]]
where the time goes in v3:
time: 183 us; the launch traced here: 182 us
  Pallas kernels  181 us (99%)
    pallas_call x1, Pallas kernels, layer(): pl.pallas_call(layer_kernel, out_shape=(jax.ShapeDtypeStruct((ROWS, WIDTH...  178 us

profile of v3, /device:TPU:0, one launch (start us, length us, event | category | flops | bytes accessed | tf_op | source)
XLA Modules:
  0.0 182.0 jit_solution(16092762479154803425)
XLA Ops:
  0.6 177.5 %layer.1 = (f32[256,1536]{1,0:T(8,128)}, bf16[256,1536]{1,0:T(8,128)(2,1)}, bf16[4,384,1536]{2,1,0:T(8,128)(2,1)}, bf16[2,4,32,1536]{3,2,1,0:T(8,128)(2,1)}, bf1...) custom-call(s32[5]{0:T(128)} %lengths.1, f32[48,1]{1,0:T(8,128)} %constant.2.clone.freq, ...), custom_call_target="tpu_custom_call" | custom-call | tf_op jit(solution)/shard_map/layer/pallas_call | solution.py:980
  178.2 3.6 %finish.1 = (bf16[256,1536]{1,0:T(8,128)(2,1)}, bf16[256,1536]{1,0:T(8,128)(2,1)}, f32[1,48]{1,0:T(1,128)}, f32[48,384]{1,0:T(8,128)}, f32[48,192]{1,0:T(8,128)}...) custom-call(f32[256,1536]{1,0:T(8,128)} %get-tuple-element.27.mixed,, ...), custom_call_target="tpu_custom_call" | custom-call | tf_op jit(solution)/shard_map/finish/pallas_call | solution.py:1093

commit v4 on v3

--- a/solution.py
+++ b/solution.py
@@ -130,9 +130,17 @@
         )[k]()
         return remote(src, self.bufs(k), self.send(k), self.recv(k), (self.right, self.left)[k % 2])
 
+    def start_far(self):
+        self.cp(0).start()
+        self.cp(1).start()
+
+    def start_near(self):
+        self.cp(2).start()
+        self.cp(3).start()
+
     def start(self):
-        for k in range(4):
-            self.cp(k).start()
+        self.start_far()
+        self.start_near()
 
     def mid(self):
         self.cp(0).wait_recv()
@@ -286,7 +294,7 @@
         self.zcp().wait_send()
 
 
-AR_PIECES = 4
+AR_PIECES = 2
 AR_ROWS = ROWS // 2 // AR_PIECES
 
 
@@ -373,9 +381,10 @@
     ("down", "plane", "y", 2304, 256, 2304),
     ("down_z", "depth", "x", 2560, 256, 2560),
     ("down_z", "depth", "y", 2816, 256, 2816),
-    ("gate", "plane", "x", 0, 384, 0),
-    ("gate", "plane", "y", 384, 384, 384),
-    ("gate_z", "depth", "x", 768, 256, 768),
+    ("gate", "plane", "x", 0, 256, 0),
+    ("gate", "plane", "y", 256, 256, 256),
+    ("gate_z", "depth", "x", 512, 256, 512),
+    ("gate_z", "depth", "y", 768, 256, 768),
     ("up", "plane", "x", 1024, 384, 1024),
     ("up", "plane", "y", 1408, 384, 1408),
     ("up_z", "depth", "y", 1792, 256, 1792),
@@ -441,13 +450,6 @@
     normed_save = pltpu.make_async_copy(normed, normed_out, load_sem.at[0])
     normed_save.start()
     cosine, sine = rotation(ends, lengths, block * ROWS, freq[...])
-    answer(peers)
-    wo_cps = [
-        remote(wo, wo_full.at[me_t], w_send.at[0], w_recv.at[0], diagonal),
-        remote(wo, wo_full.at[me_t], w_send.at[1], w_recv.at[1], core),
-    ]
-    for cp in wo_cps:
-        cp.start()
 
     def turned(u, factor):
         a, b = u[:HALF], u[HALF:]
@@ -469,13 +471,16 @@
         grp[g, 2 * HEAD : 2 * HEAD + HALF] = a.astype(BF16)
         grp[g, 2 * HEAD + HALF : 3 * HEAD] = b.astype(BF16)
         grp[g, 3 * HEAD :] = vt[g * HEAD : (g + 1) * HEAD].astype(BF16)
-    pair_cp = remote(grp.at[1 - zl], qkv.at[zl], pair_send.at[0], pair_recv.at[0], partner)
-    pair_cp.start()
+    qkv[zl] = grp[zl]
+    kv[x, y, zl] = grp[zl, 2 * HEAD :]
     for k in range(2):
         for cp in ff_loads(k):
             cp.start()
-    qkv[zl] = grp[zl]
-    kv[x, y, zl] = grp[zl, 2 * HEAD :]
+    answer(peers)
+    q_rows, k_rows = pl.ds(0, 2 * HEAD), pl.ds(2 * HEAD, 2 * HEAD)
+    k_cp = remote(grp.at[1 - zl, k_rows], kv.at[3 - x, 3 - y, zl], pair_send.at[0], pair_recv.at[0], partner)
+    q_cp = remote(grp.at[1 - zl, q_rows], qkv.at[zl, q_rows], pair_send.at[4], pair_recv.at[4], partner)
+    k_cp.start()
 
     def gather(n, slot, swap):
         me1, me2 = (y, x) if swap else (x, y)
@@ -523,10 +528,19 @@
     both = (own, other)
     begin(own[0])
     begin(own[1][0])
-    pair_cp.wait_recv()
-    kv[x, y, 1 - zl] = qkv[1 - zl, 2 * HEAD :]
+    q_cp.start()
+    wo_cps = [
+        remote(wo, wo_full.at[me_t], w_send.at[0], w_recv.at[0], diagonal),
+        remote(wo, wo_full.at[me_t], w_send.at[1], w_recv.at[1], core),
+    ]
+    for cp in wo_cps:
+        cp.start()
+    k_there = kv.at[x, y, 1 - zl]
+    remote(k_there, k_there, pair_send.at[0], pair_recv.at[0], partner).wait_recv()
     begin(other[0])
     begin(other[1][0])
+    q_there = qkv.at[1 - zl, q_rows]
+    remote(q_there, q_there, pair_send.at[4], pair_recv.at[4], partner).wait_recv()
     low = place.low_block(x, y)
     for s in range(2):
         base = jnp.where(s == 0, low, 31 - low) * ROWS
@@ -608,7 +622,8 @@
         for st in [s1, *s2]:
             for name in ("right", "left", "on_right", "on_left"):
                 st[name].wait_send()
-    pair_cp.wait_send()
+    k_cp.wait_send()
+    q_cp.wait_send()
 
     group = me_t * 2 + zl
     att[group] = mine[zl]
@@ -623,50 +638,51 @@
     remote(wo_far, wo_far, w_send.at[0], w_recv.at[0], far).wait_recv()
     wo_relay = remote(wo_far, wo_far, w_send.at[2], w_recv.at[2], core)
     wo_relay.start()
-    order = [
-        (None, group), (0, me_t * 2 + 1 - zl), (1, there_t * 2 + 1 - zl), (2, there_t * 2 + zl),
-    ]
-    relays = []
-    for n, (sem, which) in enumerate(order):
-        if sem is not None:
-            remote(att.at[which], att.at[which], o_send.at[sem], o_recv.at[sem], far).wait_recv()
-        cp = remote(att.at[which], att.at[which], o_send.at[3 + n], o_recv.at[3 + n], core)
-        cp.start()
-        relays.append(cp)
-
-    def load_wo(t, slot, own=False):
-        if own:
-            pltpu.make_async_copy(wo, wo_buf.at[slot], wo_sem.at[slot]).start()
-            return
-
-        @pl.when(me_t == t)
-        def _():
-            pltpu.make_async_copy(wo, wo_buf.at[slot], wo_sem.at[slot]).start()
-
-        @pl.when(me_t != t)
-        def _():
-            pltpu.make_async_copy(wo_full.at[t], wo_buf.at[slot], wo_sem.at[slot]).start()
+    def load_wo(src, slot):
+        pltpu.make_async_copy(src, wo_buf.at[slot], wo_sem.at[slot]).start()
 
     def wo_ready(slot):
         pltpu.make_async_copy(wo, wo_buf.at[slot], wo_sem.at[slot]).wait()
 
+    def arrived(which, n):
+        remote(att.at[which], att.at[which], o_send.at[n], o_recv.at[n], far).wait_recv()
+
+    def relay(which, n):
+        cp = remote(att.at[which], att.at[which], o_send.at[n], o_recv.at[n], core)
+        cp.start()
+        return cp
+
+    def heads_of(t):
+        return att[pl.ds(t * 2, 2)].reshape(HEADS_LOCAL, ROWS)
+
     w1, w2 = wo_full.at[mine_t], wo_full.at[other_t]
+    load_wo(wo, 0)
+    relays = [relay(group, 3)]
     remote(w1, w1, w_send.at[1], w_recv.at[1], core).wait_recv()
+    load_wo(w1, 1)
+    arrived(me_t * 2 + 1 - zl, 0)
+    relays.append(relay(me_t * 2 + 1 - zl, 4))
+    wo_ready(0)
+    mixed[...] = dot(heads_of(me_t), wo_buf[0], 0, 0)
+    load_wo(wo_far, 0)
+    arrived(mine_t * 2 + zl, 3)
+    arrived(mine_t * 2 + 1 - zl, 4)
+    arrived(there_t * 2 + zl, 2)
+    relays.append(relay(there_t * 2 + zl, 5))
+    arrived(there_t * 2 + 1 - zl, 1)
+    relays.append(relay(there_t * 2 + 1 - zl, 6))
+    wo_ready(1)
+    mixed[...] = mixed[...] + dot(heads_of(mine_t), wo_buf[1], 0, 0)
     remote(w2, w2, w_send.at[2], w_recv.at[2], core).wait_recv()
-    load_wo(0, 0)
-    load_wo(1, 1)
-    mixed[...] = tokens[...].astype(F32)
-    for n, which in enumerate([mine_t * 2 + zl, mine_t * 2 + 1 - zl, other_t * 2 + 1 - zl, other_t * 2 + zl]):
-        remote(att.at[which], att.at[which], o_send.at[3 + n], o_recv.at[3 + n], core).wait_recv()
-
-    for t in range(4):
-        wo_ready(t % 2)
-        heads = att[2 * t : 2 * t + 2].reshape(HEADS_LOCAL, ROWS)
-        mixed[...] = mixed[...] + dot(heads, wo_buf[t % 2], 0, 0)
-        if t < 2:
-            load_wo(t + 2, t % 2)
-        elif t == 2:
-            load_wo(0, 0, own=True)
+    load_wo(w2, 1)
+    wo_ready(0)
+    back[...] = dot(heads_of(there_t), wo_buf[0], 0, 0)
+    load_wo(wo, 0)
+    arrived(other_t * 2 + zl, 5)
+    arrived(other_t * 2 + 1 - zl, 6)
+    wo_ready(1)
+    back[...] = back[...] + dot(heads_of(other_t), wo_buf[1], 0, 0)
+    mixed[...] = tokens[...].astype(F32) + (mixed[...] + back[...])
     normed_save.wait()
     gain = gain2[...].reshape(1, WIDTH)
     inverse_two = lax.rsqrt(jnp.mean(mixed[...] * mixed[...], -1, keepdims=True) + EPS)
@@ -747,6 +763,7 @@
     acc[...] = jnp.zeros(acc.shape, F32)
     dq = acc
     mixed_load.wait()
+    go("down")
     sum3.fin()
     go("down_z", "gate_z", "up_z")
     sum3.landed()
@@ -762,13 +779,13 @@
     grad_cp.start()
     dout[zl] = dgrp[zl]
     left[...] = normed[...].T
-    weight_grad(att.at[pl.ds(me_t * 2, 2)][...].reshape(HEADS_LOCAL, ROWS), W_FFN, 1)
+    weight_grad(heads_of(me_t), W_FFN, 1)
     go("out")
     normed_load = pltpu.make_async_copy(normed_out, normed, load_sem.at[0])
     normed_load.start()
     for cp in projections():
         cp.start()
-    go("down")
+    go("gate")
     grad_cp.wait_recv()
     for s in range(2):
         for h in range(2):
@@ -795,12 +812,8 @@
         dv = dot(do, p.astype(BF16), 1, 1)
         return jnp.concatenate([dk, dv], 0)
 
-    first = attend_back(0, x, y, 0, low * ROWS, True) + attend_back(1, x, y, 0, low * ROWS, False)
-    kv[x, y, 0] = first.astype(BF16)
-    kv[x, y, 1] = attend_back(1, x, y, 1, (31 - low) * ROWS, True).astype(BF16)
-
-    def step(i, carry):
-        kx, ky = lax.rem(x + i // 4, 4), lax.rem(y + i % 4, 4)
+    def shard_back(dx, dy):
+        kx, ky = lax.rem(x + dx, 4), lax.rem(y + dy, 4)
         there = place.low_block(kx, ky)
         one = attend_back(1, kx, ky, 0, there * ROWS, False)
         before = there < low
@@ -809,25 +822,15 @@
         share = jnp.where(before, 1.0, 0.0)
         kv[kx, ky, 0] = (one + two * share).astype(BF16)
         kv[kx, ky, 1] = (two * (1.0 - share)).astype(BF16)
-        return carry
-
-    lax.fori_loop(1, 4, step, 0)
-    go("gate")
-    lax.fori_loop(4, 7, step, 0)
-    go("up", "out", "down_z")
-    lax.fori_loop(7, 10, step, 0)
-    go("down")
-    lax.fori_loop(10, 13, step, 0)
-    go("gate", "gate_z")
-    lax.fori_loop(13, 16, step, 0)
-
-    for s in range(2):
-        for h in range(2):
-            grp[s, h * HEAD : (h + 1) * HEAD] = (dq[s, :, h * ROWS : (h + 1) * ROWS] * SCALE).astype(BF16)
-    q_rows, k_rows = pl.ds(0, 2 * HEAD), pl.ds(2 * HEAD, 2 * HEAD)
-    dq_cp = remote(grp.at[1 - zl, q_rows], dqkv.at[zl, q_rows], pair_send.at[2], pair_recv.at[2], partner)
-    dq_cp.start()
-    dqkv[zl, : 2 * HEAD] = grp[zl, : 2 * HEAD]
+
+    def shards_back(count, offsets, events):
+        def step(i, carry):
+            shard_back(*offsets(i))
+            for at, event in events:
+                pl.when(i == at)(event)
+            return carry
+
+        lax.fori_loop(0, count, step, 0)
 
     def key_sum(slot, axis):
         other_axis = "y" if axis == "x" else "x"
@@ -846,13 +849,56 @@
         return one, two
 
     ka, kb = key_sum(0, "x"), key_sum(1, "y")
-    ka[0].start()
-    kb[0].start()
-    go("up", "out", "up_z", "down_z")
+
+    def two_away(i):
+        k, j = i // 4, i - 4
+        return (1 - k) * 2 + k * (j + j // 2), (1 - k) * i + k * 2
+
+    def one_away(i):
+        k, j = i // 4, i - 4
+        along_x = (1 - j // 2) * (2 * j + 1)
+        along_y = (j // 2) * (2 * j - 3)
+        dx = (1 - k) * (2 * (i // 2) + 1) + k * along_x
+        dy = (1 - k) * (2 * lax.rem(i, 2) + 1) + k * along_y
+        return dx, dy
+
+    shards_back(7, two_away, [(0, lambda: go("up", "out")), (3, lambda: go("down")), (6, lambda: go("gate"))])
+    ka[0].start_far()
+    kb[0].start_far()
+
+    def near(part):
+        part.start_near()
+        part.mid()
+
+    shards_back(
+        8,
+        one_away,
+        [
+            (1, lambda: go("up", "out")),
+            (3, lambda: go("down", "down_z")),
+            (5, lambda: near(ka[0])),
+            (6, lambda: go("gate")),
+        ],
+    )
+    near(kb[0])
+    first = attend_back(0, x, y, 0, low * ROWS, True) + attend_back(1, x, y, 0, low * ROWS, False)
+    kv[x, y, 0] = first.astype(BF16)
+    kv[x, y, 1] = attend_back(1, x, y, 1, (31 - low) * ROWS, True).astype(BF16)
+
+    for s in range(2):
+        for h in range(2):
+            grp[s, h * HEAD : (h + 1) * HEAD] = (dq[s, :, h * ROWS : (h + 1) * ROWS] * SCALE).astype(BF16)
+    dq_cp = remote(grp.at[1 - zl, q_rows], dqkv.at[zl, q_rows], pair_send.at[2], pair_recv.at[2], partner)
+    dq_cp.start()
+    dqkv[zl, : 2 * HEAD] = grp[zl, : 2 * HEAD]
+    go("up", "out", "down", "gate")
+
+    ka[0].fin()
+    kb[0].fin()
+    ka[1].start()
+    kb[1].start()
+    go("gate_z", "down_z")
     sum2.mid()
-    ka[0].mid()
-    kb[0].mid()
-    go("down", "gate", "gate_z", "down_z")
 
     def unturned(g, h, at):
         a = dqkv[g, h * HEAD : h * HEAD + HALF].astype(F32)
@@ -872,19 +918,13 @@
         piece.one.end()
     left[...] = normed[...].T
     weight_grad(rows.at[pl.ds(0, HEADS_LOCAL)], 2 * FFL, 1)
+    ka[1].mid()
+    kb[1].mid()
     go("query")
-    ka[0].fin()
-    kb[0].fin()
-    ka[1].start()
-    kb[1].start()
     for cp in projections():
         cp.wait()
     mixed[...] = dot(rows[:HEADS_LOCAL], gu_buf[0, :, :HEADS_LOCAL], 0, 1)
-    go("up", "out", "up_z", "gate_z", "down_z")
-    ka[1].mid()
-    kb[1].mid()
-    go("down", "gate")
-    sum2.fin()
+    go("down_z", "gate_z", "up", "out", "up_z")
     ka[1].fin()
     kb[1].fin()
     for s in range(2):
@@ -893,10 +933,10 @@
     dk_cp = remote(grp.at[1 - zl, k_rows], dqkv.at[zl, k_rows], pair_send.at[3], pair_recv.at[3], partner)
     dk_cp.start()
     dqkv[zl, 2 * HEAD :] = grp[zl, 2 * HEAD :]
-    go("query", "up", "out", "up_z", "gate_z", "down_z")
-    go("down", "gate")
+    go("down", "gate", "down_z", "gate_z", "query", "up_z", "up", "out")
     for piece in groups["gate"]:
         piece.one.end()
+    sum2.fin()
     sum3.end()
     dk_there = dqkv.at[1 - zl, k_rows]
     remote(dk_there, dk_there, pair_send.at[3], pair_recv.at[3], partner).wait_recv()
@@ -909,55 +949,53 @@
     part3[...] = ar_view(grad_in.astype(BF16))
     sum4 = TpSum(place, part3, buf4, (send4, recv4))
     sum4.start()
+    source = tokens[...].astype(F32)
+    gain_sum[0, 0:1] = jnp.sum(grad_in * source * inverse, 0, keepdims=True)
+    gain_sum[0, 1:2] = 0.25 * gain_sum[0, 1:2]
+    gain_sent = []
+
+    def gain_step(stage):
+        if stage:
+            came = gain_sum[stage - 1]
+            for k, cp in enumerate(gain_sent[-1]):
+                cp.wait_recv()
+                came = came + gain_buf[stage - 1, k]
+            gain_sum[stage] = came
+        if stage < 5:
+            there = [
+                [place.along("x", k) for k in (1, 2, 3)], [place.along("y", k) for k in (1, 2, 3)],
+                [place.at(zl=1 - zl)], [far], [core],
+            ][stage]
+            gain_sent.append(
+                [
+                    remote(gain_sum.at[stage], gain_buf.at[stage, k], gn_send.at[stage, k], gn_recv.at[stage, k], peer)
+                    for k, peer in enumerate(there)
+                ]
+            )
+            for cp in gain_sent[-1]:
+                cp.start()
+
+    gain_step(0)
     weight_grad(rows.at[pl.ds(HEADS_LOCAL, 2 * PAIRS_LOCAL)], 0, 1)
+    go("pair", "down_z", "gate_z")
+    sum4.mid()
+    gain_step(1)
+    go("query", "up_z", "pair")
+    gain_step(2)
+    go("gate_z", "query", "up_z")
+    gain_step(3)
     go("pair")
-    sum4.mid()
-    go("query", "up", "out", "up_z", "gate_z")
-    go("pair")
-    go("query")
     sum4.fin()
+    gain_step(4)
+    go("up_z", "query", "pair")
     sum4.landed()
-    source = tokens[...].astype(F32)
-    source_part, gain_grad = norm_back(source, inverse, gain1[...].reshape(1, WIDTH), ar_load(part3).astype(F32))
+    source_part, _ = norm_back(tokens[...].astype(F32), inverse, gain1[...].reshape(1, WIDTH), ar_load(part3).astype(F32))
     tokens_grad[...] = (back[...] + source_part).astype(BF16)
-    gain_sum[0, 0:1] = gain_grad
-
-    def gain_copies(stage, axis):
-        if axis == "zl":
-            there = [place.at(zl=1 - zl)]
-        else:
-            there = [place.along(axis, s) for s in (1, 2, 3)]
-        return [
-            remote(gain_sum.at[stage], gain_buf.at[stage, k], gn_send.at[stage, k], gn_recv.at[stage, k], peer)
-            for k, peer in enumerate(there)
-        ]
-
-    sent_x = gain_copies(0, "x")
-    for cp in sent_x:
-        cp.start()
-    go("pair")
-    go("query", "up_z")
-    for cp in sent_x:
-        cp.wait_recv()
-    gain_sum[1] = gain_sum[0] + gain_buf[0, 0] + gain_buf[0, 1] + gain_buf[0, 2]
-    sent_y = gain_copies(1, "y")
-    for cp in sent_y:
-        cp.start()
-    go("pair")
-    for cp in sent_y:
-        cp.wait_recv()
-    gain_sum[2] = gain_sum[1] + gain_buf[1, 0] + gain_buf[1, 1] + gain_buf[1, 2]
-    sent_z = gain_copies(2, "zl")
-    for cp in sent_z:
-        cp.start()
-    go("pair")
-    go("query")
-    for cp in sent_z:
-        cp.wait_recv()
-    gains[...] = gain_sum[2] + gain_buf[2, 0]
-    go("pair")
+    gain_step(5)
+    gains[...] = gain_sum[5]
+    go("pair", "query", "pair")
     sum2.landed()
-    for cp in [grad_cp, dq_cp, dk_cp, *wo_cps, wo_relay, *sends, *relays, *sent_x, *sent_y, *sent_z]:
+    for cp in [grad_cp, dq_cp, dk_cp, *wo_cps, wo_relay, *sends, *relays, *sum(gain_sent, [])]:
         cp.wait_send()
     sum2.end()
     sum4.end()
@@ -1040,12 +1078,12 @@
             line,
             group,
             pltpu.VMEM((W_TAIL, ROWS), BF16),
-            pltpu.VMEM((3, 2, WIDTH), F32),
-            pltpu.VMEM((3, 3, 2, WIDTH), F32),
-            dma((3, 3)),
-            dma((3, 3)),
-            dma((4,)),
-            dma((4,)),
+            pltpu.VMEM((6, 2, WIDTH), F32),
+            pltpu.VMEM((5, 3, 2, WIDTH), F32),
+            dma((5, 3)),
+            dma((5, 3)),
+            dma((5,)),
+            dma((5,)),
             dma((2, 20)),
             dma((2, 20)),
             dma((7,)),

time: 183 us -> 170 us (0.929)
  Pallas kernels: 181 us -> 169 us
    pallas_call x1, Pallas kernels: 178 us -> 165 us  [layer(): pl.pallas_call(layer_kernel, out_shape=(jax.ShapeDtypeStruct((ROWS, WIDTH...]
where the time goes in v4:
time: 170 us
  Pallas kernels  169 us (99%)
    pallas_call x1, Pallas kernels, layer(): pl.pallas_call(layer_kernel, out_shape=(jax.ShapeDtypeStruct((ROWS, WIDTH...  165 us
    pallas_call x1, Pallas kernels, finish(): pl.pallas_call(finish_kernel, out_shape=[jax.ShapeDtypeStruct(s, BF16 if...  3.6 us

profile of v4, /device:TPU:0, one launch (start us, length us, event | category | flops | bytes accessed | tf_op | source)
XLA Modules:
  0.0 169.8 jit_solution(8575180045559827699)
XLA Ops:
  0.6 165.4 %layer.1 = (f32[256,1536]{1,0:T(8,128)}, bf16[256,1536]{1,0:T(8,128)(2,1)}, bf16[4,384,1536]{2,1,0:T(8,128)(2,1)}, bf16[2,2,64,1536]{3,2,1,0:T(8,128)(2,1)}, bf1...) custom-call(s32[5]{0:T(128)} %lengths.1, f32[48,1]{1,0:T(8,128)} %constant.2.clone.freq, ...), custom_call_target="tpu_custom_call" | custom-call | tf_op jit(solution)/shard_map/layer/pallas_call | solution.py:1018
  166.0 3.6 %finish.1 = (bf16[256,1536]{1,0:T(8,128)(2,1)}, bf16[256,1536]{1,0:T(8,128)(2,1)}, f32[1,48]{1,0:T(1,128)}, f32[48,384]{1,0:T(8,128)}, f32[48,192]{1,0:T(8,128)}...) custom-call(f32[256,1536]{1,0:T(8,128)} %get-tuple-element.27.mixed,, ...), custom_call_target="tpu_custom_call" | custom-call | tf_op jit(solution)/shard_map/finish/pallas_call | solution.py:1131

commit v5 on v4

--- a/solution.py
+++ b/solution.py
@@ -402,7 +402,7 @@
 def layer_kernel(
     lengths, freq, tokens, cot, gain1, gain2, wq, wkt, wvt, wo, wg, wu, wd,
     mixed_out, normed_out, wo_full, feed_out, tokens_grad, sums, gains,
-    wo_buf, gu_buf, d_buf, mixed, back, normed, hidden, gate_grad, upper_grad, left, grads,
+    wo_buf, gu_buf, d_buf, mixed, back, normed, hidden, back_hidden, gate_grad, upper_grad, left, grads,
     b1, r1, b2, r2, zb, z0, b1z, r1z, b2z, gsend, grecv,
     part3, buf3, send3, recv3, buf2, send2, recv2, buf4, send4, recv4,
     kv, kb1, kr1, kb2, kr2, ksend, krecv,
@@ -437,8 +437,16 @@
         return [
             pltpu.make_async_copy(wg.at[:, cols], gu_buf.at[slot, :, pl.ds(0, FF_CHUNK)], ff_sem.at[slot, 0]),
             pltpu.make_async_copy(wu.at[:, cols], gu_buf.at[slot, :, pl.ds(FF_CHUNK, FF_CHUNK)], ff_sem.at[slot, 1]),
-            pltpu.make_async_copy(wd.at[cols], d_buf.at[slot], ff_sem.at[slot, 2]),
         ]
+
+    def down_load(k):
+        rows_ = pl.ds(k * FF_CHUNK, FF_CHUNK)
+        return pltpu.make_async_copy(wd.at[rows_], d_buf.at[k % 2], ff_sem.at[k % 2, 2])
+
+    def hidden_back(k):
+        down_load(k).wait()
+        back_hidden[:, k * FF_CHUNK : (k + 1) * FF_CHUNK] = dot(cot[...], d_buf[k % 2], 1, 1).astype(BF16)
+        down_load((k + 2) % 4).start()
 
     for cp in projections():
         cp.start()
@@ -474,6 +482,7 @@
     qkv[zl] = grp[zl]
     kv[x, y, zl] = grp[zl, 2 * HEAD :]
     for k in range(2):
+        down_load(k).start()
         for cp in ff_loads(k):
             cp.start()
     answer(peers)
@@ -591,18 +600,22 @@
         begin(s2[1])
     for s1, s2 in both:
         hand_on(s2[0])
+    hidden_back(0)
     shards(4, lambda i: ((1 - i // 2) * (2 * i + 1), (i // 2) * (2 * i - 3)))
     for s1, s2 in both:
         complete(s1)
         begin(s2[2])
+    hidden_back(1)
     for s1, s2 in both:
         hand_on(s2[3])
         hand_on(s2[1])
     shards(4, lambda i: (2 * (i // 2) + 1, 2 * lax.rem(i, 2) + 1))
+    hidden_back(2)
     for s1, s2 in both:
         complete(s2[0])
         hand_on(s2[2])
     shards(2, lambda i: (2 * i, 2 - 2 * i))
+    hidden_back(3)
     for s1, s2 in both:
         complete(s2[3])
         complete(s2[1])
@@ -658,6 +671,7 @@
     w1, w2 = wo_full.at[mine_t], wo_full.at[other_t]
     load_wo(wo, 0)
     relays = [relay(group, 3)]
+    left[...] = cot[...].T
     remote(w1, w1, w_send.at[1], w_recv.at[1], core).wait_recv()
     load_wo(w1, 1)
     arrived(me_t * 2 + 1 - zl, 0)
@@ -696,7 +710,7 @@
             cp.wait()
         both_ff = dot(normed[...], gu_buf[slot])
         gate, upper = both_ff[:, :FF_CHUNK], both_ff[:, FF_CHUNK:]
-        hidden_grad = dot(cot[...], d_buf[slot], 1, 1)
+        hidden_grad = back_hidden[:, cols].astype(F32)
         sig = jax.nn.sigmoid(gate)
         silu = gate * sig
         hid = (silu * upper).astype(BF16)
@@ -704,23 +718,16 @@
         ug = (hidden_grad * silu).astype(BF16)
         hidden[:, cols], gate_grad[:, cols], upper_grad[:, cols] = hid, gg, ug
         add_back = dot(jnp.concatenate([gg, ug], 1), gu_buf[slot], 1, 1)
-        add_feed = dot(hid, d_buf[slot])
         if k == 0:
-            mixed_save.wait()
-            back[...], mixed[...] = add_back, add_feed
+            back[...] = add_back
         else:
             back[...] = back[...] + add_back
-            mixed[...] = mixed[...] + add_feed
         if k + 2 < FF_CHUNKS:
             for cp in ff_loads(k + 2):
                 cp.start()
     part3[...] = ar_view(back[...].astype(BF16))
     sum3 = TpSum(place, part3, buf3, (send3, recv3))
     sum3.start()
-    feed_out[...] = ar_view(mixed[...].astype(BF16))
-    mixed_load = pltpu.make_async_copy(mixed_out, mixed, load_sem.at[1])
-    mixed_load.start()
-
     def weight_grad(rhs, lo, cb=0):
         w = rhs.shape[1 - cb]
 
@@ -746,7 +753,6 @@
             for piece in groups[name]:
                 piece.next()
 
-    left[...] = cot[...].T
     weight_grad(hidden, 2 * FFL)
     go("down")
     sum3.mid()
@@ -755,6 +761,16 @@
     go("gate")
     weight_grad(upper_grad, FFL)
     go("up")
+    mixed_save.wait()
+    for k in range(FF_CHUNKS):
+        down_load(k).wait()
+        add_feed = dot(hidden[:, k * FF_CHUNK : (k + 1) * FF_CHUNK], d_buf[k % 2])
+        mixed[...] = add_feed if k == 0 else mixed[...] + add_feed
+        if k < 2:
+            down_load(k + 2).start()
+    feed_out[...] = ar_view(mixed[...].astype(BF16))
+    mixed_load = pltpu.make_async_copy(mixed_out, mixed, load_sem.at[1])
+    mixed_load.start()
     sum2 = TpSum(place, feed_out, buf2, (send2, recv2))
     sum2.start()
     for s in range(2):
@@ -944,6 +960,8 @@
         unturned(g, 2, HEADS_LOCAL + g * HEAD)
         at = HEADS_LOCAL + PAIRS_LOCAL + g * HEAD
         rows[at : at + HEAD] = dqkv[g, 3 * HEAD :]
+    weight_grad(rows.at[pl.ds(HEADS_LOCAL, 2 * PAIRS_LOCAL)], 0, 1)
+    go("pair")
     grad_in = mixed[...] + dot(rows[HEADS_LOCAL : HEADS_LOCAL + PAIRS_LOCAL], d_buf[0, :PAIRS_LOCAL], 0, 0)
     grad_in = grad_in + dot(rows[HEADS_LOCAL + PAIRS_LOCAL :], d_buf[1, :PAIRS_LOCAL], 0, 0)
     part3[...] = ar_view(grad_in.astype(BF16))
@@ -976,8 +994,7 @@
                 cp.start()
 
     gain_step(0)
-    weight_grad(rows.at[pl.ds(HEADS_LOCAL, 2 * PAIRS_LOCAL)], 0, 1)
-    go("pair", "down_z", "gate_z")
+    go("down_z", "gate_z")
     sum4.mid()
     gain_step(1)
     go("query", "up_z", "pair")
@@ -1035,6 +1052,7 @@
             pltpu.VMEM((ROWS, WIDTH), F32),
             pltpu.VMEM((ROWS, WIDTH), F32),
             pltpu.VMEM((ROWS, WIDTH), BF16),
+            pltpu.VMEM((ROWS, FFL), BF16),
             pltpu.VMEM((ROWS, FFL), BF16),
             pltpu.VMEM((ROWS, FFL), BF16),
             pltpu.VMEM((ROWS, FFL), BF16),

time: 170 us -> 167 us (0.982)
  Pallas kernels: 169 us -> 166 us
    pallas_call x1, Pallas kernels: 165 us -> 162 us  [layer(): pl.pallas_call(layer_kernel, out_shape=(jax.ShapeDtypeStruct((ROWS, WIDTH...]
where the time goes in v5:
time: 167 us
  Pallas kernels  166 us (99%)
    pallas_call x1, Pallas kernels, layer(): pl.pallas_call(layer_kernel, out_shape=(jax.ShapeDtypeStruct((ROWS, WIDTH...  162 us
    pallas_call x1, Pallas kernels, finish(): pl.pallas_call(finish_kernel, out_shape=[jax.ShapeDtypeStruct(s, BF16 if...  3.6 us

profile of v5, /device:TPU:0, one launch (start us, length us, event | category | flops | bytes accessed | tf_op | source)
XLA Modules:
  0.0 166.9 jit_solution(358796151992140418)
XLA Ops:
  0.6 162.4 %layer.1 = (f32[256,1536]{1,0:T(8,128)}, bf16[256,1536]{1,0:T(8,128)(2,1)}, bf16[4,384,1536]{2,1,0:T(8,128)(2,1)}, bf16[2,2,64,1536]{3,2,1,0:T(8,128)(2,1)}, bf1...) custom-call(s32[5]{0:T(128)} %lengths.1, f32[48,1]{1,0:T(8,128)} %constant.2.clone.freq, ...), custom_call_target="tpu_custom_call" | custom-call | tf_op jit(solution)/shard_map/layer/pallas_call | solution.py:1035
  163.1 3.6 %finish.1 = (bf16[256,1536]{1,0:T(8,128)(2,1)}, bf16[256,1536]{1,0:T(8,128)(2,1)}, f32[1,48]{1,0:T(1,128)}, f32[48,384]{1,0:T(8,128)}, f32[48,192]{1,0:T(8,128)}...) custom-call(f32[256,1536]{1,0:T(8,128)} %get-tuple-element.27.mixed,, ...), custom_call_target="tpu_custom_call" | custom-call | tf_op jit(solution)/shard_map/finish/pallas_call | solution.py:1149

commit v6 on v5

--- a/solution.py
+++ b/solution.py
@@ -176,7 +176,7 @@
 def add_three(out, a, b, d):
     if len(out.shape) == 3:
         for i in range(out.shape[0]):
-            out[i] = (a[i].astype(F32) + b[i].astype(F32) + d[i].astype(F32)).astype(out.dtype)
+            out[i] = a[i] + (b[i] + d[i])
     else:
         out[...] = (a[...].astype(F32) + b[...].astype(F32) + d[...].astype(F32)).astype(out.dtype)
 

time: 167 us -> 167 us (level)
  no operation moved by 1% of the time
where the time goes in v6:
time: 167 us
  Pallas kernels  166 us (99%)
    pallas_call x1, Pallas kernels, layer(): pl.pallas_call(layer_kernel, out_shape=(jax.ShapeDtypeStruct((ROWS, WIDTH...  162 us
    pallas_call x1, Pallas kernels, finish(): pl.pallas_call(finish_kernel, out_shape=[jax.ShapeDtypeStruct(s, BF16 if...  3.6 us

profile of v6, /device:TPU:0, one launch (start us, length us, event | category | flops | bytes accessed | tf_op | source)
XLA Modules:
  0.0 166.8 jit_solution(12773243521998437257)
XLA Ops:
  0.6 162.4 %layer.1 = (f32[256,1536]{1,0:T(8,128)}, bf16[256,1536]{1,0:T(8,128)(2,1)}, bf16[4,384,1536]{2,1,0:T(8,128)(2,1)}, bf16[2,2,64,1536]{3,2,1,0:T(8,128)(2,1)}, bf1...) custom-call(s32[5]{0:T(128)} %lengths.1, f32[48,1]{1,0:T(8,128)} %constant.2.clone.freq, ...), custom_call_target="tpu_custom_call" | custom-call | tf_op jit(solution)/shard_map/layer/pallas_call | solution.py:1035
  163.1 3.6 %finish.1 = (bf16[256,1536]{1,0:T(8,128)(2,1)}, bf16[256,1536]{1,0:T(8,128)(2,1)}, f32[1,48]{1,0:T(1,128)}, f32[48,384]{1,0:T(8,128)}, f32[48,192]{1,0:T(8,128)}...) custom-call(f32[256,1536]{1,0:T(8,128)} %get-tuple-element.27.mixed,, ...), custom_call_target="tpu_custom_call" | custom-call | tf_op jit(solution)/shard_map/finish/pallas_call | solution.py:1149
